TPU v7x, 32 devices: a whole 2x2x4 slice. The times are simulated.
32 devices in a mesh: dp: 8 (over y, x, core), tensor: 4 (over z).
Axes of the slice: x: 2, y: 2, z: 4, core: 2. Of those that a mesh axis runs over, the one named last changes fastest.
Arguments:
- inputs: bfloat16 [16, 1024, 1024], P('dp', None, 'tensor'), may hold values from -6 to 6
- segment: int32 [16, 1024], P('dp'), may hold values from 0 to 4, as said below
- cotangent: bfloat16 [16, 1024, 1024], P('dp', None, 'tensor'), may hold values from -6 to 6
- norm_gain: float32 [1024], replicated, may hold values from 0.1 to 1.9
- weight_z: bfloat16 [1024, 2048], P(None, 'tensor'), may hold values from -0.1875 to 0.1875
- weight_x: bfloat16 [1024, 2048], P(None, 'tensor'), may hold values from -0.1875 to 0.1875
- weight_bc: bfloat16 [1024, 256], replicated, may hold values from -0.1875 to 0.1875
- weight_dt: bfloat16 [1024, 32], P(None, 'tensor'), may hold values from -0.1875 to 0.1875
- conv_weight_x: float32 [4, 2048], P(None, 'tensor'), may hold values from -3 to 3
- conv_bias_x: float32 [2048], P('tensor'), may hold values from -3 to 3
- conv_weight_bc: float32 [4, 256], replicated, may hold values from -3 to 3
- conv_bias_bc: float32 [256], replicated, may hold values from -3 to 3
- step_bias: float32 [32], P('tensor'), may hold values from -6 to -2
- decay_log: float32 [32], P('tensor'), may hold values from 0 to 2.77
- skip_gain: float32 [32], P('tensor'), may hold values from 0.5 to 2
- gate_gain: float32 [2048], P('tensor'), may hold values from 0.1 to 1.9
- weight_out: bfloat16 [2048, 1024], P('tensor'), may hold values from -0.125 to 0.125
Outputs:
- output: bfloat16 [16, 1024, 1024], P('dp', None, 'tensor')
- input_grad: float32 [16, 1024, 1024], P('dp', None, 'tensor')
- norm_gain_grad: float32 [1024], P('tensor')
- weight_z_grad: float32 [1024, 2048], P('dp', 'tensor')
- weight_x_grad: float32 [1024, 2048], P('dp', 'tensor')
- weight_bc_grad: float32 [1024, 256], P('dp')
- weight_dt_grad: float32 [1024, 32], P('dp', 'tensor')
- conv_weight_x_grad: float32 [4, 2048], P(None, 'tensor')
- conv_bias_x_grad: float32 [2048], P('tensor')
- conv_weight_bc_grad: float32 [4, 256], replicated
- conv_bias_bc_grad: float32 [256], replicated
- step_bias_grad: float32 [32], P('tensor')
- decay_log_grad: float32 [32], P('tensor')
- skip_gain_grad: float32 [32], P('tensor')
- gate_gain_grad: float32 [2048], P('tensor')
- weight_out_grad: float32 [2048, 1024], P('tensor', 'dp')
Inputs may be any that keep to these rules, and one draw needn't show every extreme that they name: `segment`: segment numbers start at 0 in each sequence and never fall along it; a new number starts a new document, where the scan state and the convolution restart. Each sequence holds one document of exactly 800 tokens, at its start or at its end; the inner documents have 60 to 800 tokens, the one at the other end may be shorter.
All inputs are finite; a program needn't handle non-finite values.
Results may differ from a plain program's by a relative error of at most 0.008.
Values may be sent and summed in bfloat16 or wider, within the bound.
No kernel may reach another device: no remote copies, remote signals or barrier semaphores. Data moves between devices by JAX's collectives and lax.ppermute only.
A program may use at most 192 MiB of HBM per device.

v0:
```python
import jax
import jax.numpy as jnp
from jax import lax
from jax.sharding import PartitionSpec as P

SPAN = 256
SEQ_MB = 1
INNER = 2048


eps = 1e-05


def causal_conv(values, weights, biases, segment):
    taps = weights.shape[0]
    total = biases + weights[taps - 1] * values
    for offset in range(1, taps):
        moved = jnp.pad(values, ((0, 0), (offset, 0), (0, 0)))[:, :-offset]
        earlier = jnp.pad(segment, ((0, 0), (offset, 0)), constant_values=-1)[:, :-offset]
        same_doc = (earlier == segment).astype(values.dtype)[..., None]
        total = total + weights[taps - 1 - offset] * moved * same_doc
    return total


def ssd_scan(values, decays, deltas, b_matrix, c_matrix, segment, block_len):
    seq_count, length, head_count, head_size = values.shape
    block_count = length // block_len

    def to_blocks(source):
        shaped = source.reshape((seq_count, block_count, block_len) + source.shape[2:])
        return jnp.moveaxis(shaped, 1, 0)

    pieces = tuple(
        (to_blocks(source) for source in (values, decays, deltas, b_matrix, c_matrix, segment))
    )
    state_init = jnp.zeros((seq_count, head_count, b_matrix.shape[-1], head_size), values.dtype)
    prev_init = jnp.full((seq_count,), -1, jnp.int32)
    lower_tri = jnp.arange(block_len)[:, None] >= jnp.arange(block_len)[None, :]

    def advance(carried_in, block_in):
        prior_state, previous = carried_in
        value_blk, decay_blk, delta_blk, b_blk, c_blk, seg_blk = block_in
        cumulative = jnp.cumsum(decay_blk, axis=1)
        allowed = (seg_blk[:, :, None] == seg_blk[:, None, :]) & lower_tri[None]
        masking = allowed.astype(values.dtype)[..., None]
        spread = cumulative[:, :, None, :] - cumulative[:, None, :, :]
        kernel = jnp.exp(jnp.where(allowed[..., None], spread, 0.0)) * masking
        scores = jnp.einsum("stn,sun->stu", c_blk, b_blk, precision=lax.Precision.HIGHEST)
        mixing = scores[..., None] * kernel * delta_blk[:, None, :, :]
        inside = jnp.einsum("stuh,suhp->sthp", mixing, value_blk, precision=lax.Precision.HIGHEST)
        final_seg = seg_blk[:, -1]
        same_end = (seg_blk == final_seg[:, None]).astype(values.dtype)[..., None]
        tail_weight = jnp.exp(cumulative[:, -1:, :] - cumulative) * same_end * delta_blk
        local_state = jnp.einsum(
            "sun,suhp->shnp",
            b_blk,
            tail_weight[..., None] * value_blk,
            precision=lax.Precision.HIGHEST,
        )
        entering = (
            jnp.exp(cumulative) * (seg_blk == previous[:, None]).astype(values.dtype)[..., None]
        )
        outside = (
            jnp.einsum("stn,shnp->sthp", c_blk, prior_state, precision=lax.Precision.HIGHEST)
            * entering[..., None]
        )
        carried = (
            jnp.exp(cumulative[:, -1, :]) * (final_seg == previous).astype(values.dtype)[:, None]
        )
        new_state = carried[:, :, None, None] * prior_state + local_state
        return ((new_state, final_seg), inside + outside)

    _, results = lax.scan(jax.checkpoint(advance), (state_init, prev_init), pieces)
    return jnp.moveaxis(results, 0, 1).reshape(seq_count, length, head_count, head_size)


def mixer(gate_pre, value_pre, bc_pre, delta_pre, params, segment):
    conv_weight_x, conv_bias_x, conv_weight_bc, conv_bias_bc, step_bias, decay_log, skip_gain = (
        params
    )
    conv_value = jax.nn.silu(causal_conv(value_pre, conv_weight_x, conv_bias_x, segment))
    conv_bc = jax.nn.silu(causal_conv(bc_pre, conv_weight_bc, conv_bias_bc, segment))
    state_size = conv_bc.shape[-1] // 2
    deltas = jax.nn.softplus(delta_pre + step_bias)
    decays = -deltas * jnp.exp(decay_log)
    seq_count, length, head_count = deltas.shape
    values = conv_value.reshape(seq_count, length, head_count, -1)
    scan_result = ssd_scan(
        values, decays, deltas, conv_bc[..., :state_size], conv_bc[..., state_size:], segment, SPAN
    )
    scan_result = scan_result + skip_gain[:, None] * values
    return scan_result.reshape(gate_pre.shape) * jax.nn.silu(gate_pre)


def project(left_operand, right_operand):
    return jnp.einsum(
        "ofp,pv->ofv", left_operand, right_operand, preferred_element_type=jnp.float32
    )


def project_back(left_operand, right_operand):
    return jnp.einsum(
        "igh,rh->igr", left_operand, right_operand, preferred_element_type=jnp.float32
    )


def outer_sum(left_operand, right_operand):
    return jnp.einsum(
        "vzq,vza->qa", left_operand, right_operand, preferred_element_type=jnp.float32
    )


def add_tree(left_operand, right_operand):
    return jax.tree.map(jnp.add, left_operand, right_operand)


def per_device(
    inputs,
    segment,
    cotangent,
    norm_gain,
    weight_z,
    weight_x,
    weight_bc,
    weight_dt,
    conv_weight_x,
    conv_bias_x,
    conv_weight_bc,
    conv_bias_bc,
    step_bias,
    decay_log,
    skip_gain,
    gate_gain,
    weight_out,
):
    model_width = weight_z.shape[0]
    share_width = inputs.shape[2]
    share_start = lax.axis_index("tensor") * share_width
    gain_share = lax.dynamic_slice_in_dim(norm_gain, share_start, share_width, 0)
    bc_share = lax.dynamic_slice_in_dim(weight_bc, share_start, share_width, 0)
    params = (
        conv_weight_x,
        conv_bias_x,
        conv_weight_bc,
        conv_bias_bc,
        step_bias,
        decay_log,
        skip_gain,
    )
    big_grads = None
    small_grads = None
    rounds = inputs.shape[0] // SEQ_MB
    outputs = []
    input_grads = []
    for batch_step in range(rounds):
        row_start = batch_step * SEQ_MB
        local_in = inputs[row_start : row_start + SEQ_MB]
        local_seg = segment[row_start : row_start + SEQ_MB]
        local_cot = cotangent[row_start : row_start + SEQ_MB]
        whole_in, cotangent_entire = (
            lax.all_gather(local_in, "tensor", axis=2, tiled=True),
            lax.all_gather(local_cot, "tensor", axis=2, tiled=True),
        )
        residual = whole_in.astype(jnp.float32)
        scale_in = lax.rsqrt(jnp.mean(residual * residual, axis=-1, keepdims=True) + eps)
        normed = (residual * scale_in * norm_gain).astype(jnp.bfloat16)
        gate_pre = project(normed, weight_z)
        value_pre = project(normed, weight_x)
        bc_pre = project(normed, weight_bc)
        delta_pre = project(normed, weight_dt)

        def local_mixer(gate_in, value_in, bc_in, delta_in, param_set):
            return mixer(gate_in, value_in, bc_in, delta_in, param_set, local_seg)

        gated_out, pullback = jax.vjp(local_mixer, gate_pre, value_pre, bc_pre, delta_pre, params)
        d_mixed = project_back(cotangent_entire, weight_out)
        squares, gate_dot = lax.psum(
            (
                jnp.sum(gated_out * gated_out, axis=-1),
                jnp.sum(d_mixed * gate_gain * gated_out, axis=-1),
            ),
            "tensor",
        )
        scale_gate = lax.rsqrt(squares / INNER + eps)[..., None]
        mixer_output = (gated_out * scale_gate * gate_gain).astype(jnp.bfloat16)
        partial_value = project(mixer_output, weight_out)
        summed = lax.psum_scatter(partial_value, "tensor", scatter_dimension=2, tiled=True)
        outputs.append((local_in.astype(jnp.float32) + summed).astype(jnp.bfloat16))
        grad_out = jnp.einsum(
            "mka,mkg->ag", mixer_output, cotangent_entire, preferred_element_type=jnp.float32
        )
        grad_gate_gain = jnp.sum(d_mixed * gated_out * scale_gate, axis=(0, 1))
        d_gated = (
            scale_gate * gate_gain * d_mixed
            - gated_out * scale_gate**3 * (gate_dot / INNER)[..., None]
        )
        d_gate, d_value, d_bc, d_delta, d_params = pullback(d_gated)
        d_bc, d_conv_weight_bc, d_conv_bias_bc = lax.psum(
            (d_bc, d_params[2], d_params[3]), "tensor"
        )
        low_gate = d_gate.astype(jnp.bfloat16)
        low_value = d_value.astype(jnp.bfloat16)
        low_bc = d_bc.astype(jnp.bfloat16)
        low_delta = d_delta.astype(jnp.bfloat16)
        grad_z = outer_sum(normed, low_gate)
        grad_x = outer_sum(normed, low_value)
        grad_bc = outer_sum(normed, low_bc)
        grad_dt = outer_sum(normed, low_delta)
        d_normed = (
            project_back(low_gate, weight_z)
            + project_back(low_value, weight_x)
            + project_back(low_delta, weight_dt)
        )
        bc_term = project_back(low_bc, bc_share)
        shared_input = lax.dynamic_slice_in_dim(residual, share_start, share_width, 2)
        d_share = lax.psum_scatter(d_normed, "tensor", scatter_dimension=2, tiled=True) + bc_term
        norm_dot = lax.psum(jnp.sum(d_share * gain_share * shared_input, axis=-1), "tensor")
        grad_norm_gain = jnp.sum(d_share * shared_input * scale_in, axis=(0, 1))
        input_grads.append(
            local_cot.astype(jnp.float32)
            + scale_in * gain_share * d_share
            - shared_input * scale_in**3 * (norm_dot / model_width)[..., None]
        )
        big_now = (grad_z, grad_x, grad_bc, grad_dt, grad_out)
        small_now = (
            grad_norm_gain,
            d_params[0],
            d_params[1],
            d_conv_weight_bc,
            d_conv_bias_bc,
            d_params[4],
            d_params[5],
            d_params[6],
            grad_gate_gain,
        )
        big_grads = big_now if big_grads is None else add_tree(big_grads, big_now)
        small_grads = small_now if small_grads is None else add_tree(small_grads, small_now)
    output = jnp.concatenate(outputs, axis=0)
    input_grad = jnp.concatenate(input_grads, axis=0)
    big_grads = (
        lax.psum_scatter(big_grads[0], "dp", scatter_dimension=0, tiled=True),
        lax.psum_scatter(big_grads[1], "dp", scatter_dimension=0, tiled=True),
        lax.psum_scatter(big_grads[2], "dp", scatter_dimension=0, tiled=True),
        lax.psum_scatter(big_grads[3], "dp", scatter_dimension=0, tiled=True),
        lax.psum_scatter(big_grads[4], "dp", scatter_dimension=1, tiled=True),
    )
    small_grads = lax.psum(small_grads, "dp")
    return (
        output,
        input_grad,
        small_grads[0],
        big_grads[0],
        big_grads[1],
        big_grads[2],
        big_grads[3],
        small_grads[1],
        small_grads[2],
        small_grads[3],
        small_grads[4],
        small_grads[5],
        small_grads[6],
        small_grads[7],
        small_grads[8],
        big_grads[4],
    )


def solution(mesh):
    return jax.shard_map(
        per_device,
        mesh=mesh,
        in_specs=(
            P("dp", None, "tensor"),
            P("dp", None),
            P("dp", None, "tensor"),
            P(),
            P(None, "tensor"),
            P(None, "tensor"),
            P(),
            P(None, "tensor"),
            P(None, "tensor"),
            P("tensor"),
            P(),
            P(),
            P("tensor"),
            P("tensor"),
            P("tensor"),
            P("tensor"),
            P("tensor", None),
        ),
        out_specs=(
            P("dp", None, "tensor"),
            P("dp", None, "tensor"),
            P("tensor"),
            P("dp", "tensor"),
            P("dp", "tensor"),
            P("dp", None),
            P("dp", "tensor"),
            P(None, "tensor"),
            P("tensor"),
            P(),
            P(),
            P("tensor"),
            P("tensor"),
            P("tensor"),
            P("tensor"),
            P("tensor", "dp"),
        ),
        check_vma=False,
    )
```

profile of v0, /device:TPU:0, one launch (start us, length us, event | category | flops | bytes accessed | tf_op | source)
XLA Modules:
  0.0 1256.3 jit_solution(11214322786182025757)
XLA Ops:
  14.4 44.7 %all-gather.5.cloned.1.call-done = bf16[1,1024,1024]{2,1,0:T(8,128)(2,1)} async-done(((bf16[1,1024,256]{2,1,0:T(8,128)(2,1)}), bf16[1,1024,1024]{2,1,0:T(8,128)(2,1)}) %all-gather.5.cloned.1.call-update) | async-done | bytes 2097168 | tf_op jit(solution)/shard_map/all_gather | solution.py:161
  62.0 43.8 %all-gather.7.cloned.1.call-done = bf16[1,1024,1024]{2,1,0:T(8,128)(2,1)} async-done(((bf16[1,1024,256]{2,1,0:T(8,128)(2,1)}), bf16[1,1024,1024]{2,1,0:T(8,128)(2,1)}) %all-gather.7.cloned.1.call-update) | async-done | bytes 2097168 | tf_op jit(solution)/shard_map/all_gather | solution.py:161
  123.0 5.0 fusion.299
  128.0 4.9 reshape.2758
  140.0 58.6 %while.91 = (s32[]{:T(128)}, f32[1,8,128,64]{2,3,1,0:T(8,128)}, s32[1]{0:T(128)}, f32[4,1,256,8,64]{2,4,3,1,0:T(8,128)}, f32[4,1,8,128,64]{3,4,2,1,0:T(8,128)}, ...) while((s32[]{:T(128)}, f32[1,8,128,64]{2,3,1,0:T(8,128)}, ...), condition=%wide.region_12.14_spmd.clone, body=%wide.region_9.13_spmd.clone.sunk | while | flops 909716480 | bytes 14458493 | solution.py:73
  202.9 4.8 reshape.2752
  220.8 58.8 %while.90 = (s32[]{:T(128)}, f32[1,8,128,64]{2,3,1,0:T(8,128)}, s32[1]{0:T(128)}, f32[4,1,256,8,64]{2,4,3,1,0:T(8,128)}, f32[4,1,8,128,64]{3,4,2,1,0:T(8,128)}, ...) while((s32[]{:T(128)}, f32[1,8,128,64]{2,3,1,0:T(8,128)}, ...), condition=%wide.region_4.6_spmd.clone, body=%wide.region_1.5_spmd.clone.sunk | while | flops 909716480 | bytes 14458309 | solution.py:73
  283.4 4.8 reshape.2751
  292.4 4.8 multiply_reduce_fusion.23
  297.1 9.4 all-reduce.58
  311.1 7.2 multiply_reduce_fusion.11
  318.3 9.8 all-reduce.57
  328.2 8.7 fusion.281
  340.4 4.7 fusion.270
  357.7 126.6 %while.92 = (s32[]{:T(128)}, f32[1,8,128,64]{2,3,1,0:T(8,128)S(1)}, f32[4,1,256,8,64]{2,4,3,1,0:T(8,128)}, f32[4,1,256,8]{2,3,1,0:T(8,128)}, f32[4,1,256,8]{2,3,...) while((s32[]{:T(128)}, f32[1,8,128,64]{2,3,1,0:T(8,128)S(1)}, ...), condition=%wide.region_31.33_spmd.clone, body=%wide.region_18.32_spmd.clone.sunk | while | flops 2126752768 | bytes 21947920 | solution.py:73
  497.0 128.5 %while.93 = (s32[]{:T(128)}, f32[1,8,128,64]{2,3,1,0:T(8,128)S(1)}, f32[4,1,256,8,64]{2,4,3,1,0:T(8,128)}, f32[4,1,256,8]{2,3,1,0:T(8,128)}, f32[4,1,256,8]{2,3,...) while((s32[]{:T(128)}, f32[1,8,128,64]{2,3,1,0:T(8,128)S(1)}, ...), condition=%wide.region_51.53_spmd.clone, body=%wide.region_38.52_spmd.clone.sunk | while | flops 2126752768 | bytes 20604208 | solution.py:73
  629.3 4.9 reshape.2754
  634.2 8.2 multiply_reduce_fusion.19
  646.2 4.9 reshape.2756
  651.2 6.6 multiply_reduce_fusion.15
  683.7 4.5 convolution_bitcast_fusion.13
  699.0 130.9 %all-reduce.60 = (bf16[1,1024,256]{2,1,0:T(8,128)(2,1)}, bf16[1,1024,256]{2,1,0:T(8,128)(2,1)}) all-reduce(f32[1,1024,256]{2,1,0:T(8,128)} %get-tuple-element.1710, f32[1,1024,256]{2,1,0:T(8,128)} %get-tuple-element.1709), channel_id=1, replica_groups=mesh['dp'=8,'tensor'=4] {'tensor'}, use_global_device_ids=true, to_apply=%region_53.55 | all-reduce | flops 524288 | bytes 3145728 | tf_op jit(solution)/shard_map/psum | solution.py:198
  863.6 14.9 %reduce-scatter.14.cloned.1.call-done = f32[1,1024,256]{2,1,0:T(8,128)} async-done(((f32[1,1024,1024]{2,1,0:T(8,128)}), f32[1,1024,256]{2,1,0:T(8,128)}) %reduce-scatter.14.cloned.1.call-update) | async-done | bytes 1048592 | tf_op jit(solution)/shard_map/reduce_scatter | solution.py:216
  881.5 18.4 %all-reduce.55 = (f32[1,1024]{1,0:T(1,128)S(1)}, f32[1,1024]{1,0:T(1,128)S(1)}, f32[4,256]{1,0:T(4,128)S(1)}, f32[256]{0:T(256)S(1)}) all-reduce(f32[1,1024]{1,0:T(1,128)S(1)} %bitcast.1481, f32[1,1024]{1,0:T(1,128)S(1)} %bitcast.1480, f32[4,256]{1,0:T(4,128)S(1)} %add_add_fusion.1, ...), channel_id=1, replica_groups=mesh['dp'=8,'tensor'=4] {'tensor'}, use_global_device_ids=true, to_apply=%region_55.57 | all-reduce | flops 3328 | bytes 26624 | tf_op jit(solution)/shard_map/psum | solution.py:217
  899.9 24.5 %all-reduce.54 = (f32[256]{0:T(256)}, f32[4,512]{1,0:T(4,128)}, f32[512]{0:T(512)}, f32[4,256]{1,0:T(4,128)}, f32[256]{0:T(256)}, /*index=5*/f32[8]{0:T(128)}, f32[8]{0:T(128)}, f32[8]{0:T(128)}, f32[512]{0:T(512)}) all-reduce(f32[256]{0:T(256)S(1)} %add.531, ...), channel_id=1, replica_groups=mesh['dp'=8,'tensor'=4] {'dp'}, use_global_device_ids=true, to_apply=%region_58.60 | all-reduce | flops 4632 | bytes 37056 | tf_op jit(solution)/shard_map/psum | solution.py:247
  924.4 34.1 %reduce-scatter.12.cloned.1.call-done = f32[1,1024,256]{2,1,0:T(8,128)} async-done(((f32[1,1024,1024]{2,1,0:T(8,128)}), f32[1,1024,256]{2,1,0:T(8,128)}) %reduce-scatter.12.cloned.1.call-update) | async-done | bytes 1048592 | tf_op jit(solution)/shard_map/reduce_scatter | solution.py:187
  958.6 79.6 %reduce-scatter.10.cloned.1.call-done = f32[1,1024,256]{2,1,0:T(8,128)} async-done(((f32[1,1024,1024]{2,1,0:T(8,128)}), f32[1,1024,256]{2,1,0:T(8,128)}) %reduce-scatter.10.cloned.1.call-update) | async-done | bytes 1048592 | tf_op jit(solution)/shard_map/reduce_scatter | solution.py:187
  1045.8 27.7 %reduce-scatter.24.cloned.1.call-done = f32[128,8]{0,1:T(8,128)} async-done(((f32[1024,8]{0,1:T(8,128)}), f32[128,8]{0,1:T(8,128)}) %reduce-scatter.24.cloned.1.call-update) | async-done | bytes 4112 | tf_op jit(solution)/shard_map/reduce_scatter | solution.py:244
  1073.5 40.0 %reduce-scatter.22.cloned.1.call-done = f32[128,256]{1,0:T(8,128)} async-done(((f32[1024,256]{1,0:T(8,128)}), f32[128,256]{1,0:T(8,128)}) %reduce-scatter.22.cloned.1.call-update) | async-done | bytes 131088 | tf_op jit(solution)/shard_map/reduce_scatter | solution.py:243
  1113.5 45.5 %reduce-scatter.26.cloned.1.call-done = f32[512,128]{1,0:T(8,128)} async-done(((f32[512,1024]{1,0:T(8,128)}), f32[512,128]{1,0:T(8,128)}) %reduce-scatter.26.cloned.1.call-update) | async-done | bytes 262160 | tf_op jit(solution)/shard_map/reduce_scatter | solution.py:245
  1159.0 44.9 %reduce-scatter.20.cloned.1.call-done = f32[128,512]{1,0:T(8,128)} async-done(((f32[1024,512]{1,0:T(8,128)}), f32[128,512]{1,0:T(8,128)}) %reduce-scatter.20.cloned.1.call-update) | async-done | bytes 262160 | tf_op jit(solution)/shard_map/reduce_scatter | solution.py:242
  1203.9 45.5 %reduce-scatter.18.cloned.1.call-done = f32[128,512]{1,0:T(8,128)} async-done(((f32[1024,512]{1,0:T(8,128)}), f32[128,512]{1,0:T(8,128)}) %reduce-scatter.18.cloned.1.call-update) | async-done | bytes 262160 | tf_op jit(solution)/shard_map/reduce_scatter | solution.py:241
  (1169 shorter events, 528.3 us)
Async XLA Ops:
  7.2 281.0 %copy-start = (bf16[1024,512]{1,0:T(8,128)(2,1)S(1)}, bf16[1024,512]{1,0:T(8,128)(2,1)}, u32[]{:S(2)}) copy-start(bf16[1024,512]{1,0:T(8,128)(2,1)} %param.30) | copy-start | bytes 3145732
  7.2 51.9 %all-gather.5.cloned.1.call-start = ((), (), s32[]{:S(2)}) async-start(), calls=%async_computation.9 | async-start | bytes 2621440 | tf_op jit(solution)/shard_map/all_gather | solution.py:161
  9.7 96.1 %all-gather.7.cloned.1.call-start = ((), (), s32[]{:S(2)}) async-start(), calls=%async_computation.11 | async-start | bytes 2621440 | tf_op jit(solution)/shard_map/all_gather | solution.py:161
  10.4 296.2 %all-gather.11.cloned.1.call-start = ((), (), s32[]{:S(2)}) async-start(), calls=%async_computation.15 | async-start | bytes 2621440 | tf_op jit(solution)/shard_map/all_gather | solution.py:162
  11.6 299.5 %all-gather.9.cloned.1.call-start = ((), (), s32[]{:S(2)}) async-start(), calls=%async_computation.13 | async-start | bytes 2621440 | tf_op jit(solution)/shard_map/all_gather | solution.py:162
  12.1 849.8 %reduce-scatter.16.cloned.1.call-start = ((), (), s32[]{:S(2)}) async-start(), calls=%async_computation.16 | async-start | bytes 5242880 | tf_op jit(solution)/shard_map/reduce_scatter | solution.py:216
  13.5 109.5 %copy-start.113 = (f32[1,512]{1,0:T(1,128)}, f32[1,512]{1,0:T(1,128)S(1)}, u32[]{:S(2)}) copy-start(f32[1,512]{1,0:T(1,128)S(1)} %get-tuple-element.1669) | copy-start | bytes 6148
  13.5 109.5 %copy-start.115 = (f32[1,512]{1,0:T(1,128)}, f32[1,512]{1,0:T(1,128)S(1)}, u32[]{:S(2)}) copy-start(f32[1,512]{1,0:T(1,128)S(1)} %get-tuple-element.1670) | copy-start | bytes 6148
  13.5 101.8 %copy-start.138 = (f32[8]{0:T(128)}, f32[8]{0:T(128)S(1)}, u32[]{:S(2)}) copy-start(f32[8]{0:T(128)S(1)} %exp.270) | copy-start | bytes 100
  14.3 108.6 %copy-start.79 = (f32[1,1024]{1,0:T(1,128)}, f32[1,1024]{1,0:T(1,128)S(1)}, u32[]{:S(2)}) copy-start(f32[1,1024]{1,0:T(1,128)S(1)} %get-tuple-element.1693) | copy-start | bytes 12292
  14.4 108.6 %copy-start.81 = (f32[1,1024]{1,0:T(1,128)}, f32[1,1024]{1,0:T(1,128)S(1)}, u32[]{:S(2)}) copy-start(f32[1,1024]{1,0:T(1,128)S(1)} %get-tuple-element.1694) | copy-start | bytes 12292
  14.4 108.6 %copy-start.83 = (f32[1,1024]{1,0:T(1,128)}, f32[1,1024]{1,0:T(1,128)S(1)}, u32[]{:S(2)}) copy-start(f32[1,1024]{1,0:T(1,128)S(1)} %get-tuple-element.1695) | copy-start | bytes 12292
  14.4 108.6 %copy-start.85 = (f32[1,1024]{1,0:T(1,128)}, f32[1,1024]{1,0:T(1,128)S(1)}, u32[]{:S(2)}) copy-start(f32[1,1024]{1,0:T(1,128)S(1)} %get-tuple-element.1719) | copy-start | bytes 12292
  14.4 108.6 %copy-start.87 = (f32[1,1024]{1,0:T(1,128)}, f32[1,1024]{1,0:T(1,128)S(1)}, u32[]{:S(2)}) copy-start(f32[1,1024]{1,0:T(1,128)S(1)} %get-tuple-element.1720) | copy-start | bytes 12292
  14.4 108.6 %copy-start.89 = (f32[1,1024]{1,0:T(1,128)}, f32[1,1024]{1,0:T(1,128)S(1)}, u32[]{:S(2)}) copy-start(f32[1,1024]{1,0:T(1,128)S(1)} %get-tuple-element.1721) | copy-start | bytes 12292
  14.4 94.2 %copy-start.137 = (f32[1024]{0:T(1024)S(1)}, f32[1024]{0:T(1024)}, u32[]{:S(2)}) copy-start(f32[1024]{0:T(1024)} %param.29) | copy-start | bytes 12292
  59.1 49.5 %copy-start.10 = (bf16[1,1024,1024]{2,1,0:T(8,128)(2,1)S(1)}, bf16[1,1024,1024]{2,1,0:T(8,128)(2,1)}, u32[]{:S(2)}) copy-start(bf16[1,1024,1024]{2,1,0:T(8,128)(2,1)} %all-gather.5.cloned.1.call-done) | copy-start | bytes 6291460
  62.0 47.9 %copy-start.105 = (f32[1024]{0:T(1024)}, f32[1024]{0:T(1024)S(1)}, u32[]{:S(2)}) copy-start(f32[1024]{0:T(1024)S(1)} %get-tuple-element.1679) | copy-start | bytes 12292
  128.0 209.0 %copy-start.1 = (f32[1,1024,512]{2,1,0:T(8,128)}, f32[1,1024,512]{2,1,0:T(8,128)S(1)}, u32[]{:S(2)}) copy-start(f32[1,1024,512]{2,1,0:T(8,128)S(1)} %get-tuple-element.1666) | copy-start | bytes 6291460
  306.5 30.4 %copy-start.103 = (f32[1,1024]{1,0:T(1,128)}, f32[1,1024]{1,0:T(1,128)S(1)}, u32[]{:S(2)}) copy-start(f32[1,1024]{1,0:T(1,128)S(1)} %add_rsqrt_fusion) | copy-start | bytes 12292
  306.6 30.4 %copy-start.101 = (f32[1,1024]{1,0:T(1,128)}, f32[1,1024]{1,0:T(1,128)S(1)}, u32[]{:S(2)}) copy-start(f32[1,1024]{1,0:T(1,128)S(1)} %add_rsqrt_fusion.2) | copy-start | bytes 12292
  328.2 12.2 copy-start.37
  668.2 210.3 %reduce-scatter.14.cloned.1.call-start = ((), (), s32[]{:S(2)}) async-start(), calls=%async_computation.14 | async-start | bytes 5242880 | tf_op jit(solution)/shard_map/reduce_scatter | solution.py:216
  676.1 282.4 %reduce-scatter.12.cloned.1.call-start = ((), (), s32[]{:S(2)}) async-start(), calls=%async_computation.12 | async-start | bytes 5242880 | tf_op jit(solution)/shard_map/reduce_scatter | solution.py:187
  682.2 356.0 %reduce-scatter.10.cloned.1.call-start = ((), (), s32[]{:S(2)}) async-start(), calls=%async_computation.10 | async-start | bytes 5242880 | tf_op jit(solution)/shard_map/reduce_scatter | solution.py:187
  688.2 385.2 %reduce-scatter.24.cloned.1.call-start = ((), (), s32[]{:S(2)}) async-start(), calls=%async_computation.20 | async-start | bytes 36864 | tf_op jit(solution)/shard_map/reduce_scatter | solution.py:244
  833.4 280.1 %reduce-scatter.22.cloned.1.call-start = ((), (), s32[]{:S(2)}) async-start(), calls=%async_computation.19 | async-start | bytes 1179648 | tf_op jit(solution)/shard_map/reduce_scatter | solution.py:243
  836.6 322.4 %reduce-scatter.26.cloned.1.call-start = ((), (), s32[]{:S(2)}) async-start(), calls=%async_computation.21 | async-start | bytes 2359296 | tf_op jit(solution)/shard_map/reduce_scatter | solution.py:245
  843.1 360.8 %reduce-scatter.20.cloned.1.call-start = ((), (), s32[]{:S(2)}) async-start(), calls=%async_computation.18 | async-start | bytes 2359296 | tf_op jit(solution)/shard_map/reduce_scatter | solution.py:242
  849.1 400.3 %reduce-scatter.18.cloned.1.call-start = ((), (), s32[]{:S(2)}) async-start(), calls=%async_computation.17 | async-start | bytes 2359296 | tf_op jit(solution)/shard_map/reduce_scatter | solution.py:241
  861.8 16.7 %copy-start.106 = (f32[1024]{0:T(1024)S(1)}, f32[1024]{0:T(1024)}, u32[]{:S(2)}) copy-start(f32[1024]{0:T(1024)} %copy-done.105) | copy-start | bytes 12292
  861.8 16.7 %copy-start.108 = (f32[1024]{0:T(1024)S(1)}, f32[1024]{0:T(1024)}, u32[]{:S(2)}) copy-start(f32[1024]{0:T(1024)} %copy-done.107) | copy-start | bytes 12292
  (232 other events, 1113.2 us)
Sparse Core Ops, SparseCore 0:
  10.2 48.9 all-gather.4
  61.3 44.4 all-gather.6
  107.4 44.4 all-gather.10
  153.3 44.4 all-gather.8
  668.4 112.8 reduce-scatter.15
  783.5 94.9 reduce-scatter.13
  880.8 77.7 reduce-scatter.11
  961.0 77.1 reduce-scatter.9
  1041.7 31.7 reduce-scatter.23
  1077.4 36.0 reduce-scatter.21
  1117.7 41.2 reduce-scatter.25
  1162.7 41.1 reduce-scatter.19
  1208.1 41.2 reduce-scatter.17
where the time goes:
time: 1270 us; the launch traced here: 1260 us
  waiting for transfers between devices  422 us (33%)
  matrix products  258 us (20%)
  blocking collectives  193 us (15%)
  local copies, waits for them, and re-layouts  174 us (14%)
  other arithmetic  169 us (13%)
  loops' own time  24.3 us (2%)
  between operations  15.9 us (1%)
    psum x1, blocking collectives, per_device(): lax.psum((d_bc, d_params[2], d_params[3]), 'tensor')  131 us
    reduce_scatter x2, waiting for transfers between devices, per_device(): lax.psum_scatter(partial_value, 'tensor', scatter_dimension=2, tiled=True)  114 us
    dot_general x24, matrix products, advance(): jnp.einsum('stuh,suhp->sthp', mixing, value_blk, precision=lax.Precision....  91.5 us
    all_gather x2, waiting for transfers between devices, per_device(): lax.all_gather(local_in, 'tensor', axis=2, tiled=True)  88.5 us
    reduce_scatter x1, waiting for transfers between devices, per_device(): lax.psum_scatter(big_grads[4], 'dp', scatter_dimension=1, tiled=True)  45.5 us
    reduce_scatter x1, waiting for transfers between devices, per_device(): lax.psum_scatter(big_grads[0], 'dp', scatter_dimension=0, tiled=True)  45.5 us
    reduce_scatter x1, waiting for transfers between devices, per_device(): lax.psum_scatter(big_grads[1], 'dp', scatter_dimension=0, tiled=True)  44.9 us
    reduce_scatter x1, waiting for transfers between devices, per_device(): lax.psum_scatter(big_grads[2], 'dp', scatter_dimension=0, tiled=True)  40 us
  transfers between devices with their start and end apart: 13, of which 10 were waited for; matrix products, arithmetic and copies ran while one was open for 20% of the time, Pallas kernels for 0%

commit v1 on v0

v1 whole, which is shorter than its diff:
```python
import functools

import jax
import jax.numpy as jnp
from jax import lax
from jax.experimental import pallas as pl
from jax.experimental.layout import Layout, with_layout_constraint
from jax.experimental.pallas import tpu as pltpu
from jax.sharding import Mesh
from jax.sharding import PartitionSpec as P

SPAN = 256
HEAD = 64
LANES = 128
LOG2E = 1.4426950408889634
FAR = -1e30
bf16 = jnp.bfloat16
f32 = jnp.float32


def dot_nn(a, b):
    return lax.dot_general(a, b, (((1,), (0,)), ((), ())), preferred_element_type=f32)


def dot_nt(a, b):
    return lax.dot_general(a, b, (((1,), (1,)), ((), ())), preferred_element_type=f32)


def dot_tn(a, b):
    return lax.dot_general(a, b, (((0,), (0,)), ((), ())), preferred_element_type=f32)


def split_dot(a, b, flip=False):
    one = a.astype(bf16)
    two = (a - one.astype(f32)).astype(bf16)
    if flip:
        return dot_nn(b, one) + dot_nn(b, two)
    return dot_nn(one, b) + dot_nn(two, b)


def conv_terms(scr, block, halo, masks):
    span = block.shape[0]
    scr[0:8, :] = halo
    scr[8 : 8 + span, :] = block
    return [block] + [scr[8 - k : 8 - k + span, :] * masks(1 + k) for k in (1, 2, 3)]


def conv_sum(terms, weights, bias):
    total = bias + weights[3:4] * terms[0]
    for k in (1, 2, 3):
        total = total + weights[3 - k : 4 - k] * terms[k]
    return total


def sigmoid(v):
    return 0.5 + 0.5 * jnp.tanh(0.5 * v)


def lanes_of(columns, pair, low):
    return jnp.where(low, columns[:, 2 * pair : 2 * pair + 1], columns[:, 2 * pair + 1 : 2 * pair + 2])


def steps_of(pre, rate, lower, upper):
    dt = jnp.maximum(pre, 0.0) + jnp.log1p(jnp.exp(-jnp.abs(pre)))
    decay = dt * (rate * LOG2E)
    cum, cum_t = None, None
    for _ in range(3):
        part = decay.astype(bf16)
        decay = decay - part.astype(f32)
        one, two = dot_nn(lower, part), dot_tn(part, upper)
        cum, cum_t = (one, two) if cum is None else (cum + one, cum_t + two)
    return dt, cum, cum_t


def forward_kernel(
    v_ref, vh_ref, bc_ref, bch_ref, pre_ref, rate_ref, aux_ref, segc_ref, segr_ref,
    cw_ref, cb_ref, cwb_ref, cbb_ref, skip_ref,
    y_ref, hprev_ref, steps_ref, cumt_ref, state, scr, scrb, far_ref, mask_ref,
):
    span = v_ref.shape[0]
    pairs = v_ref.shape[1] // LANES
    n = bc_ref.shape[1] // 2

    @pl.when(pl.program_id(0) == 0)
    def _():
        state[...] = jnp.zeros_like(state)

    aux = aux_ref[...]
    for i in range(5):
        mask_ref[i] = jnp.broadcast_to(aux[:, i : i + 1], (span, LANES))
    bc_act = conv_sum(conv_terms(scrb, bc_ref[...], bch_ref[...], lambda i: aux[:, i : i + 1]), cwb_ref[...], cbb_ref[...])
    bc_act = bc_act * sigmoid(bc_act)
    b_mat = bc_act[:, :n].astype(bf16)
    c_mat = bc_act[:, n:].astype(bf16)
    scores = dot_nt(c_mat, b_mat)
    later = lax.broadcasted_iota(jnp.int32, (span, span), 0)
    earlier = lax.broadcasted_iota(jnp.int32, (span, span), 1)
    lower = (later >= earlier).astype(f32).astype(bf16)
    upper = (earlier >= later).astype(f32).astype(bf16)
    dt, cum, cum_t = steps_of(pre_ref[...], rate_ref[...], lower, upper)
    far_ref[...] = jnp.where((segc_ref[...] == segr_ref[...]) & (later >= earlier), 0.0, FAR)
    low = lax.broadcasted_iota(jnp.int32, (1, LANES), 1) < HEAD
    steps_ref[...] = jnp.concatenate([dt, cum, sigmoid(pre_ref[...])], axis=1)
    cumt_ref[...] = cum_t
    half = span // 2
    for p in range(pairs):
        sl = slice(p * LANES, (p + 1) * LANES)
        act = conv_sum(conv_terms(scr, v_ref[:, sl], vh_ref[:, sl], lambda i: mask_ref[i]), cw_ref[:, sl], cb_ref[:, sl])
        x = act * sigmoid(act)
        v = (x * lanes_of(dt, p, low)).astype(bf16)
        inside = None
        for e in (0, 1):
            h = 2 * p + e
            mine = jnp.where(low if e == 0 else ~low, v, jnp.zeros_like(v))
            part = []
            for rows, columns in ((slice(0, half), slice(0, half)), (slice(half, span), slice(0, span))):
                spread = (cum[rows, h : h + 1] - cum_t[h : h + 1, columns]) + far_ref[rows, columns]
                mixing = (scores[rows, columns] * jnp.exp2(spread)).astype(bf16)
                part.append(dot_nn(mixing, mine[columns]))
            part = jnp.concatenate(part, axis=0)
            inside = part if inside is None else inside + part
        wide_cum = lanes_of(cum, p, low)
        enter = jnp.exp2(wide_cum) * mask_ref[0]
        tail = jnp.exp2(wide_cum[span - 1 : span] - wide_cum) * mask_ref[1]
        prior = state[:, sl]
        low_prior = prior.astype(bf16)
        hprev_ref[0, :, sl] = low_prior
        outside = dot_nn(c_mat, low_prior) * enter
        y_ref[:, sl] = inside + outside + skip_ref[:, sl] * x
        weighted = (tail * v.astype(f32)).astype(bf16)
        state[:, sl] = enter[span - 1 : span] * prior + dot_tn(b_mat, weighted)


def backward_kernel(
    first, more, shares, where_ref,
    v_ref, vh_ref, bc_ref, bch_ref, steps_ref, rate_ref, aux_ref, segc_ref, segr_ref,
    cw_ref, cb_ref, cwb_ref, cbb_ref, skip_ref, cumt_ref, y_ref, dy_ref, hprev_ref, *rest,
):
    if more:
        before_refs, rest = rest[:shares], rest[shares:]
    dbc_refs, rest = rest[:shares], rest[shares:]
    (
        dv_ref, ddelta_ref, gx_ref, gbc_ref, gh_ref,
        dstate, after, afterb, scr, scrb, far_ref, dscore, dot_y, dot_x, last, tailed, entered, mask_ref,
    ) = rest
    span = v_ref.shape[0]
    channels = v_ref.shape[1]
    pairs = channels // LANES
    heads = channels // HEAD
    everyone = steps_ref.shape[1] // 3
    dt, cum, slope_dt = (steps_ref[:, i * everyone + first : i * everyone + first + heads] for i in range(3))
    rate = rate_ref[:, first : first + heads]
    half = span // 2
    n = bc_ref.shape[1] // 2

    @pl.when(pl.program_id(0) == 0)
    def _():
        for ref in (dstate, after, afterb, gx_ref, gbc_ref, gh_ref):
            ref[...] = jnp.zeros_like(ref)

    aux = aux_ref[...]
    for i in range(8):
        mask_ref[i] = jnp.broadcast_to(aux[:, i : i + 1], (span, LANES))
    terms_bc = conv_terms(scrb, bc_ref[...], bch_ref[...], lambda i: aux[:, i : i + 1])
    act_bc = conv_sum(terms_bc, cwb_ref[...], cbb_ref[...])
    sig_bc = sigmoid(act_bc)
    bc_act = act_bc * sig_bc
    b_mat = bc_act[:, :n].astype(bf16)
    c_mat = bc_act[:, n:].astype(bf16)
    scores = dot_nt(b_mat, c_mat)
    earlier = lax.broadcasted_iota(jnp.int32, (span, span), 0)
    later = lax.broadcasted_iota(jnp.int32, (span, span), 1)
    far_ref[...] = jnp.where((segc_ref[...] == segr_ref[...]) & (later >= earlier), 0.0, FAR)
    low = lax.broadcasted_iota(jnp.int32, (1, LANES), 1) < HEAD
    upper = (later >= earlier).astype(f32).astype(bf16)
    dscore[...] = jnp.zeros_like(dscore)

    def rows_of(value):
        return jnp.sum(value, axis=0, keepdims=True)

    for p in range(pairs):
        sl = slice(p * LANES, (p + 1) * LANES)
        terms = conv_terms(scr, v_ref[:, sl], vh_ref[:, sl], lambda i: mask_ref[i])
        act = conv_sum(terms, cw_ref[:, sl], cb_ref[:, sl])
        sig = sigmoid(act)
        x = act * sig
        dt_lanes = lanes_of(dt, p, low)
        v = (x * dt_lanes).astype(bf16)
        v_wide = v.astype(f32)
        dy = dy_ref[:, sl]
        dy_wide = dy.astype(f32)
        d_inside = None
        for e in (0, 1):
            h = 2 * p + e
            mask = low if e == 0 else ~low
            mine = jnp.where(mask, dy, jnp.zeros_like(dy))
            part = []
            for rows, columns in ((slice(0, half), slice(0, span)), (slice(half, span), slice(half, span))):
                spread = (cumt_ref[first + h : first + h + 1, columns] - cum[rows, h : h + 1]) + far_ref[rows, columns]
                kernel = jnp.exp2(spread)
                mixing = (scores[rows, columns] * kernel).astype(bf16)
                part.append(dot_nn(mixing, mine[columns]))
                dscore[rows, columns] += dot_nt(v[rows], mine[columns]) * kernel
            part = jnp.concatenate(part, axis=0)
            d_inside = part if d_inside is None else d_inside + part
        wide_cum = lanes_of(cum, p, low)
        enter = jnp.exp2(wide_cum) * mask_ref[0]
        tail = jnp.exp2(wide_cum[span - 1 : span] - wide_cum) * mask_ref[1]
        d_new = dstate[:, sl]
        low_new = d_new.astype(bf16)
        d_outer = dot_nn(b_mat, low_new) * tail
        dval = d_inside + d_outer
        skip = skip_ref[:, sl]
        dot_y[:, sl] = dy_wide * (y_ref[:, sl] - skip * x) - v_wide * dval
        dot_x[:, sl] = x * dval
        entering = (enter * dy_wide).astype(bf16)
        entered[:, sl] = entering
        tailed[:, sl] = (tail * v_wide).astype(bf16)
        prior = hprev_ref[0, :, sl]
        carried = enter[span - 1 : span]
        last[:, sl] = rows_of(v_wide * d_outer) + carried * rows_of(prior.astype(f32) * d_new)
        dx = dt_lanes * dval + skip * dy_wide
        dconv = dx * (sig * (1.0 + act * (1.0 - sig)))
        scr[0:span, :] = dconv
        scr[span : span + 8, :] = after[:, sl]
        d_pre = cw_ref[3:4, sl] * dconv
        for k in (1, 2, 3):
            d_pre = d_pre + cw_ref[3 - k : 4 - k, sl] * (scr[k : k + span, :] * mask_ref[4 + k])
        dv_ref[:, sl] = d_pre.astype(bf16)
        after[:, sl] = dconv[0:8]
        for k in (0, 1, 2, 3):
            gx_ref[3 - k : 4 - k, sl] += rows_of(dconv * terms[k])
        gx_ref[4:5, sl] += rows_of(dconv)
        gx_ref[5:6, sl] += rows_of(dy_wide * x)

    ds = dscore[...].astype(bf16)
    d_b = dot_nn(ds, c_mat) + dot_nt(tailed[...], dstate[...].astype(bf16))
    d_c = dot_tn(ds, b_mat) + dot_nt(entered[...], hprev_ref[0])
    slope = sig_bc * (1.0 + act_bc * (1.0 - sig_bc))
    dconv_bc = jnp.concatenate([d_b, d_c], axis=1) * slope
    scrb[0:span, :] = dconv_bc
    scrb[span : span + 8, :] = afterb[...]
    d_pre = cwb_ref[3:4] * dconv_bc
    for k in (1, 2, 3):
        d_pre = d_pre + cwb_ref[3 - k : 4 - k] * (scrb[k : k + span, :] * aux[:, 4 + k : 5 + k])
    cut = 2 * n // shares
    pieces = [d_pre[:, s * cut : (s + 1) * cut] for s in range(shares)]
    own = jnp.full((span, cut), where_ref[0], jnp.int32)
    bit = 1
    while bit < shares:
        pieces = [jnp.where((own & bit) != 0, pieces[s ^ bit], pieces[s]) for s in range(shares)]
        bit *= 2
    for e in range(shares):
        dbc_refs[e][...] = pieces[e] + before_refs[e][...] if more else pieces[e]
    afterb[...] = dconv_bc[0:8]
    for k in (0, 1, 2, 3):
        gbc_ref[3 - k : 4 - k] += rows_of(dconv_bc * terms_bc[k])
    gbc_ref[4:5] += rows_of(dconv_bc)

    for p in range(pairs):
        sl = slice(p * LANES, (p + 1) * LANES)
        carried = jnp.exp2(lanes_of(cum[span - 1 : span], p, low)) * aux[span - 1 : span, 0:1]
        dstate[:, sl] = carried * dstate[:, sl] + dot_tn(c_mat, entered[:, sl])

    place = lax.broadcasted_iota(jnp.int32, (channels, heads), 0) // HEAD
    head = lax.broadcasted_iota(jnp.int32, (channels, heads), 1)
    select = (place == head).astype(bf16)
    d_cum = split_dot(dot_y[...], select)
    final = split_dot(jnp.broadcast_to(last[...], (8, channels)), select)[0:1]
    row = lax.broadcasted_iota(jnp.int32, (span, heads), 0)
    d_cum = d_cum + jnp.where(row == span - 1, final, 0.0)
    d_decay = split_dot(d_cum, upper, flip=True)
    d_dt = split_dot(dot_x[...], select) + d_decay * rate
    d_delta = d_dt * slope_dt
    ddelta_ref[...] = d_delta
    gh_ref[0:1] += rows_of(d_delta)
    gh_ref[1:2] += rows_of(d_decay * dt * rate)


def scan_specs(common, width, column, reverse):
    length, channels = common[0].shape
    wide, heads = common[1].shape[1], common[2].shape[1]
    blocks = length // SPAN
    tall = SPAN // 8

    def at(b):
        return blocks - 1 - b if reverse else b

    def rows(size, at_column=0):
        return pl.BlockSpec((SPAN, size), lambda b, *_: (at(b), at_column))

    def halo(size, at_column=0):
        return pl.BlockSpec((8, size), lambda b, *_: (jnp.maximum(at(b) * tall - 1, 0), at_column))

    def whole(shape, at_column=0):
        return pl.BlockSpec(shape, lambda b, *_: (0, at_column))

    states = pl.BlockSpec((1, wide // 2, width), lambda b, *_: (at(b), 0, column))
    ins = [
        rows(width, column), halo(width, column), rows(wide), halo(wide), rows(heads), whole((1, heads)), rows(8), rows(1),
        pl.BlockSpec((1, SPAN), lambda b, *_: (0, at(b))),
        whole((4, width), column), whole((1, width), column), whole((4, wide)), whole((1, wide)),
        whole((1, width), column),
    ]
    return blocks, rows, whole, states, ins


def forward_scan(common):
    v_pre, bc_pre, pre = common[:3]
    length, channels = v_pre.shape
    wide, heads = bc_pre.shape[1], pre.shape[1]
    blocks, rows, whole, states, ins = scan_specs(common, channels, 0, False)
    return pl.pallas_call(
        forward_kernel,
        grid=(blocks,),
        in_specs=ins,
        out_specs=[rows(channels), states, rows(3 * heads), pl.BlockSpec((heads, SPAN), lambda b: (0, b))],
        out_shape=[
            jax.ShapeDtypeStruct((length, channels), f32),
            jax.ShapeDtypeStruct((blocks, wide // 2, channels), bf16),
            jax.ShapeDtypeStruct((length, 3 * heads), f32), jax.ShapeDtypeStruct((heads, length), f32),
        ],
        scratch_shapes=[
            pltpu.VMEM((wide // 2, channels), f32), pltpu.VMEM((SPAN + 8, LANES), f32),
            pltpu.VMEM((SPAN + 8, wide), f32), pltpu.VMEM((SPAN, SPAN), f32), pltpu.VMEM((5, SPAN, LANES), f32),
        ],
        compiler_params=pltpu.CompilerParams(vmem_limit_bytes=56 * 2**20),
        cost_estimate=pl.CostEstimate(flops=channels * length, bytes_accessed=channels * length, transcendentals=0),
    )(v_pre, v_pre, bc_pre, bc_pre, *common[2:])


def backward_scan(common, half, shares, where, steps, cum_t, y, dy, hprev, before=()):
    v_pre, bc_pre, pre = common[:3]
    length, channels = v_pre.shape[0], v_pre.shape[1] // 2
    wide, heads = bc_pre.shape[1], pre.shape[1] // 2
    blocks, rows, whole, states, ins = scan_specs(common, channels, half, True)
    split = rows(wide // shares)
    ins[4] = rows(steps.shape[1])
    sums = pl.BlockSpec((2 * heads, SPAN), lambda b, *_: (0, blocks - 1 - b))
    out = pl.pallas_call(
        functools.partial(backward_kernel, half * heads, bool(before), shares),
        grid_spec=pltpu.PrefetchScalarGridSpec(
            num_scalar_prefetch=1,
            grid=(blocks,),
            in_specs=ins + [sums, rows(channels, half), rows(channels, half), states] + [split] * len(before),
            out_specs=[split] * shares
            + [rows(channels), rows(heads), whole((8, channels)), whole((8, wide)), whole((8, heads))],
            scratch_shapes=[
                pltpu.VMEM((wide // 2, channels), f32), pltpu.VMEM((8, channels), f32), pltpu.VMEM((8, wide), f32),
                pltpu.VMEM((SPAN + 8, LANES), f32), pltpu.VMEM((SPAN + 8, wide), f32), pltpu.VMEM((SPAN, SPAN), f32),
                pltpu.VMEM((SPAN, SPAN), f32), pltpu.VMEM((SPAN, channels), f32), pltpu.VMEM((SPAN, channels), f32),
                pltpu.VMEM((1, channels), f32), pltpu.VMEM((SPAN, channels), bf16), pltpu.VMEM((SPAN, channels), bf16),
                pltpu.VMEM((8, SPAN, LANES), f32),
            ],
        ),
        out_shape=[jax.ShapeDtypeStruct((length, wide // shares), f32)] * shares
        + [
            jax.ShapeDtypeStruct((length, channels), bf16), jax.ShapeDtypeStruct((length, heads), f32),
            jax.ShapeDtypeStruct((8, channels), f32), jax.ShapeDtypeStruct((8, wide), f32),
            jax.ShapeDtypeStruct((8, heads), f32),
        ],
        compiler_params=pltpu.CompilerParams(vmem_limit_bytes=56 * 2**20),
        cost_estimate=pl.CostEstimate(flops=channels * length, bytes_accessed=channels * length, transcendentals=0),
    )(where, v_pre, v_pre, bc_pre, bc_pre, steps, *common[3:], cum_t, y, dy, hprev, *before)
    return tuple(out[:shares]), *out[shares:]


def assemble(moves, index, sources, shape):
    def kernel(index_ref, *refs):
        out_ref = refs[-1]
        at = index_ref[0]
        for source, lead, rows, base, stride, offset, columns in moves:
            start = pl.multiple_of(base + (at ^ offset) * stride, stride)
            out_ref[pl.ds(start, rows.stop - rows.start), columns] = refs[source][(*lead, rows, slice(None))]

    return pl.pallas_call(
        kernel,
        grid_spec=pltpu.PrefetchScalarGridSpec(
            num_scalar_prefetch=1,
            grid=(1,),
            in_specs=[pl.BlockSpec(v.shape, lambda i, s, rank=v.ndim: (0,) * rank) for v in sources],
            out_specs=pl.BlockSpec(shape, lambda i, s: (0, 0)),
        ),
        out_shape=jax.ShapeDtypeStruct(shape, bf16),
        compiler_params=pltpu.CompilerParams(vmem_limit_bytes=10 * 2**20),
        cost_estimate=pl.CostEstimate(flops=0, bytes_accessed=4 * shape[0] * shape[1], transcendentals=0),
    )(index.reshape(1), *sources)


def rows_in_order(shares, blocks):
    each = blocks // shares

    def at(i, where_ref):
        return (where_ref[0] ^ (shares - 1 - i // each)) * each + i % each

    return each, at


def pick_part(shares, parts, cot):
    each = pl.num_programs(0) // shares
    for e in range(shares):
        @pl.when(pl.program_id(0) // each == shares - 1 - e)
        def _(e=e):
            cot[...] = parts[e][...]


def gate_kernel(shares, where_ref, normed_ref, wz_ref, y_ref, wo_ref, gain_ref, *refs):
    parts, (stats_ref, sent_ref, kept_ref, cot) = refs[:shares], refs[shares:]
    span, model = cot.shape
    pick_part(shares, parts, cot)
    half = model // 2
    sent_ref[...] = cot[:, pl.ds(pl.multiple_of((1 - where_ref[1]) * half, half), half)].T
    kept_ref[...] = cot[:, pl.ds(pl.multiple_of(where_ref[1] * half, half), half)].T
    gate = dot_nn(normed_ref[...], wz_ref[...])
    d_mixed = dot_nt(cot[...], wo_ref[...])
    gated = y_ref[...] * (gate * sigmoid(gate))
    squares = jnp.sum(gated * gated, axis=1, keepdims=True)
    product = jnp.sum(d_mixed * gain_ref[...] * gated, axis=1, keepdims=True)
    lane = lax.broadcasted_iota(jnp.int32, (span, LANES), 1)
    both = jnp.where(lane == 0, squares, jnp.where(lane == 1, product, 0.0))
    stats_ref[...] = both.T[0:8]


def norm_kernel(
    shares, inner, where_ref, normed_ref, wz_ref, y_ref, wo_ref, gain_ref, stats_ref, *refs
):
    parts, refs = refs[:shares], refs[shares:]
    mixed_ref, dy_ref, dgate_ref, ggain_ref, sent_ref, kept_ref, cot, gate_ref, dmix_ref = refs

    @pl.when(pl.program_id(0) == 0)
    def _():
        ggain_ref[...] = jnp.zeros_like(ggain_ref)

    pick_part(shares, parts, cot)
    gate_ref[...] = dot_nn(normed_ref[...], wz_ref[...])
    dmix_ref[...] = dot_nt(cot[...], wo_ref[...])
    stats = jnp.concatenate([stats_ref[...]] + [jnp.zeros((LANES - 8, stats_ref.shape[1]), f32)], axis=0).T
    scale = lax.rsqrt(stats[:, 0:1] * (1.0 / inner) + 1e-05)
    factor = scale * scale * scale * (stats[:, 1:2] * (1.0 / inner))
    for at in range(0, y_ref.shape[1], LANES):
        sl = slice(at, at + LANES)
        y, gate, gain = y_ref[:, sl], gate_ref[:, sl], gain_ref[:, sl]
        sig = sigmoid(gate)
        silu = gate * sig
        gated = y * silu
        scaled = dmix_ref[:, sl] * scale
        mixed_ref[:, sl] = (gated * scale * gain).astype(bf16)
        d_gated = scaled * gain - gated * factor
        dy_ref[:, sl] = (d_gated * silu).astype(bf16)
        dgate_ref[:, sl] = (d_gated * y * (sig + silu * (1.0 - sig))).astype(bf16)
        ggain_ref[0:1, sl] += jnp.sum(scaled * gated, axis=0, keepdims=True)
    result = dot_nn(mixed_ref[...], wo_ref[...])
    each = pl.num_programs(0) // shares

    @pl.when(pl.program_id(0) < (shares - 1) * each)
    def _():
        sent_ref[...] = result.astype(bf16)

    @pl.when(pl.program_id(0) >= (shares - 1) * each)
    def _():
        kept_ref[...] = result


def gated_specs(shares, normed, y):
    length, model = normed.shape
    channels = y.shape[1]
    blocks = length // SPAN
    each, at = rows_in_order(shares, blocks)

    def rows(size):
        return pl.BlockSpec((SPAN, size), lambda i, s: (at(i, s), 0))

    def whole(shape):
        return pl.BlockSpec(shape, lambda i, s: (0, 0))

    ins = [rows(model), whole((model, channels)), rows(channels), whole((channels, model)), whole((1, channels))]
    parts = [pl.BlockSpec((SPAN, model), lambda i, s: (i % each, 0))] * shares
    return blocks, each, at, rows, whole, ins, parts


def gate_step(shares, where, normed, w_z, y, w_out, gain, cot_parts):
    length, model = normed.shape
    channels = y.shape[1]
    blocks, each, at, rows, whole, ins, parts = gated_specs(shares, normed, y)
    tall = pl.BlockSpec((model // 2, SPAN), lambda i, s: (0, at(i, s)))
    return pl.pallas_call(
        functools.partial(gate_kernel, shares),
        grid_spec=pltpu.PrefetchScalarGridSpec(
            num_scalar_prefetch=1,
            grid=(blocks,),
            in_specs=ins + parts,
            out_specs=[pl.BlockSpec((8, SPAN), lambda i, s: (0, at(i, s))), tall, tall],
            scratch_shapes=[pltpu.VMEM((SPAN, model), bf16)],
        ),
        out_shape=[
            jax.ShapeDtypeStruct((8, length), f32), jax.ShapeDtypeStruct((model // 2, length), bf16),
            jax.ShapeDtypeStruct((model // 2, length), bf16),
        ],
        compiler_params=pltpu.CompilerParams(vmem_limit_bytes=20 * 2**20),
        cost_estimate=pl.CostEstimate(flops=4 * length * model * channels, bytes_accessed=8 * length * channels, transcendentals=0),
    )(where, normed, w_z, y, w_out, gain, *cot_parts)


def norm_step(shares, inner, where, normed, w_z, y, w_out, gain, stats, cot_parts):
    length, model = normed.shape
    channels = y.shape[1]
    blocks, each, at, rows, whole, ins, parts = gated_specs(shares, normed, y)
    many = (shares - 1) * each
    return pl.pallas_call(
        functools.partial(norm_kernel, shares, inner),
        grid_spec=pltpu.PrefetchScalarGridSpec(
            num_scalar_prefetch=1,
            grid=(blocks,),
            in_specs=ins + [pl.BlockSpec((8, SPAN), lambda i, s: (0, at(i, s)))] + parts,
            out_specs=[
                rows(channels), rows(channels), rows(channels), whole((8, channels)),
                pl.BlockSpec((SPAN, model), lambda i, s: (jnp.minimum(i, many - 1), 0)),
                pl.BlockSpec((SPAN, model), lambda i, s: (jnp.maximum(i - many, 0), 0)),
            ],
            scratch_shapes=[
                pltpu.VMEM((SPAN, model), bf16), pltpu.VMEM((SPAN, channels), f32), pltpu.VMEM((SPAN, channels), f32)
            ],
        ),
        out_shape=[jax.ShapeDtypeStruct((length, channels), bf16)] * 3
        + [
            jax.ShapeDtypeStruct((8, channels), f32), jax.ShapeDtypeStruct((many * SPAN, model), bf16),
            jax.ShapeDtypeStruct((each * SPAN, model), f32),
        ],
        compiler_params=pltpu.CompilerParams(vmem_limit_bytes=26 * 2**20),
        cost_estimate=pl.CostEstimate(flops=6 * length * model * channels, bytes_accessed=18 * length * channels, transcendentals=0),
    )(where, normed, w_z, y, w_out, gain, stats, *cot_parts)


def cut_kernel(size, where_ref, source_ref, sent_ref, kept_ref, turned):
    turned[...] = source_ref[...].T
    for i in range(sent_ref.shape[0] // size):
        to = slice(i * size, (i + 1) * size)
        sent_ref[to] = turned[pl.ds(pl.multiple_of((2 * i + 1 - where_ref[2]) * size, size), size)]
        kept_ref[to] = turned[pl.ds(pl.multiple_of((2 * i + where_ref[2]) * size, size), size)]


def cut_step(groups, where, source):
    length, model = source.shape
    out = pl.BlockSpec((model // 2, length), lambda i, s: (0, 0))
    return pl.pallas_call(
        functools.partial(cut_kernel, model // groups),
        grid_spec=pltpu.PrefetchScalarGridSpec(
            num_scalar_prefetch=1,
            grid=(1,),
            in_specs=[pl.BlockSpec((length, model), lambda i, s: (0, 0))],
            out_specs=[out, out],
            scratch_shapes=[pltpu.VMEM((model, length), bf16)],
        ),
        out_shape=[jax.ShapeDtypeStruct((model // 2, length), bf16)] * 2,
        compiler_params=pltpu.CompilerParams(vmem_limit_bytes=14 * 2**20),
        cost_estimate=pl.CostEstimate(flops=0, bytes_accessed=4 * length * model, transcendentals=0),
    )(where, source)


def base_kernel(gate_ref, wz_ref, value_ref, wx_ref, out_ref):
    out_ref[...] = dot_nt(gate_ref[...], wz_ref[...]) + dot_nt(value_ref[...], wx_ref[...])


def base_step(d_gate, w_z, d_value, w_x):
    length, channels = d_gate.shape
    model = w_z.shape[0]
    width = d_value.shape[1]

    def rows(size):
        return pl.BlockSpec((SPAN, size), lambda b: (b, 0))

    return pl.pallas_call(
        base_kernel,
        grid=(length // SPAN,),
        in_specs=[
            rows(channels), pl.BlockSpec((model, channels), lambda b: (0, 0)), rows(width),
            pl.BlockSpec((model, width), lambda b: (0, 0)),
        ],
        out_specs=rows(model),
        out_shape=jax.ShapeDtypeStruct((length, model), f32),
        compiler_params=pltpu.CompilerParams(vmem_limit_bytes=13 * 2**20),
        cost_estimate=pl.CostEstimate(flops=3 * length * channels * model, bytes_accessed=8 * length * channels, transcendentals=0),
    )(d_gate, w_z, d_value, w_x)


def last_kernel(shares, where_ref, *refs):
    own, parts, refs = refs[:shares], refs[shares : 2 * shares], refs[2 * shares :]
    dv_ref, one_ref, two_ref, base_ref, wx_ref, wb_ref, wd_ref, sent_ref, kept_ref, low_ref, gain_ref, u_ref = refs

    @pl.when(pl.program_id(0) == 0)
    def _():
        gain_ref[...] = jnp.zeros_like(gain_ref)

    pick_part(shares, parts, u_ref)
    low = own[0][...]
    for ref in own[1:]:
        low = low + ref[...]
    low = low.astype(bf16)
    low_ref[...] = low
    steps = jnp.concatenate([one_ref[...], two_ref[...]], axis=1).astype(bf16)
    total = dot_nt(dv_ref[...], wx_ref[...]) + dot_nt(low, wb_ref[...]) + dot_nn(steps, wd_ref[...]) + base_ref[...]
    u = u_ref[...].astype(f32)
    scale = lax.rsqrt(jnp.sum(u * u, axis=1, keepdims=True) * (1.0 / u.shape[1]) + 1e-05)
    gain_ref[0:1] += jnp.sum(total * (u * scale), axis=0, keepdims=True)
    each = pl.num_programs(0) // shares

    @pl.when(pl.program_id(0) < (shares - 1) * each)
    def _():
        sent_ref[...] = total.astype(bf16)

    @pl.when(pl.program_id(0) >= (shares - 1) * each)
    def _():
        kept_ref[...] = total


def last_step(shares, where, d_bcs, u_parts, d_value, steps, base, w_x, share_bc, w_dt):
    length, width = d_value.shape
    model = base.shape[1]
    blocks = length // SPAN
    each, at = rows_in_order(shares, blocks)

    def rows(size):
        return pl.BlockSpec((SPAN, size), lambda i, s: (at(i, s), 0))

    def whole(value):
        return pl.BlockSpec(value.shape, lambda i, s: (0, 0))

    many = (shares - 1) * each
    narrow = d_bcs[0].shape[1]
    return pl.pallas_call(
        functools.partial(last_kernel, shares),
        grid_spec=pltpu.PrefetchScalarGridSpec(
            num_scalar_prefetch=1,
            grid=(blocks,),
            in_specs=[rows(narrow)] * shares
            + [pl.BlockSpec((SPAN, model), lambda i, s: (i % each, 0))] * shares
            + [rows(width), rows(steps[0].shape[1]), rows(steps[1].shape[1]), rows(model)]
            + [pl.BlockSpec((model, width), lambda i, s: (0, 1)), whole(share_bc), whole(w_dt)],
            out_specs=[
                pl.BlockSpec((SPAN, model), lambda i, s: (jnp.minimum(i, many - 1), 0)),
                pl.BlockSpec((SPAN, model), lambda i, s: (jnp.maximum(i - many, 0), 0)),
                rows(narrow),
                pl.BlockSpec((8, model), lambda i, s: (0, 0)),
            ],
            scratch_shapes=[pltpu.VMEM((SPAN, model), bf16)],
        ),
        out_shape=[
            jax.ShapeDtypeStruct((many * SPAN, model), bf16), jax.ShapeDtypeStruct((each * SPAN, model), f32),
            jax.ShapeDtypeStruct((length, narrow), bf16), jax.ShapeDtypeStruct((8, model), f32),
        ],
        compiler_params=pltpu.CompilerParams(vmem_limit_bytes=56 * 2**20),
        cost_estimate=pl.CostEstimate(flops=2 * length * width * model, bytes_accessed=8 * length * model, transcendentals=0),
    )(where, *d_bcs, *u_parts, d_value, *steps, base, w_x, share_bc, w_dt)


def input_kernel(tensor, *refs):
    parts, (u_ref, gain_ref, out_ref) = refs[:-3], refs[-3:]
    d_part = parts[0][...]
    for ref in parts[1:]:
        d_part = d_part + ref[...].astype(f32)
    u = u_ref[...].astype(f32)
    model = u.shape[1]
    scale = lax.rsqrt(jnp.sum(u * u, axis=1, keepdims=True) * (1.0 / model) + 1e-05)
    weighted = d_part * gain_ref[...]
    dot = jnp.sum(weighted * u, axis=1, keepdims=True)
    d_input = (scale * weighted - u * (scale * scale * scale * (dot * (1.0 / model)))).astype(bf16)
    width = model // tensor
    for i in range(tensor):
        out_ref[i] = d_input[:, i * width : (i + 1) * width]


def input_step(tensor, parts, u_part, norm_gain):
    rows_in, model = u_part.shape
    rows = pl.BlockSpec((SPAN, model), lambda b: (b, 0))
    return pl.pallas_call(
        functools.partial(input_kernel, tensor),
        grid=(rows_in // SPAN,),
        in_specs=[rows] * (len(parts) + 1) + [pl.BlockSpec((1, model), lambda b: (0, 0))],
        out_specs=pl.BlockSpec((tensor, SPAN, model // tensor), lambda b: (0, b, 0)),
        out_shape=jax.ShapeDtypeStruct((tensor, rows_in, model // tensor), bf16),
        compiler_params=pltpu.CompilerParams(vmem_limit_bytes=10 * 2**20),
        cost_estimate=pl.CostEstimate(flops=10 * rows_in * model, bytes_accessed=10 * rows_in * model, transcendentals=0),
    )(*parts, u_part, norm_gain)


def finish_kernel(tensor, model, wide, heads, cells, where_ref, last_ref, *out_refs):
    width = last_ref.shape[2]
    lines = (last_ref.shape[1] - cells) // 3
    parts = None
    for i in range(tensor):
        for n in (2, 1, 0):
            piece = last_ref[i, cells + n * lines : cells + (n + 1) * lines].astype(f32)
            parts = piece if parts is None else parts + piece
    conv_ref, bias_ref, gain_ref, step_ref, decay_ref, skip_ref, norm_ref, bc_ref, bc_bias_ref = out_refs
    conv_ref[...] = parts[0:4]
    bias_ref[...] = parts[4]
    gain_ref[...] = parts[5]
    for n, ref in enumerate((step_ref, decay_ref, skip_ref)):
        ref[...] = parts[6, n * heads : (n + 1) * heads]

    def shared(start, size):
        return parts[7 + start // width, start % width : start % width + size]

    size = model // tensor
    norm = shared(0, size)
    at = jnp.full((size,), where_ref[3], jnp.int32)
    for i in range(1, tensor):
        norm = jnp.where(at == i, shared(i * size, size), norm)
    norm_ref[...] = norm
    for n in range(4):
        bc_ref[n] = shared(model + n * wide, wide)
    bc_bias_ref[...] = shared(model + 4 * wide, wide)


def finish_step(where, last, cells, model, wide, heads):
    tensor, _, width = last.shape
    shapes = [(4, width), (width,), (width,), (heads,), (heads,), (heads,), (model // tensor,), (4, wide), (wide,)]
    return pl.pallas_call(
        functools.partial(finish_kernel, tensor, model, wide, heads, cells),
        grid_spec=pltpu.PrefetchScalarGridSpec(
            num_scalar_prefetch=1,
            grid=(1,),
            in_specs=[pl.BlockSpec(last.shape, lambda i, s: (0, 0, 0))],
            out_specs=[pl.BlockSpec(v, lambda i, s, rank=len(v): (0,) * rank) for v in shapes],
        ),
        out_shape=[jax.ShapeDtypeStruct(v, f32) for v in shapes],
        compiler_params=pltpu.CompilerParams(vmem_limit_bytes=6 * 2**20),
    )(where, last)


EPS = 1e-05
AXES = ("g", "c", "t")


def tie(value, *others):
    return lax.optimization_barrier((value, *others))[0]


def row_major(value):
    return with_layout_constraint(value, Layout(major_to_minor=tuple(range(value.ndim))))


def thirds(value):
    parts = []
    for _ in range(3):
        part = lax.reduce_precision(value, 8, 7)
        parts.append(part.astype(bf16))
        value = value - part
    return parts


def side_by_side(value, width):
    each = width // value.shape[1]
    rows = value.shape[0] // each
    return jnp.concatenate([value[i * rows : (i + 1) * rows] for i in range(each)], axis=1)


def one_by_one(value, width):
    return jnp.concatenate([value[:, i : i + width] for i in range(0, value.shape[1], width)], axis=0)


def order_by_xor(pieces, index):
    bit = 1
    while bit < len(pieces):
        flip = (index & bit) != 0
        pieces = [jnp.where(flip, pieces[i ^ bit], pieces[i]) for i in range(len(pieces))]
        bit *= 2
    return pieces


class Plan:
    def __init__(self, groups, tensor, per_dp):
        self.groups, self.tensor, self.per_dp = groups, tensor, per_dp
        self.k = tensor // (2 * per_dp)
        self.shares = 2 * self.k
        self.seqs = 2 * per_dp
        self.t = lax.axis_index("t")
        self.c = lax.axis_index("c")
        self.g = lax.axis_index("g")
        self.seq = self.t // self.k
        self.share = self.c * self.k + self.t % self.k
        self.piece = (self.seq % per_dp) * self.shares + self.share
        self.bits = [1 << b for b in range(groups.bit_length() - 1)]

    def send(self, value, where):
        def number(g, c, t):
            return (g * 2 + c) * self.tensor + t

        pairs = [
            (number(g, c, t), number(*where(g, c, t)))
            for g in range(self.groups) for c in range(2) for t in range(self.tensor)
        ]
        return lax.ppermute(value, AXES, pairs)

    def across(self, value, e):
        k = self.k

        def where(g, c, t):
            other = (c * k + t % k) ^ e
            return g, other // k, t // k * k + other % k

        return self.send(value, where)

    def around(self, value, e):
        return self.send(value, lambda g, c, t: (g ^ e, c, t))

    def along(self, value, e):
        return self.send(value, lambda g, c, t: (g, c, t ^ (e * self.k)))

    def swap_for_sequence(self, sources):
        per_dp, length, width = sources[0].shape
        halves = [v.reshape(per_dp, 2, length // 2, width) for v in sources]
        sent = jnp.stack([lax.dynamic_index_in_dim(v, 1 - self.c, 1, keepdims=False) for v in halves])
        got = self.send(sent, lambda g, c, t: (g, 1 - c, t))
        out = []
        for i, v in enumerate(halves):
            kept = lax.dynamic_index_in_dim(v, self.c, 1, keepdims=False)
            out.append(jnp.concatenate(order_by_xor([kept, got[i]], self.c), axis=0))
        return out

    def to_sequence(self, source):
        seqs, rows, width = source.shape
        return lax.all_to_all(source.reshape(self.tensor, rows // self.k, width), "t", 0, 0, tiled=True)

    def pieces_of_sequence(self, got):
        return jnp.concatenate([got[i] for i in range(self.tensor)], axis=1)

    def blocks_back(self, source):
        width = source.shape[1] // self.tensor
        return jnp.stack([source[:, i * width : (i + 1) * width] for i in range(self.tensor)])

    def from_sequence(self, blocks):
        got = lax.all_to_all(blocks, "t", 0, 0, tiled=True)
        return got.reshape(self.seqs, self.k * blocks.shape[1], blocks.shape[2])

    def pieces_of_batch(self, got):
        per_dp = self.per_dp
        kept = lax.dynamic_slice_in_dim(got, self.c * per_dp, per_dp, 0)
        sent = lax.dynamic_slice_in_dim(got, (1 - self.c) * per_dp, per_dp, 0)
        other = self.send(sent, lambda g, c, t: (g, 1 - c, t))
        return jnp.concatenate(order_by_xor([kept, other], self.c), axis=1)

    def gather_shares(self, part):
        got = [part] + [self.across(part, e) for e in range(1, self.shares)]
        return jnp.concatenate(order_by_xor(got, self.share), axis=0)

    def sum_part(self, whole, axis, wire):
        size = whole.shape[axis] // self.shares
        total = lax.dynamic_slice_in_dim(whole, self.share * size, size, axis)
        for e in range(1, self.shares):
            other = lax.dynamic_slice_in_dim(whole, (self.share ^ e) * size, size, axis).astype(wire)
            total = total + self.across(other, e).astype(f32)
        return total

    def sum_shares(self, value):
        e = 1
        while e < self.shares:
            value = value + self.across(value, e)
            e *= 2
        return value

    def slot(self, value, j):
        def where(g, c, t):
            share = t // 2
            return g, share // self.k, (2 * c + (j ^ (t & 1))) * self.k + share % self.k

        return self.send(value, where)

    def unslot(self, value, j1, j0):
        def where(g, c, t):
            seq, share = t // self.k, c * self.k + t % self.k
            return g, j1 ^ (seq >> 1), 2 * share + (j0 ^ (seq & 1))

        return self.send(value, where)

    def slice_of(self, whole):
        size = whole.shape[0] // self.groups
        return lax.dynamic_slice_in_dim(whole, self.g * size, size, 0)

    def spread(self, piece, first, until=None):
        held = piece[None]
        bits = self.bits if first else self.bits[::-1]
        offsets = [0]
        for bit in bits:
            got = self.around(held, bit)
            more = [off | bit for off in offsets]
            if bit == bits[-1]:
                return [held, got if until is None else tie(got, until)], [offsets, more]
            held = jnp.concatenate([held, got], axis=0)
            offsets = offsets + more

    def halves(self, source, first):
        bit = self.bits[0] if first else self.bits[-1]
        size = source.shape[1] // self.groups
        own = self.g & bit
        out = []
        for at in (bit - own, own):
            blocks = [
                lax.dynamic_slice_in_dim(source, (r + at) * size, size, 1) for r in range(self.groups) if not r & bit
            ]
            out.append(jnp.concatenate(blocks, axis=1))
        return out

    def first_send(self, sent, first):
        return self.around(sent, self.bits[0] if first else self.bits[-1])

    def next_sums(self, held, first, after=()):
        bits = self.bits[1:] if first else self.bits[-2::-1]
        left = len(bits)
        held = held.reshape((2,) * left + (-1, held.shape[-1]))
        for bit in bits:
            axis = left - 1 if first else 0
            mine = ((self.g & bit) != 0).astype(jnp.int32)
            sent = lax.dynamic_index_in_dim(held, 1 - mine, axis, keepdims=False).astype(bf16)
            kept = lax.dynamic_index_in_dim(held, mine, axis, keepdims=False)
            got = self.around(sent, bit)
            left -= 1
            if left == 0:
                return sent, kept, got
            held = kept + got.astype(f32)

    def slot_blocks(self, held):
        half = held[0].shape[-2] // 2
        return [
            lax.dynamic_slice_in_dim(value, (j1 ^ (self.seq >> 1)) * half, half, value.ndim - 2).astype(bf16)
            for value in held for j1 in (0, 1)
        ]

    def slot_sends(self, blocks, slots):
        return [self.unslot(blocks[2 * i + j1], j1, j0) for i, j0 in enumerate(slots) for j1 in (0, 1)]

    def slot_total(self, got):
        return sum(v.astype(f32) for v in got)


def per_device(
    groups, tensor,
    inputs, segment, cotangent, norm_gain, weight_z, weight_x, weight_bc, weight_dt, conv_weight_x, conv_bias_x,
    conv_weight_bc, conv_bias_bc, step_bias, decay_log, skip_gain, gate_gain, weight_out,
):
    plan = Plan(groups, tensor, inputs.shape[0])
    shares = plan.shares
    length = inputs.shape[1]
    model = norm_gain.shape[0]
    width = conv_bias_x.shape[0]
    heads = step_bias.shape[0]
    wide = conv_bias_bc.shape[0]
    inner = width * tensor
    two = (0, 1)

    other = plan.send(segment, lambda g, c, t: (g, 1 - c, t))
    both_seg = jnp.where(plan.c == 0, jnp.concatenate([segment, other]), jnp.concatenate([other, segment]))
    seg = lax.dynamic_index_in_dim(both_seg, plan.seq, 0, keepdims=False)
    blocks = seg.reshape(length // SPAN, SPAN)
    ends = blocks[:, -1]
    starts = jnp.concatenate([jnp.full((1,), -1, jnp.int32), ends[:-1]])
    flags = [(blocks == starts[:, None]).reshape(length), (blocks == ends[:, None]).reshape(length)]
    flags += [jnp.concatenate([jnp.zeros((k,), bool), seg[k:] == seg[:-k]]) for k in (1, 2, 3)]
    flags += [jnp.concatenate([seg[k:] == seg[:-k], jnp.zeros((k,), bool)]) for k in (1, 2, 3)]
    aux = jnp.stack(flags, axis=1).astype(f32)
    seg_column, seg_row = seg[:, None], seg[None]
    head_row = jnp.zeros((1, width), f32)
    head_row = lax.dynamic_update_slice(head_row, jnp.concatenate([step_bias, decay_log, skip_gain])[None], (0, 0))
    exact = jnp.concatenate([conv_weight_x, conv_bias_x[None], gate_gain[None], head_row], axis=0)
    row_count = exact.shape[0]
    riders = [weight_dt.T.reshape(-1, width)] + thirds(exact)
    dt_rows = riders[0].shape[0]
    riders = jnp.concatenate(riders, axis=0)
    riders = jnp.pad(riders, ((0, -riders.shape[0] % 16), (0, 0)))
    mine_x = jnp.concatenate([plan.slice_of(weight_x), riders], axis=0)
    size = model // groups
    x_slots = [plan.slot(mine_x, j) for j in two]
    riders = [x_slots[j][size:] for j in two]
    mine_o = plan.slice_of(weight_out)
    mine = jnp.stack([plan.slice_of(weight_z), jnp.concatenate([mine_o[:, i : i + width] for i in range(0, model, width)], axis=0)])
    zo_slots = [plan.slot(tie(mine, *x_slots), j) for j in two]
    swapped_u, swapped_cot = plan.swap_for_sequence([inputs, cotangent])
    spread_x = [plan.spread(x_slots[j][:size], j == 0) for j in two]
    got_u = plan.to_sequence(tie(swapped_u, aux, seg_column, seg_row, spread_x[0][0][0], spread_x[1][0][0], *zo_slots))
    stacks, moves = [], []
    for j in two:
        found, offsets = spread_x[j]
        for stack, offs in zip(found, offsets):
            moves += [
                (len(stacks), (i,), slice(0, size), 0, size, off, slice(j * width, (j + 1) * width))
                for i, off in enumerate(offs)
            ]
            stacks.append(stack)
    w_x = assemble(moves, plan.g, stacks, (model, 2 * width))
    all_z = plan.spread(jnp.stack([zo_slots[j][0] for j in two]), True)
    all_o = plan.spread(jnp.stack([zo_slots[j][1] for j in two]), False)
    share_bc = lax.dynamic_slice_in_dim(weight_bc, plan.share * (wide // shares), wide // shares, 1)
    w_dt = [v[:dt_rows].reshape(heads, model) for v in riders]
    slots = [
        sum(v[dt_rows + i * row_count : dt_rows + (i + 1) * row_count].astype(f32) for i in (2, 1, 0)) for v in riders
    ]
    rows = jnp.concatenate(slots, axis=1)
    conv_w, conv_b, gain = rows[0:4], rows[4:5], rows[5:6]
    bias, log_rate, skip = (
        jnp.concatenate([v[6:7, i * heads : (i + 1) * heads] for v in slots], axis=1) for i in range(3)
    )
    w_dt = jnp.concatenate(w_dt, axis=0)
    rate, skip_lanes = -jnp.exp(log_rate), jnp.repeat(skip, HEAD, axis=1)
    where = jnp.stack([plan.share, (plan.g & plan.bits[-1]) // plan.bits[-1], plan.g & 1, plan.t])
    got_u = tie(
        got_u, w_x, all_z[0][0], all_o[0][0], share_bc, w_dt, conv_w, conv_b, gain, bias, rate, skip_lanes, where, swapped_cot
    )
    got_cot = plan.to_sequence(tie(swapped_cot, got_u))
    u_part_low = plan.pieces_of_sequence(got_u)
    u_part = u_part_low.astype(f32)
    scale_part = lax.rsqrt(jnp.mean(u_part * u_part, axis=-1, keepdims=True) + EPS)
    normed = lax.optimization_barrier(plan.gather_shares((u_part * scale_part * norm_gain).astype(bf16)))

    bc_pre = dot_nn(normed, weight_bc)
    common = (
        dot_nn(normed, w_x), bc_pre, dot_nt(normed, w_dt) + bias, rate, aux, seg_column, seg_row,
        conv_w, conv_b, conv_weight_bc, conv_bias_bc[None], skip_lanes,
    )
    y, entering, steps, cum_t = forward_scan(common)

    z_stacks, o_stacks = tie((all_z[0], all_o[0]), y)
    moves = [
        (n, (i, j), slice(0, size), 0, size, off, slice(j * width, (j + 1) * width))
        for n in two for i, off in enumerate(all_z[1][n]) for j in two
    ]
    w_z = assemble(moves, plan.g, z_stacks, (model, 2 * width))
    tall = width // groups
    moves = [
        (n, (i, j), slice(m * tall, (m + 1) * tall), j * width, tall, off, slice(m * width, (m + 1) * width))
        for n in two for i, off in enumerate(all_o[1][n]) for j in two for m in range(model // width)
    ]
    w_out = assemble(moves, plan.g, o_stacks, (2 * width, model))
    cot_part = plan.pieces_of_sequence(tie(got_cot, y))
    cot_parts = [cot_part] + [plan.across(cot_part, e) for e in range(1, shares)]
    stats, c_sent, c_kept = gate_step(shares, where, normed, w_z, y, w_out, gain, cot_parts)
    mixed, d_y, d_gate, grad_gain, sent_y, out_part = norm_step(
        shares, inner, where, normed, w_z, y, w_out, gain, plan.sum_shares(stats), cot_parts
    )
    rows_per = length // shares
    for e in range(1, shares):
        out_part = out_part + plan.across(sent_y[(shares - 1 - e) * rows_per : (shares - e) * rows_per], e).astype(f32)
    out_low = (u_part_low.astype(f32) + out_part).astype(bf16)
    out_blocks = plan.blocks_back(out_low)
    got_out = plan.from_sequence(out_blocks)
    grad_gain = grad_gain[0]

    x_sent, x_kept = cut_step(groups, where, normed)
    sent_z = dot_nn(x_sent, d_gate).astype(bf16)
    sent_o = dot_nn(c_sent, mixed).astype(bf16)
    early_z = plan.first_send(sent_z, True)
    early_o = plan.first_send(sent_o, False)

    def slots_of(value):
        return [value[:, j * width : (j + 1) * width] for j in two]

    back = [backward_scan(common, 0, shares, where, steps, cum_t, y, tie(d_y, sent_z, sent_o, out_blocks), entering)]
    early_z, early_o = tie((early_z, early_o), back[0][1])
    next_z, held_z, late_z = plan.next_sums(dot_nn(x_kept, d_gate) + early_z.astype(f32), True)
    next_o, held_o, late_o = plan.next_sums(dot_nn(c_kept, mixed) + early_o.astype(f32), False)
    first = tie(back[0][1], next_z, next_o, got_out)
    sent_x = dot_nn(x_sent, first).astype(bf16)
    early_x = plan.first_send(sent_x, True)
    kept_x = dot_nn(x_kept, first)
    base = base_step(d_gate, w_z, first, w_x)
    late_z, late_o = tie((late_z, late_o), sent_x, kept_x, base)
    late_z = held_z + late_z.astype(f32)
    late_o = held_o + late_o.astype(f32)
    zo_blocks = plan.slot_blocks([jnp.stack(v) for v in zip(slots_of(late_z), slots_of(late_o))])
    back.append(backward_scan(common, 1, shares, where, steps, cum_t, y, tie(d_y, zo_blocks), entering, back[0][0]))
    zo_sums = plan.slot_sends(zo_blocks, two)
    u_parts = [u_part_low] + [plan.across(tie(u_part_low, y), e) for e in range(1, shares)]
    back[1] = tie(back[1], zo_sums, early_x)

    next_x, held_x, late_x = plan.next_sums(kept_x + tie(early_x, back[1][1]).astype(f32), True)
    d_bcs = [back[1][0][0]] + [plan.across(back[1][0][e], e) for e in range(1, shares)]
    sent_d, d_part, low_bc, grad_norm = last_step(
        shares, where, d_bcs, u_parts, back[1][1], (back[0][2], back[1][2]), tie(base, next_x, held_x), w_x, share_bc, w_dt
    )
    x0_blocks = plan.slot_blocks([held_x + tie(late_x, sent_d).astype(f32)])
    x0_sums = plan.slot_sends(x0_blocks, (0,))
    grad_norm = grad_norm[0]
    d_parts = [d_part] + [
        plan.across(sent_d[(shares - 1 - e) * rows_per : (shares - e) * rows_per], e) for e in range(1, shares)
    ]
    back_blocks = input_step(tensor, d_parts, tie(u_part_low, x0_blocks), norm_gain[None])
    got_back = plan.from_sequence(back_blocks)
    output = plan.pieces_of_batch(tie(got_out, back_blocks))

    rows = []
    for j in two:
        g_conv, g_heads = back[j][3], back[j][5]
        head_row = jnp.zeros((1, width), f32)
        g_skip = jnp.sum(g_conv[5].reshape(-1, HEAD), axis=1)
        head_row = lax.dynamic_update_slice(head_row, jnp.concatenate([g_heads[0], g_heads[1], g_skip])[None], (0, 0))
        rows.append(jnp.concatenate([g_conv[0:5], grad_gain[None, j * width : (j + 1) * width], head_row], axis=0))
    order = [rows[0], rows[1]]
    flip = (plan.seq & 1) != 0
    order = [jnp.where(flip, rows[1 - j], rows[j]) for j in two]
    shared = jnp.concatenate([grad_norm, (back[0][4] + back[1][4])[0:5].reshape(-1)])
    shared = jnp.pad(shared, (0, -shared.shape[0] % width)).reshape(-1, width)
    small = jnp.concatenate(order + [shared], axis=0)
    count = rows[0].shape[0]

    rest = jnp.concatenate([low_bc, back[0][2].astype(bf16), back[1][2].astype(bf16)], axis=1)
    size_r = model // groups
    sent_r, kept_r = (
        one_by_one(lax.dot_general(u, v, (((0,), (1,)), ((), ())), preferred_element_type=f32), size_r)
        for u, v in ((rest, x_sent), (tie(rest, back_blocks), x_kept))
    )
    pack = None
    for n, bit in enumerate(plan.bits):
        beside = side_by_side(sent_r.astype(bf16), width)
        message = jnp.concatenate([beside] + thirds(small), axis=0)
        pack = message if pack is None else pack
        got = plan.around(message, bit)
        if n == 0:
            got = tie(got, back_blocks)
        tall, lines = beside.shape[0], small.shape[0]
        kept_r = kept_r + one_by_one(got[:tall], size_r).astype(f32)
        small = small + sum(got[tall + i * lines : tall + (i + 1) * lines].astype(f32) for i in (2, 1, 0))
        if n + 1 < len(plan.bits):
            parts = groups >> (n + 1)
            held = kept_r.reshape(parts // 2, 2, kept_r.shape[0] // parts, size_r)
            mine = ((plan.g & plan.bits[n + 1]) != 0).astype(jnp.int32)
            sent_r, kept_r = (
                lax.dynamic_index_in_dim(held, v, 1, keepdims=False).reshape(-1, size_r) for v in (1 - mine, mine)
            )
    rest = kept_r

    final = tie(back[1][1], pack)
    early_r = plan.first_send(dot_nn(x_sent, final).astype(bf16), True)
    kept_x1 = lax.optimization_barrier(dot_nn(x_kept, tie(final, back_blocks)))
    next_r, held_r, late_r = plan.next_sums(kept_x1 + tie(early_r, back_blocks).astype(f32), True)
    late_r = held_r + late_r.astype(f32)
    grad_z, grad_out = plan.slot_total(zo_sums)
    grad_out = grad_out.T
    input_grad = cotangent.astype(f32) + plan.pieces_of_batch(got_back).astype(f32)

    beyond = wide // shares
    parts = [rest[:beyond]] + [
        jnp.where(flip, rest[beyond + (1 - j) * heads : beyond + (2 - j) * heads], rest[beyond + j * heads : beyond + (j + 1) * heads])
        for j in two
    ]
    rest = jnp.concatenate(parts, axis=0).astype(bf16)
    half = size_r // 2
    columns = rest.shape[0]
    rests, smalls = [], []
    for e in range(shares):
        rows_e = lax.dynamic_slice_in_dim(rest, ((plan.share ^ e) // plan.k) * half, half, 1)
        rests.append(plan.across(rows_e, e) if e else rows_e)
        smalls.append(plan.across(small, e) if e else small)
    rests = side_by_side(jnp.concatenate(order_by_xor(rests, plan.share), axis=0), width)
    smalls = order_by_xor(smalls, plan.share)
    shared = sum(v[2 * count :] for v in smalls)
    smalls = jnp.stack([
        jnp.concatenate([smalls[i // 2][(i % 2) * count : (i % 2 + 1) * count], shared], axis=0) for i in range(tensor)
    ])
    cells = rests.shape[0]
    rests = jnp.broadcast_to(rests[None], (tensor, cells, width))
    last = jnp.concatenate([rests] + thirds(smalls), axis=1)
    last = tie(last, next_r)
    x1_sums = plan.slot_sends(plan.slot_blocks([tie(late_r, last)]), (1,))
    last = lax.all_to_all(tie(last, got_back), "t", 0, 0, tiled=True).reshape(tensor, -1, width)
    grad_x = plan.slot_total(tie(x0_sums + x1_sums, last))
    rests = one_by_one(jnp.sum(last[:, :cells].astype(f32), axis=0), half)
    rests = [rests[i * columns : (i + 1) * columns] for i in range(shares)]
    grad_bc = jnp.concatenate([v[:beyond] for v in rests], axis=0).T
    dts = [v[beyond + j * heads : beyond + (j + 1) * heads] for v in rests for j in two]
    grad_dt = lax.dynamic_index_in_dim(jnp.stack(dts), plan.t, 0, keepdims=False).T
    g_conv, g_conv_bias, g_gain, g_step, g_decay, g_skip, g_norm, g_conv_bc, g_conv_bc_bias = finish_step(
        where, last, cells, model, wide, heads
    )
    return (
        output, input_grad, g_norm, grad_z, grad_x, grad_bc, grad_dt, g_conv, g_conv_bias, g_conv_bc, g_conv_bc_bias,
        g_step, g_decay, g_skip, g_gain, grad_out,
    )


def solution(mesh):
    data, tensor = mesh.shape["dp"], mesh.shape["tensor"]
    groups = data // 2
    fine = Mesh(mesh.devices.reshape(groups, 2, tensor), AXES)
    dp = ("g", "c")

    def step(*args):
        return per_device(groups, tensor, *args)

    return jax.shard_map(
        step,
        mesh=fine,
        in_specs=(
            P(dp, None, "t"), P(dp, None), P(dp, None, "t"), P(), P(None, "t"), P(None, "t"), P(), P(None, "t"),
            P(None, "t"), P("t"), P(), P(), P("t"), P("t"), P("t"), P("t"), P("t", None),
        ),
        out_specs=(
            P(dp, None, "t"), P(dp, None, "t"), P("t"), P(dp, "t"), P(dp, "t"), P(dp, None), P(dp, "t"),
            P(None, "t"), P("t"), P(), P(), P("t"), P("t"), P("t"), P("t"), P("t", dp),
        ),
        check_vma=False,
    )
```

time: 1270 us -> 330 us (0.26)
  waiting for transfers between devices: 422 us -> 51.6 us
  matrix products: 258 us -> 26.5 us
  blocking collectives: 193 us -> 0 us
  local copies, waits for them, and re-layouts: 174 us -> 35.6 us
  other arithmetic: 169 us -> 43.5 us
  Pallas kernels: 0 us -> 90.1 us
  starting transfers between devices: 1 us -> 74.2 us
  loops' own time: 24.3 us -> 0 us
  between operations: 15.9 us -> 2.42 us
    reduce_scatter x9 -> x0, waiting for transfers between devices: 332 us -> none  [the longest x2 114 us: per_device(): lax.psum_scatter(partial_value, 'tensor', scatter_dimension=2, tiled=True)]
    dot_general x126 -> x13, matrix products: 241 us -> 26.5 us  [the longest x10 24 us: dot_nn(): lax.dot_general(a, b, (((1,), (0,)), ((), ())), preferred_element_type=f32)]
    psum x5 -> x0, blocking collectives: 193 us -> none  [the longest x1 131 us: per_device(): lax.psum((d_bc, d_params[2], d_params[3]), 'tensor')]
    pallas_call x0 -> x13, Pallas kernels: none -> 90.1 us  [the longest x2 36.9 us: backward_scan(): pl.pallas_call(functools.partial(backward_kernel, half * heads, bool(befo...]
    all_gather x4 -> x0, waiting for transfers between devices: 88.6 us -> none  [the longest x2 88.5 us: per_device(): lax.all_gather(local_in, 'tensor', axis=2, tiled=True)]
    ppermute x0 -> x43, starting transfers between devices: none -> 44.2 us  [send(): return lax.ppermute(value, AXES, pairs)]
    reduce_sum x34 -> x4, other arithmetic: 41.3 us -> 0.56 us  [the longest x1 0.28 us: per_device(): jnp.mean(u_part * u_part, axis=-1, keepdims=True) + EPS]
    another operation x65 -> x7, other arithmetic: 37.9 us -> 3.16 us  [the longest x2 1.88 us: per_device(): jnp.stack([plan.slice_of(weight_z), jnp.concatenate([mine_o[:, i:i + widt...]
  transfers between devices with their start and end apart: 13 -> 48, of which waited for: 10 -> 14; matrix products, arithmetic and copies ran while one was open for 20% -> 27% of each run, Pallas kernels for 0% -> 22%
where the time goes in v1:
time: 330 us; the launch traced here: 324 us
  Pallas kernels  90.1 us (27%)
  starting transfers between devices  74.2 us (22%)
  waiting for transfers between devices  51.6 us (16%)
  other arithmetic  43.5 us (13%)
  local copies, waits for them, and re-layouts  35.6 us (11%)
  matrix products  26.5 us (8%)
    ppermute x43, starting transfers between devices, send(): return lax.ppermute(value, AXES, pairs)  44.2 us
    pallas_call x2, Pallas kernels, backward_scan(): pl.pallas_call(functools.partial(backward_kernel, half * heads, bool(befo...  36.9 us
    ppermute x43, waiting for transfers between devices, send(): return lax.ppermute(value, AXES, pairs)  27.8 us
    dot_general x10, matrix products, dot_nn(): lax.dot_general(a, b, (((1,), (0,)), ((), ())), preferred_element_type=f32)  24 us
    all_to_all x2, starting transfers between devices, to_sequence(): lax.all_to_all(source.reshape(self.tensor, rows // self.k, width), 't', 0...  17 us
    pallas_call x1, Pallas kernels, forward_scan(): pl.pallas_call(forward_kernel, grid=(blocks,), in_specs=ins, out_specs=[r...  13.8 us
    unnamed x113, local copies, waits for them, and re-layouts  13.5 us
    pallas_call x1, Pallas kernels, norm_step(): pl.pallas_call(functools.partial(norm_kernel, shares, inner), grid_spec=p...  10.6 us
  transfers between devices with their start and end apart: 48, of which 14 were waited for; matrix products, arithmetic and copies ran while one was open for 27% of the time, Pallas kernels for 22%

profile of v1, /device:TPU:0, one launch (start us, length us, event | category | flops | bytes accessed | tf_op | source)
XLA Modules:
  0.0 324.0 jit_solution(4053435729845722134)
XLA Ops:
  4.2 3.1 collective-permute-start.4
  7.3 3.4 %collective-permute-start.1 = (s32[2,1024]{1,0:T(2,128)}, s32[2,1024]{1,0:T(2,128)S(1)}, u32[]{:S(2)}, u32[]{:S(2)}) collective-permute-start(s32[2,1024]{1,0:T(2,128)} %param.18), channel_id=1, source_target_pairs={{0,4},{1,5},{2,6},{3,7},{4,0},{5,1},{6,2},{7,3},{8,12},{9,13},{10,... | collective-permute-start | bytes 24584 | tf_op jit(solution)/shard_map/ppermute | solution.py:793
  19.4 5.4 %collective-permute-start.6 = (bf16[2,256,512]{2,1,0:T(8,128)(2,1)}, bf16[2,256,512]{2,1,0:T(8,128)(2,1)}, u32[]{:S(2)}, u32[]{:S(2)}) collective-permute-start(bf16[2,256,512]{2,1,0:T(8,128)(2,1)} %pad_maximum_fusion.12), channel_id=1, source_target_pairs={{0,0},{1,1},{2,4},{3,5},{4,2},{5,3},{6,6},{7,7},{8,8},{9,9},{10,12... | collective-permute-start | bytes 1572872 | tf_op jit(solution)/shard_map/ppermute | solution.py:793
  33.6 4.6 %collective-permute-done.5 = bf16[1,256,512]{2,1,0:T(8,128)(2,1)S(1)} collective-permute-done((bf16[1,256,512]{2,1,0:T(8,128)(2,1)S(1)}, bf16[1,256,512]{2,1,0:T(8,128)(2,1)S(1)}, u32[]{:S(2)}, u32[]{:S(2)}) %collective-permute-start.5) | collective-permute-done | bytes 262176 | tf_op jit(solution)/shard_map/ppermute | solution.py:793
  38.2 2.5 bitcast_select_fusion.1
  41.7 12.0 %all-to-all-start = ((bf16[4,512,256]{2,1,0:T(8,128)(2,1)}), bf16[4,512,256]{2,1,0:T(8,128)(2,1)S(1)}, u32[]{:S(2)}, u32[]{:S(2)}) async-start(bf16[4,512,256]{2,1,0:T(8,128)(2,1)} %pad_maximum_fusion.2), calls=%async_computation | async-start | bytes 2097152 | tf_op jit(solution)/shard_map/all_to_all | solution.py:823
  63.1 2.3 pad_maximum_fusion.5
  65.4 3.6 %collective-permute-done.8.refs_1_ = bf16[2,256,512]{2,1,0:T(8,128)(2,1)S(1)} collective-permute-done((bf16[2,256,512]{2,1,0:T(8,128)(2,1)S(1)}, bf16[2,256,512]{2,1,0:T(8,128)(2,1)S(1)}, u32[]{:S(2)}, u32[]{:S(2)}) %collective-permute-start.8) | collective-permute-done | bytes 524320 | tf_op jit(solution)/shard_map/ppermute | solution.py:793
  72.1 8.0 %collective-permute-done.11 = bf16[1,2,256,512]{3,2,1,0:T(8,128)(2,1)} collective-permute-done((bf16[1,2,256,512]{3,2,1,0:T(8,128)(2,1)}, bf16[1,2,256,512]{3,2,1,0:T(8,128)(2,1)}, u32[]{:S(2)}, u32[]{:S(2)}) %collective-permute-start.11) | collective-permute-done | bytes 524320 | tf_op jit(solution)/shard_map/ppermute | solution.py:793
  80.1 2.3 pad_maximum_fusion.4.refs_0_
  82.4 2.3 pad_maximum_fusion.3.refs_0_
  89.9 5.0 %all-to-all-start.1 = ((bf16[4,512,256]{2,1,0:T(8,128)(2,1)}), bf16[4,512,256]{2,1,0:T(8,128)(2,1)}, u32[]{:S(2)}, u32[]{:S(2)}) async-start(bf16[4,512,256]{2,1,0:T(8,128)(2,1)} %pad_maximum_fusion.5), calls=%async_computation.1 | async-start | bytes 2097152 | tf_op jit(solution)/shard_map/all_to_all | solution.py:823
  98.9 4.4 %fusion.64.v_ref.vh_ref = f32[1024,1024]{1,0:T(8,128)} fusion(bf16[1024,1024]{1,0:T(8,128)(2,1)S(1)} %pad_maximum_fusion.normed_ref.source_ref, bf16[1024,1024]{1,0:T(8,128)(2,1)S(1)} %copy-done.6), kind=kOutput, calls=%fused_computation.262 | convolution fusion | flops 2147483648 | bytes 8388608 | tf_op jit(solution)/shard_map/dot_general | solution.py:22
  103.3 13.8 %shard_map.289 = (f32[1024,1024]{1,0:T(8,128)}, bf16[4,128,1024]{2,1,0:T(8,128)(2,1)}, f32[1024,48]{1,0:T(8,128)}, f32[16,1024]{1,0:T(8,128)}) custom-call(f32[1024,1024]{1,0:T(8,128)} %fusion.64.v_ref.vh_ref, f32[1024,1024]{1,0:T(8,128)} %fusion.64.v_ref.vh_ref, f32[1024,256]{1,0:T(8,128)} %fusion.65.bc_ref.bch_ref, f32[1024,256]{1,0:T(8,128)} %fusion.65.bc_ref.bch_ref, ...), custom_call_target="tpu_custom_call" | custom-call | flops 1048576 | bytes 1048576 | tf_op jit(solution)/shard_map/pallas_call | solution.py:313
  117.1 3.7 %all-to-all-done.1 = bf16[4,512,256]{2,1,0:T(8,128)(2,1)} async-done(((bf16[4,512,256]{2,1,0:T(8,128)(2,1)}), bf16[4,512,256]{2,1,0:T(8,128)(2,1)}, u32[]{:S(2)}, u32[]{:S(2)}) %all-to-all-start.1) | async-done | bytes 1048608 | tf_op jit(solution)/shard_map/all_to_all | solution.py:823
  126.9 7.4 %shard_map.292 = (f32[8,1024]{1,0:T(8,128)S(1)}, bf16[512,1024]{1,0:T(8,128)(2,1)S(1)}, bf16[512,1024]{1,0:T(8,128)(2,1)S(1)}) custom-call(s32[4]{0:T(128)S(1)} %pad_add_fusion.3.where_ref, bf16[1024,1024]{1,0:T(8,128)(2,1)S(1)} %pad_maximum_fusion.normed_ref.source_ref, bf16[1024,1024]{1,0:T(8,128)(2,1)S(1)} %shard_map.290.wz_ref, ...), custom_call_target="tpu_custom_call" | custom-call | flops 4294967296 | bytes 8388608 | tf_op jit(solution)/shard_map/pallas_call | solution.py:486
  135.8 10.6 %shard_map.293 = (bf16[1024,1024]{1,0:T(8,128)(2,1)S(1)}, bf16[1024,1024]{1,0:T(8,128)(2,1)S(1)}, bf16[1024,1024]{1,0:T(8,128)(2,1)S(1)}, f32[8,1024]{1,0:T(8,12...) custom-call(s32[4]{0:T(128)S(1)} %pad_add_fusion.3.where_ref, ...), custom_call_target="tpu_custom_call" | custom-call | flops 6442450944 | bytes 18874368 | tf_op jit(solution)/shard_map/pallas_call | solution.py:509
  149.3 2.3 convolution_convert_fusion
  156.6 4.2 %all-to-all-start.2 = ((bf16[4,512,256]{2,1,0:T(8,128)(2,1)}), bf16[4,512,256]{2,1,0:T(8,128)(2,1)}, u32[]{:S(2)}, u32[]{:S(2)}) async-start(bf16[4,512,256]{2,1,0:T(8,128)(2,1)} %pad_maximum_fusion.8), calls=%async_computation.2 | async-start | bytes 2097152 | tf_op jit(solution)/shard_map/all_to_all | solution.py:833
  160.9 18.5 %shard_map.295 = (f32[1024,128]{1,0:T(8,128)}, f32[1024,128]{1,0:T(8,128)}, bf16[1024,512]{1,0:T(8,128)(2,1)}, f32[1024,8]{1,0:T(8,128)}, f32[8,512]{1,0:T(8,128)}, /*index=5*/f32[8,256]{1,0:T(8,128)}, f32[8,8]{1,0:T(8,128)}) custom-call(s32[4]{0:T(128)} %copy-done.20, f32[1024,1024]{1,0:T(8,128)} %fusion.64.v_ref.vh_ref, f32[1024,1024]{1,0:T(8,128)} %fusion.64.v_ref.vh_ref, ...), custom_call_target="tpu_custom_call" | custom-call | flops 524288 | bytes 524288 | tf_op jit(solution)/shard_map/pallas_call | solution.py:340
  179.8 2.6 convert_add_fusion.2
  184.6 2.6 convert_add_fusion.3
  195.7 4.1 %shard_map.296.refs_7_ = f32[1024,1024]{1,0:T(8,128)S(1)} custom-call(bf16[1024,1024]{1,0:T(8,128)(2,1)S(1)} %copy-done.25, bf16[1024,1024]{1,0:T(8,128)(2,1)S(1)} %copy-done.11, bf16[1024,512]{1,0:T(8,128)(2,1)S(1)} %copy-done.22, bf16[1024,1024]{1,0:T(8,128)(2,1)S(1)} %copy-done.7), custom_call_target="tpu_custom_call" | custom-call | flops 3221225472 | bytes 8388608 | tf_op jit(solution)/shard_map/pallas_call | solution.py:572
  214.1 18.5 %shard_map.297 = (f32[1024,128]{1,0:T(8,128)}, f32[1024,128]{1,0:T(8,128)}, bf16[1024,512]{1,0:T(8,128)(2,1)}, f32[1024,8]{1,0:T(8,128)}, f32[8,512]{1,0:T(8,128)}, /*index=5*/f32[8,256]{1,0:T(8,128)}, f32[8,8]{1,0:T(8,128)}) custom-call(s32[4]{0:T(128)} %copy-done.20, f32[1024,1024]{1,0:T(8,128)} %fusion.64.v_ref.vh_ref, f32[1024,1024]{1,0:T(8,128)} %fusion.64.v_ref.vh_ref, ...), custom_call_target="tpu_custom_call" | custom-call | flops 524288 | bytes 524288 | tf_op jit(solution)/shard_map/pallas_call | solution.py:340
  241.1 9.3 %shard_map.298 = (bf16[512,1024]{1,0:T(8,128)(2,1)}, f32[512,1024]{1,0:T(8,128)}, bf16[1024,128]{1,0:T(8,128)(2,1)}, f32[8,1024]{1,0:T(8,128)}) custom-call(s32[4]{0:T(128)} %copy-done.20, f32[1024,128]{1,0:T(8,128)} %get-tuple-element.139.refs_0_, f32[1024,128]{1,0:T(8,128)} %collective-permute-done.27.refs_1_, bf16[512,1024]{1,0:T(8,128)(2,1)} %copy-done.2, ...), custom_call_target="tpu_custom_call" | custom-call | flops 1073741824 | bytes 8388608 | tf_op jit(solution)/shard_map/pallas_call | solution.py:630
  254.6 3.0 convolution_convert_fusion.2
  266.4 3.6 %all-to-all-start.3 = ((bf16[4,512,256]{2,1,0:T(8,128)(2,1)}), bf16[4,512,256]{2,1,0:T(8,128)(2,1)S(1)}, u32[]{:S(2)}, u32[]{:S(2)}) async-start(bf16[4,512,256]{2,1,0:T(8,128)(2,1)} %shard_map.299), calls=%async_computation.3 | async-start | bytes 2097152 | tf_op jit(solution)/shard_map/all_to_all | solution.py:833
  270.0 2.7 collective-permute-done.37
  279.6 3.1 collective-permute-done.34
  286.3 9.8 %all-to-all-done.3 = bf16[4,512,256]{2,1,0:T(8,128)(2,1)S(1)} async-done(((bf16[4,512,256]{2,1,0:T(8,128)(2,1)}), bf16[4,512,256]{2,1,0:T(8,128)(2,1)S(1)}, u32[]{:S(2)}, u32[]{:S(2)}) %all-to-all-start.3) | async-done | bytes 1048608 | tf_op jit(solution)/shard_map/all_to_all | solution.py:833
  299.9 5.2 %all-to-all-start.4 = ((bf16[4,108,512]{2,1,0:T(8,128)(2,1)}), bf16[4,108,512]{2,1,0:T(8,128)(2,1)S(1)}, u32[]{:S(2)}, u32[]{:S(2)}) async-start(bf16[4,108,512]{2,1,0:T(8,128)(2,1)} %pad_maximum_fusion.14), calls=%async_computation.4 | async-start | bytes 917504 | tf_op jit(solution)/shard_map/all_to_all | solution.py:1163
  308.9 10.2 %all-to-all-done.4.last_ref = bf16[4,108,512]{2,1,0:T(8,128)(2,1)S(1)} async-done(((bf16[4,108,512]{2,1,0:T(8,128)(2,1)}), bf16[4,108,512]{2,1,0:T(8,128)(2,1)S(1)}, u32[]{:S(2)}, u32[]{:S(2)}) %all-to-all-start.4) | async-done | bytes 442400 | tf_op jit(solution)/shard_map/all_to_all | solution.py:1163
  (360 shorter events, 127.6 us)
Async XLA Ops:
  3.5 15.9 %collective-permute-start.2 = (bf16[304,512]{1,0:T(8,128)(2,1)S(1)}, bf16[304,512]{1,0:T(8,128)(2,1)S(1)}, u32[]{:S(2)}, u32[]{:S(2)}) collective-permute-start(bf16[304,512]{1,0:T(8,128)(2,1)S(1)} %pad_maximum_fusion.15), channel_id=1, source_target_pairs={{0,0},{1,1},{2,4},{3,5},{4,2},{5,3},{6,6},{7,7},{8,8},{9,9},{10,12... | collective-permute-start | bytes 933896 | tf_op jit(solution)/shard_map/ppermute | solution.py:793
  4.2 15.3 %collective-permute-start.4 = (bf16[304,512]{1,0:T(8,128)(2,1)S(1)}, bf16[304,512]{1,0:T(8,128)(2,1)S(1)}, u32[]{:S(2)}, u32[]{:S(2)}) collective-permute-start(bf16[304,512]{1,0:T(8,128)(2,1)S(1)} %pad_maximum_fusion.15), channel_id=1, source_target_pairs={{0,1},{1,0},{2,5},{3,4},{4,3},{5,2},{6,7},{7,6},{8,9},{9,8},{10,13... | collective-permute-start | bytes 933896 | tf_op jit(solution)/shard_map/ppermute | solution.py:793
  12.0 26.2 %collective-permute-start = (bf16[2,2,512,256]{3,2,1,0:T(8,128)(2,1)S(1)}, bf16[2,2,512,256]{3,2,1,0:T(8,128)(2,1)}, u32[]{:S(2)}, u32[]{:S(2)}) collective-permute-start(bf16[2,2,512,256]{3,2,1,0:T(8,128)(2,1)S(1)} %pad_maximum_fusion.1), channel_id=1, source_target_pairs={{0,4},{1,5},{2,6},{3,7},{4,0},{5,1},{6,2},{7,3},{8,12},{9,13},{10,... | collective-permute-start | bytes 3145736 | tf_op jit(solution)/shard_map/ppermute | solution.py:793
  19.4 22.3 %collective-permute-start.6 = (bf16[2,256,512]{2,1,0:T(8,128)(2,1)}, bf16[2,256,512]{2,1,0:T(8,128)(2,1)}, u32[]{:S(2)}, u32[]{:S(2)}) collective-permute-start(bf16[2,256,512]{2,1,0:T(8,128)(2,1)} %pad_maximum_fusion.12), channel_id=1, source_target_pairs={{0,0},{1,1},{2,4},{3,5},{4,2},{5,3},{6,6},{7,7},{8,8},{9,9},{10,12... | collective-permute-start | bytes 1572872 | tf_op jit(solution)/shard_map/ppermute | solution.py:793
  24.8 16.9 %collective-permute-start.7 = (bf16[2,256,512]{2,1,0:T(8,128)(2,1)}, bf16[2,256,512]{2,1,0:T(8,128)(2,1)}, u32[]{:S(2)}, u32[]{:S(2)}) collective-permute-start(bf16[2,256,512]{2,1,0:T(8,128)(2,1)} %pad_maximum_fusion.12), channel_id=1, source_target_pairs={{0,1},{1,0},{2,5},{3,4},{4,3},{5,2},{6,7},{7,6},{8,9},{9,8},{10,13... | collective-permute-start | bytes 1572872 | tf_op jit(solution)/shard_map/ppermute | solution.py:793
  41.7 42.9 %all-to-all-start = ((bf16[4,512,256]{2,1,0:T(8,128)(2,1)}), bf16[4,512,256]{2,1,0:T(8,128)(2,1)S(1)}, u32[]{:S(2)}, u32[]{:S(2)}) async-start(bf16[4,512,256]{2,1,0:T(8,128)(2,1)} %pad_maximum_fusion.2), calls=%async_computation | async-start | bytes 2097152 | tf_op jit(solution)/shard_map/all_to_all | solution.py:823
  55.9 14.8 %collective-permute-start.9 = (bf16[2,256,512]{2,1,0:T(8,128)(2,1)S(1)}, bf16[2,256,512]{2,1,0:T(8,128)(2,1)S(1)}, u32[]{:S(2)}, u32[]{:S(2)}) collective-permute-start(bf16[2,256,512]{2,1,0:T(8,128)(2,1)S(1)} %pad_maximum_fusion.11.refs_2_), channel_id=1, source_target_pairs={{0,8},{1,9},{2,10},{3,11},{4,12},{5,13},{6,14},{7,15},{8,0},{9,1},... | collective-permute-start | bytes 1572872 | tf_op jit(solution)/shard_map/ppermute | solution.py:793
  60.4 19.7 %collective-permute-start.11 = (bf16[1,2,256,512]{3,2,1,0:T(8,128)(2,1)}, bf16[1,2,256,512]{3,2,1,0:T(8,128)(2,1)}, u32[]{:S(2)}, u32[]{:S(2)}) collective-permute-start(bf16[1,2,256,512]{3,2,1,0:T(8,128)(2,1)} %maximum_bitcast_fusion.1), channel_id=1, source_target_pairs={{0,16},{1,17},{2,18},{3,19},{4,20},{5,21},{6,22},{7,23},{8,24},{9,... | collective-permute-start | bytes 1572872 | tf_op jit(solution)/shard_map/ppermute | solution.py:793
  61.8 20.6 %collective-permute-start.10 = (bf16[1,2,256,512]{3,2,1,0:T(8,128)(2,1)}, bf16[1,2,256,512]{3,2,1,0:T(8,128)(2,1)}, u32[]{:S(2)}, u32[]{:S(2)}) collective-permute-start(bf16[1,2,256,512]{3,2,1,0:T(8,128)(2,1)} %maximum_bitcast_fusion), channel_id=1, source_target_pairs={{0,8},{1,9},{2,10},{3,11},{4,12},{5,13},{6,14},{7,15},{8,0},{9,1},... | collective-permute-start | bytes 1572872 | tf_op jit(solution)/shard_map/ppermute | solution.py:793
  86.9 35.4 %collective-permute-start.14 = (bf16[2,2,256,512]{3,2,1,0:T(8,128)(2,1)}, bf16[2,2,256,512]{3,2,1,0:T(8,128)(2,1)}, u32[]{:S(2)}, u32[]{:S(2)}) collective-permute-start(bf16[2,2,256,512]{3,2,1,0:T(8,128)(2,1)} %pad_maximum_fusion.4.refs_0_), channel_id=1, source_target_pairs={{0,8},{1,9},{2,10},{3,11},{4,12},{5,13},{6,14},{7,15},{8,0},{9,1},... | collective-permute-start | bytes 3145736 | tf_op jit(solution)/shard_map/ppermute | solution.py:793
  88.4 33.9 %collective-permute-start.13 = (bf16[2,2,256,512]{3,2,1,0:T(8,128)(2,1)}, bf16[2,2,256,512]{3,2,1,0:T(8,128)(2,1)}, u32[]{:S(2)}, u32[]{:S(2)}) collective-permute-start(bf16[2,2,256,512]{3,2,1,0:T(8,128)(2,1)} %pad_maximum_fusion.3.refs_0_), channel_id=1, source_target_pairs={{0,16},{1,17},{2,18},{3,19},{4,20},{5,21},{6,22},{7,23},{8,24},{9,... | collective-permute-start | bytes 3145736 | tf_op jit(solution)/shard_map/ppermute | solution.py:793
  89.9 30.9 %all-to-all-start.1 = ((bf16[4,512,256]{2,1,0:T(8,128)(2,1)}), bf16[4,512,256]{2,1,0:T(8,128)(2,1)}, u32[]{:S(2)}, u32[]{:S(2)}) async-start(bf16[4,512,256]{2,1,0:T(8,128)(2,1)} %pad_maximum_fusion.5), calls=%async_computation.1 | async-start | bytes 2097152 | tf_op jit(solution)/shard_map/all_to_all | solution.py:823
  151.6 27.8 %collective-permute-start.19 = (bf16[512,1024]{1,0:T(8,128)(2,1)}, bf16[512,1024]{1,0:T(8,128)(2,1)}, u32[]{:S(2)}, u32[]{:S(2)}) collective-permute-start(bf16[512,1024]{1,0:T(8,128)(2,1)} %convolution_convert_fusion), channel_id=1, source_target_pairs={{0,16},{1,17},{2,18},{3,19},{4,20},{5,21},{6,22},{7,23},{8,24},{9,... | collective-permute-start | bytes 3145736 | tf_op jit(solution)/shard_map/ppermute | solution.py:793
  154.3 25.4 %collective-permute-start.18 = (bf16[512,1024]{1,0:T(8,128)(2,1)}, bf16[512,1024]{1,0:T(8,128)(2,1)}, u32[]{:S(2)}, u32[]{:S(2)}) collective-permute-start(bf16[512,1024]{1,0:T(8,128)(2,1)} %convolution_convert_fusion.1), channel_id=1, source_target_pairs={{0,8},{1,9},{2,10},{3,11},{4,12},{5,13},{6,14},{7,15},{8,0},{9,1},... | collective-permute-start | bytes 3145736 | tf_op jit(solution)/shard_map/ppermute | solution.py:793
  156.6 34.6 %all-to-all-start.2 = ((bf16[4,512,256]{2,1,0:T(8,128)(2,1)}), bf16[4,512,256]{2,1,0:T(8,128)(2,1)}, u32[]{:S(2)}, u32[]{:S(2)}) async-start(bf16[4,512,256]{2,1,0:T(8,128)(2,1)} %pad_maximum_fusion.8), calls=%async_computation.2 | async-start | bytes 2097152 | tf_op jit(solution)/shard_map/all_to_all | solution.py:833
  183.4 20.2 %collective-permute-start.21 = (bf16[256,1024]{1,0:T(8,128)(2,1)}, bf16[256,1024]{1,0:T(8,128)(2,1)}, u32[]{:S(2)}, u32[]{:S(2)}) collective-permute-start(bf16[256,1024]{1,0:T(8,128)(2,1)} %fusion.5), channel_id=1, source_target_pairs={{0,8},{1,9},{2,10},{3,11},{4,12},{5,13},{6,14},{7,15},{8,0},{9,1},... | collective-permute-start | bytes 1572872 | tf_op jit(solution)/shard_map/ppermute | solution.py:793
  206.6 25.9 %collective-permute-start.24 = (bf16[2,128,512]{2,1,0:T(8,128)(2,1)S(1)}, bf16[2,128,512]{2,1,0:T(8,128)(2,1)S(1)}, u32[]{:S(2)}, u32[]{:S(2)}) collective-permute-start(bf16[2,128,512]{2,1,0:T(8,128)(2,1)S(1)} %get-tuple-element.281), channel_id=1, source_target_pairs={{0,1},{1,0},{2,5},{3,4},{4,3},{5,2},{6,7},{7,6},{8,9},{9,8},{10,13... | collective-permute-start | bytes 786440 | tf_op jit(solution)/shard_map/ppermute | solution.py:793
  208.6 24.0 %collective-permute-start.25 = (bf16[2,128,512]{2,1,0:T(8,128)(2,1)S(1)}, bf16[2,128,512]{2,1,0:T(8,128)(2,1)S(1)}, u32[]{:S(2)}, u32[]{:S(2)}) collective-permute-start(bf16[2,128,512]{2,1,0:T(8,128)(2,1)S(1)} %get-tuple-element.280), channel_id=1, source_target_pairs={{0,5},{1,4},{2,1},{3,0},{4,7},{5,6},{6,3},{7,2},{8,13},{9,12},{10,... | collective-permute-start | bytes 786440 | tf_op jit(solution)/shard_map/ppermute | solution.py:793
  209.9 22.8 %collective-permute-start.22 = (bf16[2,128,512]{2,1,0:T(8,128)(2,1)S(1)}, bf16[2,128,512]{2,1,0:T(8,128)(2,1)S(1)}, u32[]{:S(2)}, u32[]{:S(2)}) collective-permute-start(bf16[2,128,512]{2,1,0:T(8,128)(2,1)S(1)} %get-tuple-element.287), channel_id=1, source_target_pairs={{0,0},{1,1},{2,4},{3,5},{4,2},{5,3},{6,6},{7,7},{8,8},{9,9},{10,12... | collective-permute-start | bytes 786440 | tf_op jit(solution)/shard_map/ppermute | solution.py:793
  210.5 23.0 %collective-permute-start.23 = (bf16[2,128,512]{2,1,0:T(8,128)(2,1)S(1)}, bf16[2,128,512]{2,1,0:T(8,128)(2,1)S(1)}, u32[]{:S(2)}, u32[]{:S(2)}) collective-permute-start(bf16[2,128,512]{2,1,0:T(8,128)(2,1)S(1)} %get-tuple-element.286), channel_id=1, source_target_pairs={{0,4},{1,5},{2,0},{3,1},{4,6},{5,7},{6,2},{7,3},{8,12},{9,13},{10,... | collective-permute-start | bytes 786440 | tf_op jit(solution)/shard_map/ppermute | solution.py:793
  213.3 21.9 %collective-permute-start.26 = (bf16[512,512]{1,0:T(8,128)(2,1)}, bf16[512,512]{1,0:T(8,128)(2,1)}, u32[]{:S(2)}, u32[]{:S(2)}) collective-permute-start(bf16[512,512]{1,0:T(8,128)(2,1)} %convolution_convert_fusion.3), channel_id=1, source_target_pairs={{0,8},{1,9},{2,10},{3,11},{4,12},{5,13},{6,14},{7,15},{8,0},{9,1},... | collective-permute-start | bytes 1572872 | tf_op jit(solution)/shard_map/ppermute | solution.py:793
  237.7 21.2 %collective-permute-start.30 = (bf16[256,512]{1,0:T(8,128)(2,1)}, bf16[256,512]{1,0:T(8,128)(2,1)}, u32[]{:S(2)}, u32[]{:S(2)}) collective-permute-start(bf16[256,512]{1,0:T(8,128)(2,1)} %fusion.14), channel_id=1, source_target_pairs={{0,16},{1,17},{2,18},{3,19},{4,20},{5,21},{6,22},{7,23},{8,24},{9,... | collective-permute-start | bytes 786440 | tf_op jit(solution)/shard_map/ppermute | solution.py:793
  254.1 15.9 %collective-permute-start.33 = (bf16[201,512]{1,0:T(8,128)(2,1)}, bf16[201,512]{1,0:T(8,128)(2,1)S(1)}, u32[]{:S(2)}, u32[]{:S(2)}) collective-permute-start(bf16[201,512]{1,0:T(8,128)(2,1)} %pad_maximum_fusion.16), channel_id=1, source_target_pairs={{0,8},{1,9},{2,10},{3,11},{4,12},{5,13},{6,14},{7,15},{8,0},{9,1},... | collective-permute-start | bytes 617480 | tf_op jit(solution)/shard_map/ppermute | solution.py:793
  257.6 15.1 %collective-permute-start.37 = (bf16[512,512]{1,0:T(8,128)(2,1)}, bf16[512,512]{1,0:T(8,128)(2,1)S(1)}, u32[]{:S(2)}, u32[]{:S(2)}) collective-permute-start(bf16[512,512]{1,0:T(8,128)(2,1)} %convolution_convert_fusion.2), channel_id=1, source_target_pairs={{0,8},{1,9},{2,10},{3,11},{4,12},{5,13},{6,14},{7,15},{8,0},{9,1},... | collective-permute-start | bytes 1572872 | tf_op jit(solution)/shard_map/ppermute | solution.py:793
  260.6 59.4 %collective-permute-start.38 = (bf16[128,512]{1,0:T(8,128)(2,1)}, bf16[128,512]{1,0:T(8,128)(2,1)}, u32[]{:S(2)}, u32[]{:S(2)}) collective-permute-start(bf16[128,512]{1,0:T(8,128)(2,1)} %get-tuple-element.297), channel_id=1, source_target_pairs={{0,0},{1,1},{2,4},{3,5},{4,2},{5,3},{6,6},{7,7},{8,8},{9,9},{10,12... | collective-permute-start | bytes 393224 | tf_op jit(solution)/shard_map/ppermute | solution.py:793
  262.8 57.2 %collective-permute-start.39 = (bf16[128,512]{1,0:T(8,128)(2,1)}, bf16[128,512]{1,0:T(8,128)(2,1)}, u32[]{:S(2)}, u32[]{:S(2)}) collective-permute-start(bf16[128,512]{1,0:T(8,128)(2,1)} %get-tuple-element.296), channel_id=1, source_target_pairs={{0,4},{1,5},{2,0},{3,1},{4,6},{5,7},{6,2},{7,3},{8,12},{9,13},{10,... | collective-permute-start | bytes 393224 | tf_op jit(solution)/shard_map/ppermute | solution.py:793
  266.4 29.7 %all-to-all-start.3 = ((bf16[4,512,256]{2,1,0:T(8,128)(2,1)}), bf16[4,512,256]{2,1,0:T(8,128)(2,1)S(1)}, u32[]{:S(2)}, u32[]{:S(2)}) async-start(bf16[4,512,256]{2,1,0:T(8,128)(2,1)} %shard_map.299), calls=%async_computation.3 | async-start | bytes 2097152 | tf_op jit(solution)/shard_map/all_to_all | solution.py:833
  277.9 19.0 %collective-permute-start.40 = (bf16[256,512]{1,0:T(8,128)(2,1)S(1)}, bf16[256,512]{1,0:T(8,128)(2,1)}, u32[]{:S(2)}, u32[]{:S(2)}) collective-permute-start(bf16[256,512]{1,0:T(8,128)(2,1)S(1)} %fusion.15), channel_id=1, source_target_pairs={{0,16},{1,17},{2,18},{3,19},{4,20},{5,21},{6,22},{7,23},{8,24},{9,... | collective-permute-start | bytes 786440 | tf_op jit(solution)/shard_map/ppermute | solution.py:793
  279.6 19.1 %collective-permute-start.31 = (bf16[2,512,256]{2,1,0:T(8,128)(2,1)S(1)}, bf16[2,512,256]{2,1,0:T(8,128)(2,1)}, u32[]{:S(2)}, u32[]{:S(2)}) collective-permute-start(bf16[2,512,256]{2,1,0:T(8,128)(2,1)S(1)} %constant_dynamic-slice_fusion.3), channel_id=1, source_target_pairs={{0,4},{1,5},{2,6},{3,7},{4,0},{5,1},{6,2},{7,3},{8,12},{9,13},{10,... | collective-permute-start | bytes 1572872 | tf_op jit(solution)/shard_map/ppermute | solution.py:793
  298.7 21.3 %collective-permute-start.41 = (bf16[128,512]{1,0:T(8,128)(2,1)}, bf16[128,512]{1,0:T(8,128)(2,1)S(1)}, u32[]{:S(2)}, u32[]{:S(2)}) collective-permute-start(bf16[128,512]{1,0:T(8,128)(2,1)} %get-tuple-element.295), channel_id=1, source_target_pairs={{0,1},{1,0},{2,5},{3,4},{4,3},{5,2},{6,7},{7,6},{8,9},{9,8},{10,13... | collective-permute-start | bytes 393224 | tf_op jit(solution)/shard_map/ppermute | solution.py:793
  298.7 21.3 %collective-permute-start.42 = (bf16[128,512]{1,0:T(8,128)(2,1)S(1)}, bf16[128,512]{1,0:T(8,128)(2,1)S(1)}, u32[]{:S(2)}, u32[]{:S(2)}) collective-permute-start(bf16[128,512]{1,0:T(8,128)(2,1)S(1)} %get-tuple-element.294), channel_id=1, source_target_pairs={{0,5},{1,4},{2,1},{3,0},{4,7},{5,6},{6,3},{7,2},{8,13},{9,12},{10,... | collective-permute-start | bytes 393224 | tf_op jit(solution)/shard_map/ppermute | solution.py:793
  299.9 19.2 %all-to-all-start.4 = ((bf16[4,108,512]{2,1,0:T(8,128)(2,1)}), bf16[4,108,512]{2,1,0:T(8,128)(2,1)S(1)}, u32[]{:S(2)}, u32[]{:S(2)}) async-start(bf16[4,108,512]{2,1,0:T(8,128)(2,1)} %pad_maximum_fusion.14), calls=%async_computation.4 | async-start | bytes 917504 | tf_op jit(solution)/shard_map/all_to_all | solution.py:1163
  (71 other events, 803.4 us)

commit v2 on v1

--- a/solution.py
+++ b/solution.py
@@ -272,7 +272,7 @@
     d_decay = split_dot(d_cum, upper, flip=True)
     d_dt = split_dot(dot_x[...], select) + d_decay * rate
     d_delta = d_dt * slope_dt
-    ddelta_ref[...] = d_delta
+    ddelta_ref[...] = d_delta.astype(bf16)
     gh_ref[0:1] += rows_of(d_delta)
     gh_ref[1:2] += rows_of(d_decay * dt * rate)
 
@@ -324,7 +324,7 @@
             pltpu.VMEM((wide // 2, channels), f32), pltpu.VMEM((SPAN + 8, LANES), f32),
             pltpu.VMEM((SPAN + 8, wide), f32), pltpu.VMEM((SPAN, SPAN), f32), pltpu.VMEM((5, SPAN, LANES), f32),
         ],
-        compiler_params=pltpu.CompilerParams(vmem_limit_bytes=56 * 2**20),
+        compiler_params=pltpu.CompilerParams(vmem_limit_bytes=20 * 2**20),
         cost_estimate=pl.CostEstimate(flops=channels * length, bytes_accessed=channels * length, transcendentals=0),
     )(v_pre, v_pre, bc_pre, bc_pre, *common[2:])
 
@@ -355,7 +355,7 @@
         ),
         out_shape=[jax.ShapeDtypeStruct((length, wide // shares), f32)] * shares
         + [
-            jax.ShapeDtypeStruct((length, channels), bf16), jax.ShapeDtypeStruct((length, heads), f32),
+            jax.ShapeDtypeStruct((length, channels), bf16), jax.ShapeDtypeStruct((length, heads), bf16),
             jax.ShapeDtypeStruct((8, channels), f32), jax.ShapeDtypeStruct((8, wide), f32),
             jax.ShapeDtypeStruct((8, heads), f32),
         ],
@@ -458,7 +458,7 @@
 
     @pl.when(pl.program_id(0) >= (shares - 1) * each)
     def _():
-        kept_ref[...] = result
+        kept_ref[...] = result.astype(bf16)
 
 
 def gated_specs(shares, normed, y):
@@ -524,7 +524,7 @@
         out_shape=[jax.ShapeDtypeStruct((length, channels), bf16)] * 3
         + [
             jax.ShapeDtypeStruct((8, channels), f32), jax.ShapeDtypeStruct((many * SPAN, model), bf16),
-            jax.ShapeDtypeStruct((each * SPAN, model), f32),
+            jax.ShapeDtypeStruct((each * SPAN, model), bf16),
         ],
         compiler_params=pltpu.CompilerParams(vmem_limit_bytes=26 * 2**20),
         cost_estimate=pl.CostEstimate(flops=6 * length * model * channels, bytes_accessed=18 * length * channels, transcendentals=0),
@@ -558,7 +558,7 @@
 
 
 def base_kernel(gate_ref, wz_ref, value_ref, wx_ref, out_ref):
-    out_ref[...] = dot_nt(gate_ref[...], wz_ref[...]) + dot_nt(value_ref[...], wx_ref[...])
+    out_ref[...] = (dot_nt(gate_ref[...], wz_ref[...]) + dot_nt(value_ref[...], wx_ref[...])).astype(bf16)
 
 
 def base_step(d_gate, w_z, d_value, w_x):
@@ -577,8 +577,8 @@
             pl.BlockSpec((model, width), lambda b: (0, 0)),
         ],
         out_specs=rows(model),
-        out_shape=jax.ShapeDtypeStruct((length, model), f32),
-        compiler_params=pltpu.CompilerParams(vmem_limit_bytes=13 * 2**20),
+        out_shape=jax.ShapeDtypeStruct((length, model), bf16),
+        compiler_params=pltpu.CompilerParams(vmem_limit_bytes=56 * 2**20),
         cost_estimate=pl.CostEstimate(flops=3 * length * channels * model, bytes_accessed=8 * length * channels, transcendentals=0),
     )(d_gate, w_z, d_value, w_x)
 
@@ -597,8 +597,9 @@
         low = low + ref[...]
     low = low.astype(bf16)
     low_ref[...] = low
-    steps = jnp.concatenate([one_ref[...], two_ref[...]], axis=1).astype(bf16)
-    total = dot_nt(dv_ref[...], wx_ref[...]) + dot_nt(low, wb_ref[...]) + dot_nn(steps, wd_ref[...]) + base_ref[...]
+    steps = jnp.concatenate([one_ref[...].astype(f32), two_ref[...].astype(f32)], axis=1).astype(bf16)
+    total = dot_nt(dv_ref[...], wx_ref[...]) + dot_nt(low, wb_ref[...]) + dot_nn(steps, wd_ref[...])
+    total = total + base_ref[...].astype(f32)
     u = u_ref[...].astype(f32)
     scale = lax.rsqrt(jnp.sum(u * u, axis=1, keepdims=True) * (1.0 / u.shape[1]) + 1e-05)
     gain_ref[0:1] += jnp.sum(total * (u * scale), axis=0, keepdims=True)
@@ -610,7 +611,7 @@
 
     @pl.when(pl.program_id(0) >= (shares - 1) * each)
     def _():
-        kept_ref[...] = total
+        kept_ref[...] = total.astype(bf16)
 
 
 def last_step(shares, where, d_bcs, u_parts, d_value, steps, base, w_x, share_bc, w_dt):
@@ -645,7 +646,7 @@
             scratch_shapes=[pltpu.VMEM((SPAN, model), bf16)],
         ),
         out_shape=[
-            jax.ShapeDtypeStruct((many * SPAN, model), bf16), jax.ShapeDtypeStruct((each * SPAN, model), f32),
+            jax.ShapeDtypeStruct((many * SPAN, model), bf16), jax.ShapeDtypeStruct((each * SPAN, model), bf16),
             jax.ShapeDtypeStruct((length, narrow), bf16), jax.ShapeDtypeStruct((8, model), f32),
         ],
         compiler_params=pltpu.CompilerParams(vmem_limit_bytes=56 * 2**20),
@@ -655,7 +656,7 @@
 
 def input_kernel(tensor, *refs):
     parts, (u_ref, gain_ref, out_ref) = refs[:-3], refs[-3:]
-    d_part = parts[0][...]
+    d_part = parts[0][...].astype(f32)
     for ref in parts[1:]:
         d_part = d_part + ref[...].astype(f32)
     u = u_ref[...].astype(f32)
@@ -1038,7 +1039,7 @@
     )
     rows_per = length // shares
     for e in range(1, shares):
-        out_part = out_part + plan.across(sent_y[(shares - 1 - e) * rows_per : (shares - e) * rows_per], e).astype(f32)
+        out_part = out_part.astype(f32) + plan.across(sent_y[(shares - 1 - e) * rows_per : (shares - e) * rows_per], e).astype(f32)
     out_low = (u_part_low.astype(f32) + out_part).astype(bf16)
     out_blocks = plan.blocks_back(out_low)
     got_out = plan.from_sequence(out_blocks)
@@ -1101,7 +1102,7 @@
     small = jnp.concatenate(order + [shared], axis=0)
     count = rows[0].shape[0]
 
-    rest = jnp.concatenate([low_bc, back[0][2].astype(bf16), back[1][2].astype(bf16)], axis=1)
+    rest = jnp.concatenate([low_bc, back[0][2], back[1][2]], axis=1)
     size_r = model // groups
     sent_r, kept_r = (
         one_by_one(lax.dot_general(u, v, (((0,), (1,)), ((), ())), preferred_element_type=f32), size_r)
@@ -1127,9 +1128,9 @@
             )
     rest = kept_r
 
-    final = tie(back[1][1], pack)
+    final = tie(back[1][1], back_blocks)
     early_r = plan.first_send(dot_nn(x_sent, final).astype(bf16), True)
-    kept_x1 = lax.optimization_barrier(dot_nn(x_kept, tie(final, back_blocks)))
+    kept_x1 = lax.optimization_barrier(dot_nn(x_kept, final))
     next_r, held_r, late_r = plan.next_sums(kept_x1 + tie(early_r, back_blocks).astype(f32), True)
     late_r = held_r + late_r.astype(f32)
     grad_z, grad_out = plan.slot_total(zo_sums)

time: 330 us -> 327 us (level)
  starting transfers between devices: 74.2 us -> 80.5 us
  matrix products: 26.5 us -> 20.8 us
  other arithmetic: 43.5 us -> 38.2 us
    ppermute x43, waiting for transfers between devices: 27.8 us -> 35 us  [send(): return lax.ppermute(value, AXES, pairs)]
    dot_general x10, matrix products: 24 us -> 19.1 us  [dot_nn(): lax.dot_general(a, b, (((1,), (0,)), ((), ())), preferred_element_type=f32)]
    ppermute x43, starting transfers between devices: 44.2 us -> 48.3 us  [send(): return lax.ppermute(value, AXES, pairs)]
    all_to_all x2, starting transfers between devices: 17 us -> 20.3 us  [to_sequence(): lax.all_to_all(source.reshape(self.tensor, rows // self.k, width), 't', 0...]
    unnamed x113 -> x127, local copies, waits for them, and re-layouts: 13.5 us -> 16.4 us
  transfers between devices with their start and end apart: 48 -> 48, of which waited for: 14 -> 16; matrix products, arithmetic and copies ran while one was open for 27% -> 22% of each run, Pallas kernels for 22% -> 22%
where the time goes in v2:
time: 327 us; the launch traced here: 321 us
  Pallas kernels  90 us (28%)
  starting transfers between devices  80.5 us (25%)
  waiting for transfers between devices  53.4 us (16%)
  other arithmetic  38.2 us (12%)
  local copies, waits for them, and re-layouts  35.5 us (11%)
  matrix products  20.8 us (6%)
    ppermute x43, starting transfers between devices, send(): return lax.ppermute(value, AXES, pairs)  48.3 us
    pallas_call x2, Pallas kernels, backward_scan(): pl.pallas_call(functools.partial(backward_kernel, half * heads, bool(befo...  36.6 us
    ppermute x43, waiting for transfers between devices, send(): return lax.ppermute(value, AXES, pairs)  35 us
    all_to_all x2, starting transfers between devices, to_sequence(): lax.all_to_all(source.reshape(self.tensor, rows // self.k, width), 't', 0...  20.3 us
    dot_general x10, matrix products, dot_nn(): lax.dot_general(a, b, (((1,), (0,)), ((), ())), preferred_element_type=f32)  19.1 us
    unnamed x127, local copies, waits for them, and re-layouts  16.4 us
    pallas_call x1, Pallas kernels, forward_scan(): pl.pallas_call(forward_kernel, grid=(blocks,), in_specs=ins, out_specs=[r...  11.3 us
    pallas_call x1, Pallas kernels, norm_step(): pl.pallas_call(functools.partial(norm_kernel, shares, inner), grid_spec=p...  10.4 us
  transfers between devices with their start and end apart: 48, of which 16 were waited for; matrix products, arithmetic and copies ran while one was open for 22% of the time, Pallas kernels for 22%

profile of v2, /device:TPU:0, one launch (start us, length us, event | category | flops | bytes accessed | tf_op | source)
XLA Modules:
  0.0 321.0 jit_solution(7512384073783208439)
XLA Ops:
  4.2 3.1 collective-permute-start.4
  7.3 3.4 %collective-permute-start.1 = (s32[2,1024]{1,0:T(2,128)}, s32[2,1024]{1,0:T(2,128)S(1)}, u32[]{:S(2)}, u32[]{:S(2)}) collective-permute-start(s32[2,1024]{1,0:T(2,128)} %param.18), channel_id=1, source_target_pairs={{0,4},{1,5},{2,6},{3,7},{4,0},{5,1},{6,2},{7,3},{8,12},{9,13},{10,... | collective-permute-start | bytes 24584 | tf_op jit(solution)/shard_map/ppermute | solution.py:794
  19.5 5.4 %collective-permute-start.6 = (bf16[2,256,512]{2,1,0:T(8,128)(2,1)}, bf16[2,256,512]{2,1,0:T(8,128)(2,1)}, u32[]{:S(2)}, u32[]{:S(2)}) collective-permute-start(bf16[2,256,512]{2,1,0:T(8,128)(2,1)} %pad_maximum_fusion.12), channel_id=1, source_target_pairs={{0,0},{1,1},{2,4},{3,5},{4,2},{5,3},{6,6},{7,7},{8,8},{9,9},{10,12... | collective-permute-start | bytes 1572872 | tf_op jit(solution)/shard_map/ppermute | solution.py:794
  29.0 3.2 %collective-permute-done.3 = bf16[1,256,512]{2,1,0:T(8,128)(2,1)S(1)} collective-permute-done((bf16[1,256,512]{2,1,0:T(8,128)(2,1)S(1)}, bf16[1,256,512]{2,1,0:T(8,128)(2,1)S(1)}, u32[]{:S(2)}, u32[]{:S(2)}) %collective-permute-start.3) | collective-permute-done | bytes 262176 | tf_op jit(solution)/shard_map/ppermute | solution.py:794
  34.4 2.5 bitcast_select_fusion.1
  38.4 15.3 %all-to-all-start = ((bf16[4,512,256]{2,1,0:T(8,128)(2,1)}), bf16[4,512,256]{2,1,0:T(8,128)(2,1)}, u32[]{:S(2)}, u32[]{:S(2)}) async-start(bf16[4,512,256]{2,1,0:T(8,128)(2,1)} %pad_maximum_fusion.2), calls=%async_computation | async-start | bytes 2097152 | tf_op jit(solution)/shard_map/all_to_all | solution.py:824
  64.2 4.4 %collective-permute-done.8.refs_1_ = bf16[2,256,512]{2,1,0:T(8,128)(2,1)S(1)} collective-permute-done((bf16[2,256,512]{2,1,0:T(8,128)(2,1)S(1)}, bf16[2,256,512]{2,1,0:T(8,128)(2,1)S(1)}, u32[]{:S(2)}, u32[]{:S(2)}) %collective-permute-start.8) | collective-permute-done | bytes 524320 | tf_op jit(solution)/shard_map/ppermute | solution.py:794
  71.7 8.0 %collective-permute-done.11 = bf16[1,2,256,512]{3,2,1,0:T(8,128)(2,1)} collective-permute-done((bf16[1,2,256,512]{3,2,1,0:T(8,128)(2,1)}, bf16[1,2,256,512]{3,2,1,0:T(8,128)(2,1)}, u32[]{:S(2)}, u32[]{:S(2)}) %collective-permute-start.11) | collective-permute-done | bytes 524320 | tf_op jit(solution)/shard_map/ppermute | solution.py:794
  79.7 2.3 pad_maximum_fusion.4.refs_0_
  82.0 2.3 pad_maximum_fusion.3.refs_0_
  89.6 5.0 %all-to-all-start.1 = ((bf16[4,512,256]{2,1,0:T(8,128)(2,1)}), bf16[4,512,256]{2,1,0:T(8,128)(2,1)}, u32[]{:S(2)}, u32[]{:S(2)}) async-start(bf16[4,512,256]{2,1,0:T(8,128)(2,1)} %pad_maximum_fusion.5), calls=%async_computation.1 | async-start | bytes 2097152 | tf_op jit(solution)/shard_map/all_to_all | solution.py:824
  99.7 2.3 fusion.64.v_ref.vh_ref
  102.1 11.3 %shard_map.289 = (f32[1024,1024]{1,0:T(8,128)S(1)}, bf16[4,128,1024]{2,1,0:T(8,128)(2,1)S(1)}, f32[1024,48]{1,0:T(8,128)S(1)}, f32[16,1024]{1,0:T(8,128)S(1)}) custom-call(f32[1024,1024]{1,0:T(8,128)S(1)} %fusion.64.v_ref.vh_ref, f32[1024,1024]{1,0:T(8,128)S(1)} %fusion.64.v_ref.vh_ref, f32[1024,256]{1,0:T(8,128)S(1)} %fusion.65.bc_ref.bch_ref, ...), custom_call_target="tpu_custom_call" | custom-call | flops 1048576 | bytes 1048576 | tf_op jit(solution)/shard_map/pallas_call | solution.py:313
  126.3 7.4 %shard_map.292 = (f32[8,1024]{1,0:T(8,128)S(1)}, bf16[512,1024]{1,0:T(8,128)(2,1)S(1)}, bf16[512,1024]{1,0:T(8,128)(2,1)S(1)}) custom-call(s32[4]{0:T(128)S(1)} %pad_add_fusion.3.where_ref, bf16[1024,1024]{1,0:T(8,128)(2,1)S(1)} %copy-done.7, bf16[1024,1024]{1,0:T(8,128)(2,1)S(1)} %shard_map.290.wz_ref, f32[1024,1024]{1,0:T(8,128)S(1)} %copy-done.9, ...), custom_call_target="tpu_custom_call" | custom-call | flops 4294967296 | bytes 8388608 | tf_op jit(solution)/shard_map/pallas_call | solution.py:486
  136.0 10.4 %shard_map.293 = (bf16[1024,1024]{1,0:T(8,128)(2,1)S(1)}, bf16[1024,1024]{1,0:T(8,128)(2,1)S(1)}, bf16[1024,1024]{1,0:T(8,128)(2,1)S(1)}, f32[8,1024]{1,0:T(8,12...) custom-call(s32[4]{0:T(128)S(1)} %pad_add_fusion.3.where_ref, bf16[1024,1024]{1,0:T(8,128)(2,1)S(1)} %copy-done.7, ...), custom_call_target="tpu_custom_call" | custom-call | flops 6442450944 | bytes 18874368 | tf_op jit(solution)/shard_map/pallas_call | solution.py:509
  148.2 2.3 convolution_convert_fusion
  151.0 2.3 convolution_convert_fusion.1
  155.7 4.5 %all-to-all-start.2 = ((bf16[4,512,256]{2,1,0:T(8,128)(2,1)}), bf16[4,512,256]{2,1,0:T(8,128)(2,1)}, u32[]{:S(2)}, u32[]{:S(2)}) async-start(bf16[4,512,256]{2,1,0:T(8,128)(2,1)} %pad_maximum_fusion.8), calls=%async_computation.2 | async-start | bytes 2097152 | tf_op jit(solution)/shard_map/all_to_all | solution.py:834
  160.2 18.3 %shard_map.295 = (f32[1024,128]{1,0:T(8,128)}, f32[1024,128]{1,0:T(8,128)}, bf16[1024,512]{1,0:T(8,128)(2,1)}, bf16[1024,8]{1,0:T(8,128)(2,1)}, f32[8,512]{1,0:T...) custom-call(s32[4]{0:T(128)} %copy-done.26, f32[1024,1024]{1,0:T(8,128)} %copy-done.2, f32[1024,1024]{1,0:T(8,128)} %copy-done.2, ...), custom_call_target="tpu_custom_call" | custom-call | flops 524288 | bytes 524288 | tf_op jit(solution)/shard_map/pallas_call | solution.py:340
  178.6 2.6 convert_add_fusion.2
  183.7 2.5 convert_add_fusion.3
  190.2 7.4 %shard_map.296.refs_7_ = bf16[1024,1024]{1,0:T(8,128)(2,1)} custom-call(bf16[1024,1024]{1,0:T(8,128)(2,1)} %copy-done.30, bf16[1024,1024]{1,0:T(8,128)(2,1)} %copy-done.16, bf16[1024,512]{1,0:T(8,128)(2,1)} %get-tuple-element.125.value_ref, bf16[1024,1024]{1,0:T(8,128)(2,1)} %copy-done.10), custom_call_target="tpu_custom_call" | custom-call | flops 3221225472 | bytes 8388608 | tf_op jit(solution)/shard_map/pallas_call | solution.py:572
  211.4 18.3 %shard_map.297 = (f32[1024,128]{1,0:T(8,128)}, f32[1024,128]{1,0:T(8,128)}, bf16[1024,512]{1,0:T(8,128)(2,1)}, bf16[1024,8]{1,0:T(8,128)(2,1)}, f32[8,512]{1,0:T...) custom-call(s32[4]{0:T(128)} %copy-done.26, f32[1024,1024]{1,0:T(8,128)} %copy-done.2, f32[1024,1024]{1,0:T(8,128)} %copy-done.2, ...), custom_call_target="tpu_custom_call" | custom-call | flops 524288 | bytes 524288 | tf_op jit(solution)/shard_map/pallas_call | solution.py:340
  238.5 8.6 %shard_map.298 = (bf16[512,1024]{1,0:T(8,128)(2,1)}, bf16[512,1024]{1,0:T(8,128)(2,1)}, bf16[1024,128]{1,0:T(8,128)(2,1)}, f32[8,1024]{1,0:T(8,128)}) custom-call(s32[4]{0:T(128)} %copy-done.26, f32[1024,128]{1,0:T(8,128)} %get-tuple-element.138.refs_0_, f32[1024,128]{1,0:T(8,128)} %collective-permute-done.27.refs_1_, bf16[512,1024]{1,0:T(8,128)(2,1)} %copy-done.3, ...), custom_call_target="tpu_custom_call" | custom-call | flops 1073741824 | bytes 8388608 | tf_op jit(solution)/shard_map/pallas_call | solution.py:631
  252.3 2.1 collective-permute-start.38
  254.5 2.4 collective-permute-start.39
  263.3 3.7 %all-to-all-start.3 = ((bf16[4,512,256]{2,1,0:T(8,128)(2,1)}), bf16[4,512,256]{2,1,0:T(8,128)(2,1)S(1)}, u32[]{:S(2)}, u32[]{:S(2)}) async-start(bf16[4,512,256]{2,1,0:T(8,128)(2,1)} %shard_map.299), calls=%async_computation.3 | async-start | bytes 2097152 | tf_op jit(solution)/shard_map/all_to_all | solution.py:834
  272.9 7.8 %collective-permute-done.37 = bf16[512,512]{1,0:T(8,128)(2,1)S(1)} collective-permute-done((bf16[512,512]{1,0:T(8,128)(2,1)}, bf16[512,512]{1,0:T(8,128)(2,1)S(1)}, u32[]{:S(2)}, u32[]{:S(2)}) %collective-permute-start.37) | collective-permute-done | bytes 524320 | tf_op jit(solution)/shard_map/ppermute | solution.py:794
  283.3 9.4 %all-to-all-done.3 = bf16[4,512,256]{2,1,0:T(8,128)(2,1)S(1)} async-done(((bf16[4,512,256]{2,1,0:T(8,128)(2,1)}), bf16[4,512,256]{2,1,0:T(8,128)(2,1)S(1)}, u32[]{:S(2)}, u32[]{:S(2)}) %all-to-all-start.3) | async-done | bytes 1048608 | tf_op jit(solution)/shard_map/all_to_all | solution.py:834
  295.2 3.6 %all-to-all-start.4 = ((bf16[4,108,512]{2,1,0:T(8,128)(2,1)}), bf16[4,108,512]{2,1,0:T(8,128)(2,1)S(1)}, u32[]{:S(2)}, u32[]{:S(2)}) async-start(bf16[4,108,512]{2,1,0:T(8,128)(2,1)} %pad_maximum_fusion.14), calls=%async_computation.4 | async-start | bytes 917504 | tf_op jit(solution)/shard_map/all_to_all | solution.py:1164
  305.4 8.3 %all-to-all-done.4.last_ref = bf16[4,108,512]{2,1,0:T(8,128)(2,1)S(1)} async-done(((bf16[4,108,512]{2,1,0:T(8,128)(2,1)}), bf16[4,108,512]{2,1,0:T(8,128)(2,1)S(1)}, u32[]{:S(2)}, u32[]{:S(2)}) %all-to-all-start.4) | async-done | bytes 442400 | tf_op jit(solution)/shard_map/all_to_all | solution.py:1164
  314.6 2.4 collective-permute-done.42
  (371 shorter events, 125.3 us)
Async XLA Ops:
  3.5 16.0 %collective-permute-start.2 = (bf16[304,512]{1,0:T(8,128)(2,1)S(1)}, bf16[304,512]{1,0:T(8,128)(2,1)S(1)}, u32[]{:S(2)}, u32[]{:S(2)}) collective-permute-start(bf16[304,512]{1,0:T(8,128)(2,1)S(1)} %pad_maximum_fusion.15), channel_id=1, source_target_pairs={{0,0},{1,1},{2,4},{3,5},{4,2},{5,3},{6,6},{7,7},{8,8},{9,9},{10,12... | collective-permute-start | bytes 933896 | tf_op jit(solution)/shard_map/ppermute | solution.py:794
  4.2 15.3 %collective-permute-start.4 = (bf16[304,512]{1,0:T(8,128)(2,1)S(1)}, bf16[304,512]{1,0:T(8,128)(2,1)S(1)}, u32[]{:S(2)}, u32[]{:S(2)}) collective-permute-start(bf16[304,512]{1,0:T(8,128)(2,1)S(1)} %pad_maximum_fusion.15), channel_id=1, source_target_pairs={{0,1},{1,0},{2,5},{3,4},{4,3},{5,2},{6,7},{7,6},{8,9},{9,8},{10,13... | collective-permute-start | bytes 933896 | tf_op jit(solution)/shard_map/ppermute | solution.py:794
  13.0 21.3 %collective-permute-start = (bf16[2,2,512,256]{3,2,1,0:T(8,128)(2,1)}, bf16[2,2,512,256]{3,2,1,0:T(8,128)(2,1)}, u32[]{:S(2)}, u32[]{:S(2)}) collective-permute-start(bf16[2,2,512,256]{3,2,1,0:T(8,128)(2,1)} %pad_maximum_fusion.1), channel_id=1, source_target_pairs={{0,4},{1,5},{2,6},{3,7},{4,0},{5,1},{6,2},{7,3},{8,12},{9,13},{10,... | collective-permute-start | bytes 3145736 | tf_op jit(solution)/shard_map/ppermute | solution.py:794
  19.5 18.4 %collective-permute-start.6 = (bf16[2,256,512]{2,1,0:T(8,128)(2,1)}, bf16[2,256,512]{2,1,0:T(8,128)(2,1)}, u32[]{:S(2)}, u32[]{:S(2)}) collective-permute-start(bf16[2,256,512]{2,1,0:T(8,128)(2,1)} %pad_maximum_fusion.12), channel_id=1, source_target_pairs={{0,0},{1,1},{2,4},{3,5},{4,2},{5,3},{6,6},{7,7},{8,8},{9,9},{10,12... | collective-permute-start | bytes 1572872 | tf_op jit(solution)/shard_map/ppermute | solution.py:794
  24.9 13.6 %collective-permute-start.7 = (bf16[2,256,512]{2,1,0:T(8,128)(2,1)}, bf16[2,256,512]{2,1,0:T(8,128)(2,1)}, u32[]{:S(2)}, u32[]{:S(2)}) collective-permute-start(bf16[2,256,512]{2,1,0:T(8,128)(2,1)} %pad_maximum_fusion.12), channel_id=1, source_target_pairs={{0,1},{1,0},{2,5},{3,4},{4,3},{5,2},{6,7},{7,6},{8,9},{9,8},{10,13... | collective-permute-start | bytes 1572872 | tf_op jit(solution)/shard_map/ppermute | solution.py:794
  38.4 45.8 %all-to-all-start = ((bf16[4,512,256]{2,1,0:T(8,128)(2,1)}), bf16[4,512,256]{2,1,0:T(8,128)(2,1)}, u32[]{:S(2)}, u32[]{:S(2)}) async-start(bf16[4,512,256]{2,1,0:T(8,128)(2,1)} %pad_maximum_fusion.2), calls=%async_computation | async-start | bytes 2097152 | tf_op jit(solution)/shard_map/all_to_all | solution.py:824
  53.9 14.8 %collective-permute-start.8 = (bf16[2,256,512]{2,1,0:T(8,128)(2,1)S(1)}, bf16[2,256,512]{2,1,0:T(8,128)(2,1)S(1)}, u32[]{:S(2)}, u32[]{:S(2)}) collective-permute-start(bf16[2,256,512]{2,1,0:T(8,128)(2,1)S(1)} %pad_maximum_fusion.10.refs_0_), channel_id=1, source_target_pairs={{0,16},{1,17},{2,18},{3,19},{4,20},{5,21},{6,22},{7,23},{8,24},{9,... | collective-permute-start | bytes 1572872 | tf_op jit(solution)/shard_map/ppermute | solution.py:794
  55.4 14.8 %collective-permute-start.9 = (bf16[2,256,512]{2,1,0:T(8,128)(2,1)S(1)}, bf16[2,256,512]{2,1,0:T(8,128)(2,1)S(1)}, u32[]{:S(2)}, u32[]{:S(2)}) collective-permute-start(bf16[2,256,512]{2,1,0:T(8,128)(2,1)S(1)} %pad_maximum_fusion.11.refs_2_), channel_id=1, source_target_pairs={{0,8},{1,9},{2,10},{3,11},{4,12},{5,13},{6,14},{7,15},{8,0},{9,1},... | collective-permute-start | bytes 1572872 | tf_op jit(solution)/shard_map/ppermute | solution.py:794
  59.9 19.7 %collective-permute-start.11 = (bf16[1,2,256,512]{3,2,1,0:T(8,128)(2,1)}, bf16[1,2,256,512]{3,2,1,0:T(8,128)(2,1)}, u32[]{:S(2)}, u32[]{:S(2)}) collective-permute-start(bf16[1,2,256,512]{3,2,1,0:T(8,128)(2,1)} %maximum_bitcast_fusion.1), channel_id=1, source_target_pairs={{0,16},{1,17},{2,18},{3,19},{4,20},{5,21},{6,22},{7,23},{8,24},{9,... | collective-permute-start | bytes 1572872 | tf_op jit(solution)/shard_map/ppermute | solution.py:794
  61.3 20.7 %collective-permute-start.10 = (bf16[1,2,256,512]{3,2,1,0:T(8,128)(2,1)}, bf16[1,2,256,512]{3,2,1,0:T(8,128)(2,1)}, u32[]{:S(2)}, u32[]{:S(2)}) collective-permute-start(bf16[1,2,256,512]{3,2,1,0:T(8,128)(2,1)} %maximum_bitcast_fusion), channel_id=1, source_target_pairs={{0,8},{1,9},{2,10},{3,11},{4,12},{5,13},{6,14},{7,15},{8,0},{9,1},... | collective-permute-start | bytes 1572872 | tf_op jit(solution)/shard_map/ppermute | solution.py:794
  86.6 35.4 %collective-permute-start.14 = (bf16[2,2,256,512]{3,2,1,0:T(8,128)(2,1)}, bf16[2,2,256,512]{3,2,1,0:T(8,128)(2,1)}, u32[]{:S(2)}, u32[]{:S(2)}) collective-permute-start(bf16[2,2,256,512]{3,2,1,0:T(8,128)(2,1)} %pad_maximum_fusion.4.refs_0_), channel_id=1, source_target_pairs={{0,8},{1,9},{2,10},{3,11},{4,12},{5,13},{6,14},{7,15},{8,0},{9,1},... | collective-permute-start | bytes 3145736 | tf_op jit(solution)/shard_map/ppermute | solution.py:794
  88.1 33.9 %collective-permute-start.13 = (bf16[2,2,256,512]{3,2,1,0:T(8,128)(2,1)}, bf16[2,2,256,512]{3,2,1,0:T(8,128)(2,1)}, u32[]{:S(2)}, u32[]{:S(2)}) collective-permute-start(bf16[2,2,256,512]{3,2,1,0:T(8,128)(2,1)} %pad_maximum_fusion.3.refs_0_), channel_id=1, source_target_pairs={{0,16},{1,17},{2,18},{3,19},{4,20},{5,21},{6,22},{7,23},{8,24},{9,... | collective-permute-start | bytes 3145736 | tf_op jit(solution)/shard_map/ppermute | solution.py:794
  89.6 30.9 %all-to-all-start.1 = ((bf16[4,512,256]{2,1,0:T(8,128)(2,1)}), bf16[4,512,256]{2,1,0:T(8,128)(2,1)}, u32[]{:S(2)}, u32[]{:S(2)}) async-start(bf16[4,512,256]{2,1,0:T(8,128)(2,1)} %pad_maximum_fusion.5), calls=%async_computation.1 | async-start | bytes 2097152 | tf_op jit(solution)/shard_map/all_to_all | solution.py:824
  150.5 28.1 %collective-permute-start.19 = (bf16[512,1024]{1,0:T(8,128)(2,1)}, bf16[512,1024]{1,0:T(8,128)(2,1)}, u32[]{:S(2)}, u32[]{:S(2)}) collective-permute-start(bf16[512,1024]{1,0:T(8,128)(2,1)} %convolution_convert_fusion), channel_id=1, source_target_pairs={{0,16},{1,17},{2,18},{3,19},{4,20},{5,21},{6,22},{7,23},{8,24},{9,... | collective-permute-start | bytes 3145736 | tf_op jit(solution)/shard_map/ppermute | solution.py:794
  153.3 25.3 %collective-permute-start.18 = (bf16[512,1024]{1,0:T(8,128)(2,1)}, bf16[512,1024]{1,0:T(8,128)(2,1)}, u32[]{:S(2)}, u32[]{:S(2)}) collective-permute-start(bf16[512,1024]{1,0:T(8,128)(2,1)} %convolution_convert_fusion.1), channel_id=1, source_target_pairs={{0,8},{1,9},{2,10},{3,11},{4,12},{5,13},{6,14},{7,15},{8,0},{9,1},... | collective-permute-start | bytes 3145736 | tf_op jit(solution)/shard_map/ppermute | solution.py:794
  155.7 34.5 %all-to-all-start.2 = ((bf16[4,512,256]{2,1,0:T(8,128)(2,1)}), bf16[4,512,256]{2,1,0:T(8,128)(2,1)}, u32[]{:S(2)}, u32[]{:S(2)}) async-start(bf16[4,512,256]{2,1,0:T(8,128)(2,1)} %pad_maximum_fusion.8), calls=%async_computation.2 | async-start | bytes 2097152 | tf_op jit(solution)/shard_map/all_to_all | solution.py:834
  182.2 18.6 %collective-permute-start.21 = (bf16[256,1024]{1,0:T(8,128)(2,1)}, bf16[256,1024]{1,0:T(8,128)(2,1)}, u32[]{:S(2)}, u32[]{:S(2)}) collective-permute-start(bf16[256,1024]{1,0:T(8,128)(2,1)} %fusion.5), channel_id=1, source_target_pairs={{0,8},{1,9},{2,10},{3,11},{4,12},{5,13},{6,14},{7,15},{8,0},{9,1},... | collective-permute-start | bytes 1572872 | tf_op jit(solution)/shard_map/ppermute | solution.py:794
  188.4 13.2 %collective-permute-start.20 = (bf16[256,1024]{1,0:T(8,128)(2,1)}, bf16[256,1024]{1,0:T(8,128)(2,1)}, u32[]{:S(2)}, u32[]{:S(2)}) collective-permute-start(bf16[256,1024]{1,0:T(8,128)(2,1)} %fusion.4), channel_id=1, source_target_pairs={{0,16},{1,17},{2,18},{3,19},{4,20},{5,21},{6,22},{7,23},{8,24},{9,... | collective-permute-start | bytes 1572872 | tf_op jit(solution)/shard_map/ppermute | solution.py:794
  204.2 25.5 %collective-permute-start.24 = (bf16[2,128,512]{2,1,0:T(8,128)(2,1)S(1)}, bf16[2,128,512]{2,1,0:T(8,128)(2,1)S(1)}, u32[]{:S(2)}, u32[]{:S(2)}) collective-permute-start(bf16[2,128,512]{2,1,0:T(8,128)(2,1)S(1)} %get-tuple-element.279), channel_id=1, source_target_pairs={{0,1},{1,0},{2,5},{3,4},{4,3},{5,2},{6,7},{7,6},{8,9},{9,8},{10,13... | collective-permute-start | bytes 786440 | tf_op jit(solution)/shard_map/ppermute | solution.py:794
  206.1 23.7 %collective-permute-start.25 = (bf16[2,128,512]{2,1,0:T(8,128)(2,1)S(1)}, bf16[2,128,512]{2,1,0:T(8,128)(2,1)S(1)}, u32[]{:S(2)}, u32[]{:S(2)}) collective-permute-start(bf16[2,128,512]{2,1,0:T(8,128)(2,1)S(1)} %get-tuple-element.278), channel_id=1, source_target_pairs={{0,5},{1,4},{2,1},{3,0},{4,7},{5,6},{6,3},{7,2},{8,13},{9,12},{10,... | collective-permute-start | bytes 786440 | tf_op jit(solution)/shard_map/ppermute | solution.py:794
  207.3 22.5 %collective-permute-start.22 = (bf16[2,128,512]{2,1,0:T(8,128)(2,1)S(1)}, bf16[2,128,512]{2,1,0:T(8,128)(2,1)S(1)}, u32[]{:S(2)}, u32[]{:S(2)}) collective-permute-start(bf16[2,128,512]{2,1,0:T(8,128)(2,1)S(1)} %get-tuple-element.285), channel_id=1, source_target_pairs={{0,0},{1,1},{2,4},{3,5},{4,2},{5,3},{6,6},{7,7},{8,8},{9,9},{10,12... | collective-permute-start | bytes 786440 | tf_op jit(solution)/shard_map/ppermute | solution.py:794
  208.0 23.0 %collective-permute-start.23 = (bf16[2,128,512]{2,1,0:T(8,128)(2,1)S(1)}, bf16[2,128,512]{2,1,0:T(8,128)(2,1)S(1)}, u32[]{:S(2)}, u32[]{:S(2)}) collective-permute-start(bf16[2,128,512]{2,1,0:T(8,128)(2,1)S(1)} %get-tuple-element.284), channel_id=1, source_target_pairs={{0,4},{1,5},{2,0},{3,1},{4,6},{5,7},{6,2},{7,3},{8,12},{9,13},{10,... | collective-permute-start | bytes 786440 | tf_op jit(solution)/shard_map/ppermute | solution.py:794
  210.8 21.9 %collective-permute-start.26 = (bf16[512,512]{1,0:T(8,128)(2,1)}, bf16[512,512]{1,0:T(8,128)(2,1)}, u32[]{:S(2)}, u32[]{:S(2)}) collective-permute-start(bf16[512,512]{1,0:T(8,128)(2,1)} %convolution_convert_fusion.3), channel_id=1, source_target_pairs={{0,8},{1,9},{2,10},{3,11},{4,12},{5,13},{6,14},{7,15},{8,0},{9,1},... | collective-permute-start | bytes 1572872 | tf_op jit(solution)/shard_map/ppermute | solution.py:794
  252.3 62.3 %collective-permute-start.38 = (bf16[128,512]{1,0:T(8,128)(2,1)}, bf16[128,512]{1,0:T(8,128)(2,1)}, u32[]{:S(2)}, u32[]{:S(2)}) collective-permute-start(bf16[128,512]{1,0:T(8,128)(2,1)} %get-tuple-element.295), channel_id=1, source_target_pairs={{0,0},{1,1},{2,4},{3,5},{4,2},{5,3},{6,6},{7,7},{8,8},{9,9},{10,12... | collective-permute-start | bytes 393224 | tf_op jit(solution)/shard_map/ppermute | solution.py:794
  254.5 60.1 %collective-permute-start.39 = (bf16[128,512]{1,0:T(8,128)(2,1)}, bf16[128,512]{1,0:T(8,128)(2,1)}, u32[]{:S(2)}, u32[]{:S(2)}) collective-permute-start(bf16[128,512]{1,0:T(8,128)(2,1)} %get-tuple-element.294), channel_id=1, source_target_pairs={{0,4},{1,5},{2,0},{3,1},{4,6},{5,7},{6,2},{7,3},{8,12},{9,13},{10,... | collective-permute-start | bytes 393224 | tf_op jit(solution)/shard_map/ppermute | solution.py:794
  263.3 29.4 %all-to-all-start.3 = ((bf16[4,512,256]{2,1,0:T(8,128)(2,1)}), bf16[4,512,256]{2,1,0:T(8,128)(2,1)S(1)}, u32[]{:S(2)}, u32[]{:S(2)}) async-start(bf16[4,512,256]{2,1,0:T(8,128)(2,1)} %shard_map.299), calls=%async_computation.3 | async-start | bytes 2097152 | tf_op jit(solution)/shard_map/all_to_all | solution.py:834
  267.1 13.7 %collective-permute-start.37 = (bf16[512,512]{1,0:T(8,128)(2,1)}, bf16[512,512]{1,0:T(8,128)(2,1)S(1)}, u32[]{:S(2)}, u32[]{:S(2)}) collective-permute-start(bf16[512,512]{1,0:T(8,128)(2,1)} %convolution_convert_fusion.2), channel_id=1, source_target_pairs={{0,8},{1,9},{2,10},{3,11},{4,12},{5,13},{6,14},{7,15},{8,0},{9,1},... | collective-permute-start | bytes 1572872 | tf_op jit(solution)/shard_map/ppermute | solution.py:794
  268.7 24.2 %collective-permute-start.31 = (bf16[2,512,256]{2,1,0:T(8,128)(2,1)S(1)}, bf16[2,512,256]{2,1,0:T(8,128)(2,1)S(1)}, u32[]{:S(2)}, u32[]{:S(2)}) collective-permute-start(bf16[2,512,256]{2,1,0:T(8,128)(2,1)S(1)} %constant_dynamic-slice_fusion.3), channel_id=1, source_target_pairs={{0,4},{1,5},{2,6},{3,7},{4,0},{5,1},{6,2},{7,3},{8,12},{9,13},{10,... | collective-permute-start | bytes 1572872 | tf_op jit(solution)/shard_map/ppermute | solution.py:794
  281.9 13.3 %collective-permute-start.40 = (bf16[256,512]{1,0:T(8,128)(2,1)S(1)}, bf16[256,512]{1,0:T(8,128)(2,1)S(1)}, u32[]{:S(2)}, u32[]{:S(2)}) collective-permute-start(bf16[256,512]{1,0:T(8,128)(2,1)S(1)} %fusion.15), channel_id=1, source_target_pairs={{0,16},{1,17},{2,18},{3,19},{4,20},{5,21},{6,22},{7,23},{8,24},{9,... | collective-permute-start | bytes 786440 | tf_op jit(solution)/shard_map/ppermute | solution.py:794
  295.2 18.5 %all-to-all-start.4 = ((bf16[4,108,512]{2,1,0:T(8,128)(2,1)}), bf16[4,108,512]{2,1,0:T(8,128)(2,1)S(1)}, u32[]{:S(2)}, u32[]{:S(2)}) async-start(bf16[4,108,512]{2,1,0:T(8,128)(2,1)} %pad_maximum_fusion.14), calls=%async_computation.4 | async-start | bytes 917504 | tf_op jit(solution)/shard_map/all_to_all | solution.py:1164
  299.5 15.1 %collective-permute-start.41 = (bf16[128,512]{1,0:T(8,128)(2,1)}, bf16[128,512]{1,0:T(8,128)(2,1)S(1)}, u32[]{:S(2)}, u32[]{:S(2)}) collective-permute-start(bf16[128,512]{1,0:T(8,128)(2,1)} %get-tuple-element.293), channel_id=1, source_target_pairs={{0,1},{1,0},{2,5},{3,4},{4,3},{5,2},{6,7},{7,6},{8,9},{9,8},{10,13... | collective-permute-start | bytes 393224 | tf_op jit(solution)/shard_map/ppermute | solution.py:794
  301.5 15.5 %collective-permute-start.42 = (bf16[128,512]{1,0:T(8,128)(2,1)S(1)}, bf16[128,512]{1,0:T(8,128)(2,1)S(1)}, u32[]{:S(2)}, u32[]{:S(2)}) collective-permute-start(bf16[128,512]{1,0:T(8,128)(2,1)S(1)} %get-tuple-element.292), channel_id=1, source_target_pairs={{0,5},{1,4},{2,1},{3,0},{4,7},{5,6},{6,3},{7,2},{8,13},{9,12},{10,... | collective-permute-start | bytes 393224 | tf_op jit(solution)/shard_map/ppermute | solution.py:794
  (77 other events, 1107.0 us)

commit v3 on v2

--- a/solution.py
+++ b/solution.py
@@ -839,7 +839,7 @@
         kept = lax.dynamic_slice_in_dim(got, self.c * per_dp, per_dp, 0)
         sent = lax.dynamic_slice_in_dim(got, (1 - self.c) * per_dp, per_dp, 0)
         other = self.send(sent, lambda g, c, t: (g, 1 - c, t))
-        return jnp.concatenate(order_by_xor([kept, other], self.c), axis=1)
+        return jnp.concatenate(order_by_xor([kept, other], self.c), axis=1), other
 
     def gather_shares(self, part):
         got = [part] + [self.across(part, e) for e in range(1, self.shares)]
@@ -1085,7 +1085,7 @@
     ]
     back_blocks = input_step(tensor, d_parts, tie(u_part_low, x0_blocks), norm_gain[None])
     got_back = plan.from_sequence(back_blocks)
-    output = plan.pieces_of_batch(tie(got_out, back_blocks))
+    output, done = plan.pieces_of_batch(tie(got_out, back_blocks))
 
     rows = []
     for j in two:
@@ -1106,7 +1106,7 @@
     size_r = model // groups
     sent_r, kept_r = (
         one_by_one(lax.dot_general(u, v, (((0,), (1,)), ((), ())), preferred_element_type=f32), size_r)
-        for u, v in ((rest, x_sent), (tie(rest, back_blocks), x_kept))
+        for u, v in ((rest, x_sent), (tie(rest, done), x_kept))
     )
     pack = None
     for n, bit in enumerate(plan.bits):
@@ -1115,7 +1115,7 @@
         pack = message if pack is None else pack
         got = plan.around(message, bit)
         if n == 0:
-            got = tie(got, back_blocks)
+            got = tie(got, done)
         tall, lines = beside.shape[0], small.shape[0]
         kept_r = kept_r + one_by_one(got[:tall], size_r).astype(f32)
         small = small + sum(got[tall + i * lines : tall + (i + 1) * lines].astype(f32) for i in (2, 1, 0))
@@ -1128,14 +1128,14 @@
             )
     rest = kept_r
 
-    final = tie(back[1][1], back_blocks)
+    final = tie(back[1][1], done)
     early_r = plan.first_send(dot_nn(x_sent, final).astype(bf16), True)
     kept_x1 = lax.optimization_barrier(dot_nn(x_kept, final))
-    next_r, held_r, late_r = plan.next_sums(kept_x1 + tie(early_r, back_blocks).astype(f32), True)
+    next_r, held_r, late_r = plan.next_sums(kept_x1 + tie(early_r, done).astype(f32), True)
     late_r = held_r + late_r.astype(f32)
     grad_z, grad_out = plan.slot_total(zo_sums)
     grad_out = grad_out.T
-    input_grad = cotangent.astype(f32) + plan.pieces_of_batch(got_back).astype(f32)
+    input_grad = cotangent.astype(f32) + plan.pieces_of_batch(got_back)[0].astype(f32)
 
     beyond = wide // shares
     parts = [rest[:beyond]] + [

time: 327 us -> 329 us (level)
    unnamed x127 -> x129, local copies, waits for them, and re-layouts: 16.4 us -> 16.7 us
  transfers between devices with their start and end apart: 48 -> 48, of which waited for: 16 -> 18; matrix products, arithmetic and copies ran while one was open for 22% -> 23% of each run, Pallas kernels for 22% -> 22%
where the time goes in v3:
time: 329 us; the launch traced here: 323 us
  Pallas kernels  89.9 us (27%)
  starting transfers between devices  83.6 us (25%)
  waiting for transfers between devices  52.1 us (16%)
  other arithmetic  37.6 us (11%)
  local copies, waits for them, and re-layouts  37.1 us (11%)
  matrix products  20.3 us (6%)
    ppermute x43, starting transfers between devices, send(): return lax.ppermute(value, AXES, pairs)  49 us
    pallas_call x2, Pallas kernels, backward_scan(): pl.pallas_call(functools.partial(backward_kernel, half * heads, bool(befo...  36.6 us
    ppermute x43, waiting for transfers between devices, send(): return lax.ppermute(value, AXES, pairs)  35.1 us
    all_to_all x2, starting transfers between devices, to_sequence(): lax.all_to_all(source.reshape(self.tensor, rows // self.k, width), 't', 0...  20.3 us
    dot_general x10, matrix products, dot_nn(): lax.dot_general(a, b, (((1,), (0,)), ((), ())), preferred_element_type=f32)  18.6 us
    unnamed x129, local copies, waits for them, and re-layouts  16.7 us
    pallas_call x1, Pallas kernels, forward_scan(): pl.pallas_call(forward_kernel, grid=(blocks,), in_specs=ins, out_specs=[r...  11.3 us
    pallas_call x1, Pallas kernels, norm_step(): pl.pallas_call(functools.partial(norm_kernel, shares, inner), grid_spec=p...  10.4 us
  transfers between devices with their start and end apart: 48, of which 18 were waited for; matrix products, arithmetic and copies ran while one was open for 23% of the time, Pallas kernels for 22%

profile of v3, /device:TPU:0, one launch (start us, length us, event | category | flops | bytes accessed | tf_op | source)
XLA Modules:
  0.0 323.3 jit_solution(1833308487143448200)
XLA Ops:
  4.2 3.1 collective-permute-start.4
  7.3 3.4 %collective-permute-start.1 = (s32[2,1024]{1,0:T(2,128)}, s32[2,1024]{1,0:T(2,128)S(1)}, u32[]{:S(2)}, u32[]{:S(2)}) collective-permute-start(s32[2,1024]{1,0:T(2,128)} %param.18), channel_id=1, source_target_pairs={{0,4},{1,5},{2,6},{3,7},{4,0},{5,1},{6,2},{7,3},{8,12},{9,13},{10,... | collective-permute-start | bytes 24584 | tf_op jit(solution)/shard_map/ppermute | solution.py:794
  19.5 5.4 %collective-permute-start.6 = (bf16[2,256,512]{2,1,0:T(8,128)(2,1)}, bf16[2,256,512]{2,1,0:T(8,128)(2,1)}, u32[]{:S(2)}, u32[]{:S(2)}) collective-permute-start(bf16[2,256,512]{2,1,0:T(8,128)(2,1)} %pad_maximum_fusion.12), channel_id=1, source_target_pairs={{0,0},{1,1},{2,4},{3,5},{4,2},{5,3},{6,6},{7,7},{8,8},{9,9},{10,12... | collective-permute-start | bytes 1572872 | tf_op jit(solution)/shard_map/ppermute | solution.py:794
  29.1 3.2 %collective-permute-done.3 = bf16[1,256,512]{2,1,0:T(8,128)(2,1)S(1)} collective-permute-done((bf16[1,256,512]{2,1,0:T(8,128)(2,1)S(1)}, bf16[1,256,512]{2,1,0:T(8,128)(2,1)S(1)}, u32[]{:S(2)}, u32[]{:S(2)}) %collective-permute-start.3) | collective-permute-done | bytes 262176 | tf_op jit(solution)/shard_map/ppermute | solution.py:794
  34.4 2.5 bitcast_select_fusion.1
  38.5 15.3 %all-to-all-start = ((bf16[4,512,256]{2,1,0:T(8,128)(2,1)}), bf16[4,512,256]{2,1,0:T(8,128)(2,1)}, u32[]{:S(2)}, u32[]{:S(2)}) async-start(bf16[4,512,256]{2,1,0:T(8,128)(2,1)} %pad_maximum_fusion.2), calls=%async_computation | async-start | bytes 2097152 | tf_op jit(solution)/shard_map/all_to_all | solution.py:824
  64.2 4.4 %collective-permute-done.8.refs_1_ = bf16[2,256,512]{2,1,0:T(8,128)(2,1)S(1)} collective-permute-done((bf16[2,256,512]{2,1,0:T(8,128)(2,1)S(1)}, bf16[2,256,512]{2,1,0:T(8,128)(2,1)S(1)}, u32[]{:S(2)}, u32[]{:S(2)}) %collective-permute-start.8) | collective-permute-done | bytes 524320 | tf_op jit(solution)/shard_map/ppermute | solution.py:794
  71.7 8.0 %collective-permute-done.11 = bf16[1,2,256,512]{3,2,1,0:T(8,128)(2,1)} collective-permute-done((bf16[1,2,256,512]{3,2,1,0:T(8,128)(2,1)}, bf16[1,2,256,512]{3,2,1,0:T(8,128)(2,1)}, u32[]{:S(2)}, u32[]{:S(2)}) %collective-permute-start.11) | collective-permute-done | bytes 524320 | tf_op jit(solution)/shard_map/ppermute | solution.py:794
  79.7 2.4 pad_maximum_fusion.4.refs_0_
  82.0 2.3 pad_maximum_fusion.3.refs_0_
  89.7 5.0 %all-to-all-start.1 = ((bf16[4,512,256]{2,1,0:T(8,128)(2,1)}), bf16[4,512,256]{2,1,0:T(8,128)(2,1)}, u32[]{:S(2)}, u32[]{:S(2)}) async-start(bf16[4,512,256]{2,1,0:T(8,128)(2,1)} %pad_maximum_fusion.5), calls=%async_computation.1 | async-start | bytes 2097152 | tf_op jit(solution)/shard_map/all_to_all | solution.py:824
  99.8 2.3 fusion.64.v_ref.vh_ref
  102.2 11.3 %shard_map.289 = (f32[1024,1024]{1,0:T(8,128)S(1)}, bf16[4,128,1024]{2,1,0:T(8,128)(2,1)S(1)}, f32[1024,48]{1,0:T(8,128)S(1)}, f32[16,1024]{1,0:T(8,128)S(1)}) custom-call(f32[1024,1024]{1,0:T(8,128)S(1)} %fusion.64.v_ref.vh_ref, f32[1024,1024]{1,0:T(8,128)S(1)} %fusion.64.v_ref.vh_ref, f32[1024,256]{1,0:T(8,128)S(1)} %fusion.65.bc_ref.bch_ref, ...), custom_call_target="tpu_custom_call" | custom-call | flops 1048576 | bytes 1048576 | tf_op jit(solution)/shard_map/pallas_call | solution.py:313
  126.4 7.4 %shard_map.292 = (f32[8,1024]{1,0:T(8,128)S(1)}, bf16[512,1024]{1,0:T(8,128)(2,1)S(1)}, bf16[512,1024]{1,0:T(8,128)(2,1)S(1)}) custom-call(s32[4]{0:T(128)S(1)} %pad_add_fusion.3.where_ref, bf16[1024,1024]{1,0:T(8,128)(2,1)S(1)} %copy-done.7, bf16[1024,1024]{1,0:T(8,128)(2,1)S(1)} %shard_map.290.wz_ref, f32[1024,1024]{1,0:T(8,128)S(1)} %copy-done.9, ...), custom_call_target="tpu_custom_call" | custom-call | flops 4294967296 | bytes 8388608 | tf_op jit(solution)/shard_map/pallas_call | solution.py:486
  136.2 10.4 %shard_map.293 = (bf16[1024,1024]{1,0:T(8,128)(2,1)S(1)}, bf16[1024,1024]{1,0:T(8,128)(2,1)S(1)}, bf16[1024,1024]{1,0:T(8,128)(2,1)S(1)}, f32[8,1024]{1,0:T(8,12...) custom-call(s32[4]{0:T(128)S(1)} %pad_add_fusion.3.where_ref, bf16[1024,1024]{1,0:T(8,128)(2,1)S(1)} %copy-done.7, ...), custom_call_target="tpu_custom_call" | custom-call | flops 6442450944 | bytes 18874368 | tf_op jit(solution)/shard_map/pallas_call | solution.py:509
  148.4 2.3 convolution_convert_fusion
  151.1 2.3 convolution_convert_fusion.1
  155.8 4.6 %all-to-all-start.2 = ((bf16[4,512,256]{2,1,0:T(8,128)(2,1)}), bf16[4,512,256]{2,1,0:T(8,128)(2,1)}, u32[]{:S(2)}, u32[]{:S(2)}) async-start(bf16[4,512,256]{2,1,0:T(8,128)(2,1)} %pad_maximum_fusion.8), calls=%async_computation.2 | async-start | bytes 2097152 | tf_op jit(solution)/shard_map/all_to_all | solution.py:834
  160.4 18.3 %shard_map.295 = (f32[1024,128]{1,0:T(8,128)}, f32[1024,128]{1,0:T(8,128)}, bf16[1024,512]{1,0:T(8,128)(2,1)}, bf16[1024,8]{1,0:T(8,128)(2,1)}, f32[8,512]{1,0:T...) custom-call(s32[4]{0:T(128)} %copy-done.28, f32[1024,1024]{1,0:T(8,128)} %copy-done.2, f32[1024,1024]{1,0:T(8,128)} %copy-done.2, ...), custom_call_target="tpu_custom_call" | custom-call | flops 524288 | bytes 524288 | tf_op jit(solution)/shard_map/pallas_call | solution.py:340
  178.8 2.6 convert_add_fusion.2
  184.0 2.5 convert_add_fusion.3
  190.5 7.4 %shard_map.296.refs_7_ = bf16[1024,1024]{1,0:T(8,128)(2,1)} custom-call(bf16[1024,1024]{1,0:T(8,128)(2,1)} %copy-done.32, bf16[1024,1024]{1,0:T(8,128)(2,1)} %copy-done.16, bf16[1024,512]{1,0:T(8,128)(2,1)} %get-tuple-element.125.value_ref, bf16[1024,1024]{1,0:T(8,128)(2,1)} %copy-done.10), custom_call_target="tpu_custom_call" | custom-call | flops 3221225472 | bytes 8388608 | tf_op jit(solution)/shard_map/pallas_call | solution.py:572
  213.8 18.3 %shard_map.297 = (f32[1024,128]{1,0:T(8,128)}, f32[1024,128]{1,0:T(8,128)}, bf16[1024,512]{1,0:T(8,128)(2,1)}, bf16[1024,8]{1,0:T(8,128)(2,1)}, f32[8,512]{1,0:T...) custom-call(s32[4]{0:T(128)} %copy-done.28, f32[1024,1024]{1,0:T(8,128)} %copy-done.2, f32[1024,1024]{1,0:T(8,128)} %copy-done.2, ...), custom_call_target="tpu_custom_call" | custom-call | flops 524288 | bytes 524288 | tf_op jit(solution)/shard_map/pallas_call | solution.py:340
  234.3 2.5 collective-permute-start.27
  240.9 8.6 %shard_map.298 = (bf16[512,1024]{1,0:T(8,128)(2,1)}, bf16[512,1024]{1,0:T(8,128)(2,1)}, bf16[1024,128]{1,0:T(8,128)(2,1)}, f32[8,1024]{1,0:T(8,128)}) custom-call(s32[4]{0:T(128)} %copy-done.28, f32[1024,128]{1,0:T(8,128)} %get-tuple-element.138.refs_0_, f32[1024,128]{1,0:T(8,128)} %copy-done.49, bf16[512,1024]{1,0:T(8,128)(2,1)} %copy-done.3, ...), custom_call_target="tpu_custom_call" | custom-call | flops 1073741824 | bytes 8388608 | tf_op jit(solution)/shard_map/pallas_call | solution.py:631
  263.2 5.5 %all-to-all-start.3 = ((bf16[4,512,256]{2,1,0:T(8,128)(2,1)}), bf16[4,512,256]{2,1,0:T(8,128)(2,1)}, u32[]{:S(2)}, u32[]{:S(2)}) async-start(bf16[4,512,256]{2,1,0:T(8,128)(2,1)} %shard_map.299), calls=%async_computation.3 | async-start | bytes 2097152 | tf_op jit(solution)/shard_map/all_to_all | solution.py:834
  275.6 2.4 collective-permute-done.34
  279.7 5.6 %collective-permute-done.37 = bf16[512,512]{1,0:T(8,128)(2,1)S(1)} collective-permute-done((bf16[512,512]{1,0:T(8,128)(2,1)S(1)}, bf16[512,512]{1,0:T(8,128)(2,1)S(1)}, u32[]{:S(2)}, u32[]{:S(2)}) %collective-permute-start.37) | collective-permute-done | bytes 524320 | tf_op jit(solution)/shard_map/ppermute | solution.py:794
  286.1 8.8 %all-to-all-done.3 = bf16[4,512,256]{2,1,0:T(8,128)(2,1)} async-done(((bf16[4,512,256]{2,1,0:T(8,128)(2,1)}), bf16[4,512,256]{2,1,0:T(8,128)(2,1)}, u32[]{:S(2)}, u32[]{:S(2)}) %all-to-all-start.3) | async-done | bytes 1048608 | tf_op jit(solution)/shard_map/all_to_all | solution.py:834
  297.0 4.4 %all-to-all-start.4 = ((bf16[4,108,512]{2,1,0:T(8,128)(2,1)}), bf16[4,108,512]{2,1,0:T(8,128)(2,1)S(1)}, u32[]{:S(2)}, u32[]{:S(2)}) async-start(bf16[4,108,512]{2,1,0:T(8,128)(2,1)} %pad_maximum_fusion.14), calls=%async_computation.4 | async-start | bytes 917504 | tf_op jit(solution)/shard_map/all_to_all | solution.py:1164
  308.1 7.7 %all-to-all-done.4.last_ref = bf16[4,108,512]{2,1,0:T(8,128)(2,1)S(1)} async-done(((bf16[4,108,512]{2,1,0:T(8,128)(2,1)}), bf16[4,108,512]{2,1,0:T(8,128)(2,1)S(1)}, u32[]{:S(2)}, u32[]{:S(2)}) %all-to-all-start.4) | async-done | bytes 442400 | tf_op jit(solution)/shard_map/all_to_all | solution.py:1164
  316.7 2.6 collective-permute-done.42
  (373 shorter events, 128.0 us)
Async XLA Ops:
  3.5 16.0 %collective-permute-start.2 = (bf16[304,512]{1,0:T(8,128)(2,1)S(1)}, bf16[304,512]{1,0:T(8,128)(2,1)S(1)}, u32[]{:S(2)}, u32[]{:S(2)}) collective-permute-start(bf16[304,512]{1,0:T(8,128)(2,1)S(1)} %pad_maximum_fusion.15), channel_id=1, source_target_pairs={{0,0},{1,1},{2,4},{3,5},{4,2},{5,3},{6,6},{7,7},{8,8},{9,9},{10,12... | collective-permute-start | bytes 933896 | tf_op jit(solution)/shard_map/ppermute | solution.py:794
  4.2 15.3 %collective-permute-start.4 = (bf16[304,512]{1,0:T(8,128)(2,1)S(1)}, bf16[304,512]{1,0:T(8,128)(2,1)S(1)}, u32[]{:S(2)}, u32[]{:S(2)}) collective-permute-start(bf16[304,512]{1,0:T(8,128)(2,1)S(1)} %pad_maximum_fusion.15), channel_id=1, source_target_pairs={{0,1},{1,0},{2,5},{3,4},{4,3},{5,2},{6,7},{7,6},{8,9},{9,8},{10,13... | collective-permute-start | bytes 933896 | tf_op jit(solution)/shard_map/ppermute | solution.py:794
  13.0 21.4 %collective-permute-start = (bf16[2,2,512,256]{3,2,1,0:T(8,128)(2,1)}, bf16[2,2,512,256]{3,2,1,0:T(8,128)(2,1)}, u32[]{:S(2)}, u32[]{:S(2)}) collective-permute-start(bf16[2,2,512,256]{3,2,1,0:T(8,128)(2,1)} %pad_maximum_fusion.1), channel_id=1, source_target_pairs={{0,4},{1,5},{2,6},{3,7},{4,0},{5,1},{6,2},{7,3},{8,12},{9,13},{10,... | collective-permute-start | bytes 3145736 | tf_op jit(solution)/shard_map/ppermute | solution.py:794
  19.5 18.5 %collective-permute-start.6 = (bf16[2,256,512]{2,1,0:T(8,128)(2,1)}, bf16[2,256,512]{2,1,0:T(8,128)(2,1)}, u32[]{:S(2)}, u32[]{:S(2)}) collective-permute-start(bf16[2,256,512]{2,1,0:T(8,128)(2,1)} %pad_maximum_fusion.12), channel_id=1, source_target_pairs={{0,0},{1,1},{2,4},{3,5},{4,2},{5,3},{6,6},{7,7},{8,8},{9,9},{10,12... | collective-permute-start | bytes 1572872 | tf_op jit(solution)/shard_map/ppermute | solution.py:794
  24.9 13.6 %collective-permute-start.7 = (bf16[2,256,512]{2,1,0:T(8,128)(2,1)}, bf16[2,256,512]{2,1,0:T(8,128)(2,1)}, u32[]{:S(2)}, u32[]{:S(2)}) collective-permute-start(bf16[2,256,512]{2,1,0:T(8,128)(2,1)} %pad_maximum_fusion.12), channel_id=1, source_target_pairs={{0,1},{1,0},{2,5},{3,4},{4,3},{5,2},{6,7},{7,6},{8,9},{9,8},{10,13... | collective-permute-start | bytes 1572872 | tf_op jit(solution)/shard_map/ppermute | solution.py:794
  38.5 45.9 %all-to-all-start = ((bf16[4,512,256]{2,1,0:T(8,128)(2,1)}), bf16[4,512,256]{2,1,0:T(8,128)(2,1)}, u32[]{:S(2)}, u32[]{:S(2)}) async-start(bf16[4,512,256]{2,1,0:T(8,128)(2,1)} %pad_maximum_fusion.2), calls=%async_computation | async-start | bytes 2097152 | tf_op jit(solution)/shard_map/all_to_all | solution.py:824
  53.9 14.8 %collective-permute-start.8 = (bf16[2,256,512]{2,1,0:T(8,128)(2,1)S(1)}, bf16[2,256,512]{2,1,0:T(8,128)(2,1)S(1)}, u32[]{:S(2)}, u32[]{:S(2)}) collective-permute-start(bf16[2,256,512]{2,1,0:T(8,128)(2,1)S(1)} %pad_maximum_fusion.10.refs_0_), channel_id=1, source_target_pairs={{0,16},{1,17},{2,18},{3,19},{4,20},{5,21},{6,22},{7,23},{8,24},{9,... | collective-permute-start | bytes 1572872 | tf_op jit(solution)/shard_map/ppermute | solution.py:794
  55.4 14.8 %collective-permute-start.9 = (bf16[2,256,512]{2,1,0:T(8,128)(2,1)S(1)}, bf16[2,256,512]{2,1,0:T(8,128)(2,1)S(1)}, u32[]{:S(2)}, u32[]{:S(2)}) collective-permute-start(bf16[2,256,512]{2,1,0:T(8,128)(2,1)S(1)} %pad_maximum_fusion.11.refs_2_), channel_id=1, source_target_pairs={{0,8},{1,9},{2,10},{3,11},{4,12},{5,13},{6,14},{7,15},{8,0},{9,1},... | collective-permute-start | bytes 1572872 | tf_op jit(solution)/shard_map/ppermute | solution.py:794
  59.9 19.7 %collective-permute-start.11 = (bf16[1,2,256,512]{3,2,1,0:T(8,128)(2,1)}, bf16[1,2,256,512]{3,2,1,0:T(8,128)(2,1)}, u32[]{:S(2)}, u32[]{:S(2)}) collective-permute-start(bf16[1,2,256,512]{3,2,1,0:T(8,128)(2,1)} %maximum_bitcast_fusion.1), channel_id=1, source_target_pairs={{0,16},{1,17},{2,18},{3,19},{4,20},{5,21},{6,22},{7,23},{8,24},{9,... | collective-permute-start | bytes 1572872 | tf_op jit(solution)/shard_map/ppermute | solution.py:794
  61.3 20.7 %collective-permute-start.10 = (bf16[1,2,256,512]{3,2,1,0:T(8,128)(2,1)}, bf16[1,2,256,512]{3,2,1,0:T(8,128)(2,1)}, u32[]{:S(2)}, u32[]{:S(2)}) collective-permute-start(bf16[1,2,256,512]{3,2,1,0:T(8,128)(2,1)} %maximum_bitcast_fusion), channel_id=1, source_target_pairs={{0,8},{1,9},{2,10},{3,11},{4,12},{5,13},{6,14},{7,15},{8,0},{9,1},... | collective-permute-start | bytes 1572872 | tf_op jit(solution)/shard_map/ppermute | solution.py:794
  86.7 35.4 %collective-permute-start.14 = (bf16[2,2,256,512]{3,2,1,0:T(8,128)(2,1)}, bf16[2,2,256,512]{3,2,1,0:T(8,128)(2,1)}, u32[]{:S(2)}, u32[]{:S(2)}) collective-permute-start(bf16[2,2,256,512]{3,2,1,0:T(8,128)(2,1)} %pad_maximum_fusion.4.refs_0_), channel_id=1, source_target_pairs={{0,8},{1,9},{2,10},{3,11},{4,12},{5,13},{6,14},{7,15},{8,0},{9,1},... | collective-permute-start | bytes 3145736 | tf_op jit(solution)/shard_map/ppermute | solution.py:794
  88.2 33.9 %collective-permute-start.13 = (bf16[2,2,256,512]{3,2,1,0:T(8,128)(2,1)}, bf16[2,2,256,512]{3,2,1,0:T(8,128)(2,1)}, u32[]{:S(2)}, u32[]{:S(2)}) collective-permute-start(bf16[2,2,256,512]{3,2,1,0:T(8,128)(2,1)} %pad_maximum_fusion.3.refs_0_), channel_id=1, source_target_pairs={{0,16},{1,17},{2,18},{3,19},{4,20},{5,21},{6,22},{7,23},{8,24},{9,... | collective-permute-start | bytes 3145736 | tf_op jit(solution)/shard_map/ppermute | solution.py:794
  89.7 30.9 %all-to-all-start.1 = ((bf16[4,512,256]{2,1,0:T(8,128)(2,1)}), bf16[4,512,256]{2,1,0:T(8,128)(2,1)}, u32[]{:S(2)}, u32[]{:S(2)}) async-start(bf16[4,512,256]{2,1,0:T(8,128)(2,1)} %pad_maximum_fusion.5), calls=%async_computation.1 | async-start | bytes 2097152 | tf_op jit(solution)/shard_map/all_to_all | solution.py:824
  150.6 28.1 %collective-permute-start.19 = (bf16[512,1024]{1,0:T(8,128)(2,1)}, bf16[512,1024]{1,0:T(8,128)(2,1)}, u32[]{:S(2)}, u32[]{:S(2)}) collective-permute-start(bf16[512,1024]{1,0:T(8,128)(2,1)} %convolution_convert_fusion), channel_id=1, source_target_pairs={{0,16},{1,17},{2,18},{3,19},{4,20},{5,21},{6,22},{7,23},{8,24},{9,... | collective-permute-start | bytes 3145736 | tf_op jit(solution)/shard_map/ppermute | solution.py:794
  153.4 25.3 %collective-permute-start.18 = (bf16[512,1024]{1,0:T(8,128)(2,1)}, bf16[512,1024]{1,0:T(8,128)(2,1)}, u32[]{:S(2)}, u32[]{:S(2)}) collective-permute-start(bf16[512,1024]{1,0:T(8,128)(2,1)} %convolution_convert_fusion.1), channel_id=1, source_target_pairs={{0,8},{1,9},{2,10},{3,11},{4,12},{5,13},{6,14},{7,15},{8,0},{9,1},... | collective-permute-start | bytes 3145736 | tf_op jit(solution)/shard_map/ppermute | solution.py:794
  155.8 34.7 %all-to-all-start.2 = ((bf16[4,512,256]{2,1,0:T(8,128)(2,1)}), bf16[4,512,256]{2,1,0:T(8,128)(2,1)}, u32[]{:S(2)}, u32[]{:S(2)}) async-start(bf16[4,512,256]{2,1,0:T(8,128)(2,1)} %pad_maximum_fusion.8), calls=%async_computation.2 | async-start | bytes 2097152 | tf_op jit(solution)/shard_map/all_to_all | solution.py:834
  160.3 79.7 %collective-permute-start.28 = (bf16[512,1024]{1,0:T(8,128)(2,1)S(1)}, bf16[512,1024]{1,0:T(8,128)(2,1)}, u32[]{:S(2)}, u32[]{:S(2)}) collective-permute-start(bf16[512,1024]{1,0:T(8,128)(2,1)S(1)} %get-tuple-element.149.refs_2_), channel_id=1, source_target_pairs={{0,4},{1,5},{2,6},{3,7},{4,0},{5,1},{6,2},{7,3},{8,12},{9,13},{10,... | collective-permute-start | bytes 3145736 | tf_op jit(solution)/shard_map/ppermute | solution.py:794
  182.5 18.7 %collective-permute-start.21 = (bf16[256,1024]{1,0:T(8,128)(2,1)}, bf16[256,1024]{1,0:T(8,128)(2,1)}, u32[]{:S(2)}, u32[]{:S(2)}) collective-permute-start(bf16[256,1024]{1,0:T(8,128)(2,1)} %fusion.5), channel_id=1, source_target_pairs={{0,8},{1,9},{2,10},{3,11},{4,12},{5,13},{6,14},{7,15},{8,0},{9,1},... | collective-permute-start | bytes 1572872 | tf_op jit(solution)/shard_map/ppermute | solution.py:794
  188.7 14.3 %collective-permute-start.20 = (bf16[256,1024]{1,0:T(8,128)(2,1)}, bf16[256,1024]{1,0:T(8,128)(2,1)}, u32[]{:S(2)}, u32[]{:S(2)}) collective-permute-start(bf16[256,1024]{1,0:T(8,128)(2,1)} %fusion.4), channel_id=1, source_target_pairs={{0,16},{1,17},{2,18},{3,19},{4,20},{5,21},{6,22},{7,23},{8,24},{9,... | collective-permute-start | bytes 1572872 | tf_op jit(solution)/shard_map/ppermute | solution.py:794
  207.7 24.4 %collective-permute-start.25 = (bf16[2,128,512]{2,1,0:T(8,128)(2,1)S(1)}, bf16[2,128,512]{2,1,0:T(8,128)(2,1)S(1)}, u32[]{:S(2)}, u32[]{:S(2)}) collective-permute-start(bf16[2,128,512]{2,1,0:T(8,128)(2,1)S(1)} %get-tuple-element.278), channel_id=1, source_target_pairs={{0,5},{1,4},{2,1},{3,0},{4,7},{5,6},{6,3},{7,2},{8,13},{9,12},{10,... | collective-permute-start | bytes 786440 | tf_op jit(solution)/shard_map/ppermute | solution.py:794
  209.0 23.1 %collective-permute-start.22 = (bf16[2,128,512]{2,1,0:T(8,128)(2,1)S(1)}, bf16[2,128,512]{2,1,0:T(8,128)(2,1)S(1)}, u32[]{:S(2)}, u32[]{:S(2)}) collective-permute-start(bf16[2,128,512]{2,1,0:T(8,128)(2,1)S(1)} %get-tuple-element.285), channel_id=1, source_target_pairs={{0,0},{1,1},{2,4},{3,5},{4,2},{5,3},{6,6},{7,7},{8,8},{9,9},{10,12... | collective-permute-start | bytes 786440 | tf_op jit(solution)/shard_map/ppermute | solution.py:794
  209.6 23.0 %collective-permute-start.23 = (bf16[2,128,512]{2,1,0:T(8,128)(2,1)S(1)}, bf16[2,128,512]{2,1,0:T(8,128)(2,1)S(1)}, u32[]{:S(2)}, u32[]{:S(2)}) collective-permute-start(bf16[2,128,512]{2,1,0:T(8,128)(2,1)S(1)} %get-tuple-element.284), channel_id=1, source_target_pairs={{0,4},{1,5},{2,0},{3,1},{4,6},{5,7},{6,2},{7,3},{8,12},{9,13},{10,... | collective-permute-start | bytes 786440 | tf_op jit(solution)/shard_map/ppermute | solution.py:794
  213.2 21.2 %collective-permute-start.26 = (bf16[512,512]{1,0:T(8,128)(2,1)}, bf16[512,512]{1,0:T(8,128)(2,1)}, u32[]{:S(2)}, u32[]{:S(2)}) collective-permute-start(bf16[512,512]{1,0:T(8,128)(2,1)} %convolution_convert_fusion.3), channel_id=1, source_target_pairs={{0,8},{1,9},{2,10},{3,11},{4,12},{5,13},{6,14},{7,15},{8,0},{9,1},... | collective-permute-start | bytes 1572872 | tf_op jit(solution)/shard_map/ppermute | solution.py:794
  238.5 12.3 %collective-permute-start.30 = (bf16[256,512]{1,0:T(8,128)(2,1)S(1)}, bf16[256,512]{1,0:T(8,128)(2,1)}, u32[]{:S(2)}, u32[]{:S(2)}) collective-permute-start(bf16[256,512]{1,0:T(8,128)(2,1)S(1)} %fusion.14), channel_id=1, source_target_pairs={{0,16},{1,17},{2,18},{3,19},{4,20},{5,21},{6,22},{7,23},{8,24},{9,... | collective-permute-start | bytes 786440 | tf_op jit(solution)/shard_map/ppermute | solution.py:794
  252.7 64.0 %collective-permute-start.38 = (bf16[128,512]{1,0:T(8,128)(2,1)}, bf16[128,512]{1,0:T(8,128)(2,1)}, u32[]{:S(2)}, u32[]{:S(2)}) collective-permute-start(bf16[128,512]{1,0:T(8,128)(2,1)} %get-tuple-element.295), channel_id=1, source_target_pairs={{0,0},{1,1},{2,4},{3,5},{4,2},{5,3},{6,6},{7,7},{8,8},{9,9},{10,12... | collective-permute-start | bytes 393224 | tf_op jit(solution)/shard_map/ppermute | solution.py:794
  254.9 61.8 %collective-permute-start.39 = (bf16[128,512]{1,0:T(8,128)(2,1)}, bf16[128,512]{1,0:T(8,128)(2,1)}, u32[]{:S(2)}, u32[]{:S(2)}) collective-permute-start(bf16[128,512]{1,0:T(8,128)(2,1)} %get-tuple-element.294), channel_id=1, source_target_pairs={{0,4},{1,5},{2,0},{3,1},{4,6},{5,7},{6,2},{7,3},{8,12},{9,13},{10,... | collective-permute-start | bytes 393224 | tf_op jit(solution)/shard_map/ppermute | solution.py:794
  263.2 31.6 %all-to-all-start.3 = ((bf16[4,512,256]{2,1,0:T(8,128)(2,1)}), bf16[4,512,256]{2,1,0:T(8,128)(2,1)}, u32[]{:S(2)}, u32[]{:S(2)}) async-start(bf16[4,512,256]{2,1,0:T(8,128)(2,1)} %shard_map.299), calls=%async_computation.3 | async-start | bytes 2097152 | tf_op jit(solution)/shard_map/all_to_all | solution.py:834
  271.5 13.8 %collective-permute-start.37 = (bf16[512,512]{1,0:T(8,128)(2,1)S(1)}, bf16[512,512]{1,0:T(8,128)(2,1)S(1)}, u32[]{:S(2)}, u32[]{:S(2)}) collective-permute-start(bf16[512,512]{1,0:T(8,128)(2,1)S(1)} %convolution_convert_fusion.2), channel_id=1, source_target_pairs={{0,8},{1,9},{2,10},{3,11},{4,12},{5,13},{6,14},{7,15},{8,0},{9,1},... | collective-permute-start | bytes 1572872 | tf_op jit(solution)/shard_map/ppermute | solution.py:794
  285.5 11.4 %collective-permute-start.40 = (bf16[256,512]{1,0:T(8,128)(2,1)S(1)}, bf16[256,512]{1,0:T(8,128)(2,1)S(1)}, u32[]{:S(2)}, u32[]{:S(2)}) collective-permute-start(bf16[256,512]{1,0:T(8,128)(2,1)S(1)} %fusion.15), channel_id=1, source_target_pairs={{0,16},{1,17},{2,18},{3,19},{4,20},{5,21},{6,22},{7,23},{8,24},{9,... | collective-permute-start | bytes 786440 | tf_op jit(solution)/shard_map/ppermute | solution.py:794
  297.0 18.8 %all-to-all-start.4 = ((bf16[4,108,512]{2,1,0:T(8,128)(2,1)}), bf16[4,108,512]{2,1,0:T(8,128)(2,1)S(1)}, u32[]{:S(2)}, u32[]{:S(2)}) async-start(bf16[4,108,512]{2,1,0:T(8,128)(2,1)} %pad_maximum_fusion.14), calls=%async_computation.4 | async-start | bytes 917504 | tf_op jit(solution)/shard_map/all_to_all | solution.py:1164
  302.0 14.7 %collective-permute-start.41 = (bf16[128,512]{1,0:T(8,128)(2,1)}, bf16[128,512]{1,0:T(8,128)(2,1)S(1)}, u32[]{:S(2)}, u32[]{:S(2)}) collective-permute-start(bf16[128,512]{1,0:T(8,128)(2,1)} %get-tuple-element.293), channel_id=1, source_target_pairs={{0,1},{1,0},{2,5},{3,4},{4,3},{5,2},{6,7},{7,6},{8,9},{9,8},{10,13... | collective-permute-start | bytes 393224 | tf_op jit(solution)/shard_map/ppermute | solution.py:794
  304.0 15.2 %collective-permute-start.42 = (bf16[128,512]{1,0:T(8,128)(2,1)S(1)}, bf16[128,512]{1,0:T(8,128)(2,1)S(1)}, u32[]{:S(2)}, u32[]{:S(2)}) collective-permute-start(bf16[128,512]{1,0:T(8,128)(2,1)S(1)} %get-tuple-element.292), channel_id=1, source_target_pairs={{0,5},{1,4},{2,1},{3,0},{4,7},{5,6},{6,3},{7,2},{8,13},{9,12},{10,... | collective-permute-start | bytes 393224 | tf_op jit(solution)/shard_map/ppermute | solution.py:794
  (78 other events, 1081.3 us)
